TPU v7x, 32 devices: a whole 2x2x4 slice. The times are simulated.
32 devices in a mesh: dp: 8 (over z, x), head: 4 (over y, core).
Axes of the slice: x: 2, y: 2, z: 4, core: 2. Of those that a mesh axis runs over, the one named last changes fastest.
Arguments:
- layer_in: float32 [24576, 1024], P('dp', 'head'), may hold values from -6 to 6
- bucket: int32 [8], P('dp'), may hold values from 0 to 1, as said below
- w_query: bfloat16 [1024, 1024], P(None, 'head'), may hold values from -0.1875 to 0.1875
- w_key: bfloat16 [1024, 1024], P(None, 'head'), may hold values from -0.1875 to 0.1875
- w_value: bfloat16 [1024, 1024], P(None, 'head'), may hold values from -0.1875 to 0.1875
- w_proj: bfloat16 [1024, 1024], P('head'), may hold values from -0.75 to 0.75
- attn_gain: float32 [1024], replicated, may hold values from 0.5 to 1.5
- attn_shift: float32 [1024], replicated, may hold values from -3 to 3
- ffn_gain: float32 [1024], replicated, may hold values from 0.5 to 1.5
- ffn_shift: float32 [1024], replicated, may hold values from -3 to 3
- w_expand: bfloat16 [1024, 4096], P(None, ('dp', 'head')), may hold values from -0.1875 to 0.1875
- bias_expand: bfloat16 [1, 4096], P(None, ('dp', 'head')), may hold values from -3 to 3
- w_reduce: bfloat16 [1024, 4096], P(None, ('dp', 'head')), may hold values from -0.09375 to 0.09375
- bias_reduce: float32 [1024], P('head'), may hold values from -3 to 3
- grad_out: float32 [24576, 1024], P('dp', 'head'), may hold values from -6 to 6
Outputs:
- layer_out: float32 [24576, 1024], P('dp', 'head')
- grad_in: float32 [24576, 1024], P('dp', 'head')
- grad_query: float32 [1024, 1024], P(None, 'head')
- grad_key: float32 [1024, 1024], P(None, 'head')
- grad_value: float32 [1024, 1024], P(None, 'head')
- grad_proj: float32 [1024, 1024], P('head')
- grad_attn_gain: float32 [1024], replicated
- grad_attn_shift: float32 [1024], replicated
- grad_ffn_gain: float32 [1024], replicated
- grad_ffn_shift: float32 [1024], replicated
- grad_expand: float32 [1024, 4096], P(None, ('dp', 'head'))
- grad_bias_expand: float32 [1, 4096], P(None, ('dp', 'head'))
- grad_reduce: float32 [1024, 4096], P(None, ('dp', 'head'))
- grad_bias_reduce: float32 [1024], P('head')
Inputs may be any that keep to these rules, and one draw needn't show every extreme that they name: Group g's 3072 rows hold one sequence of 3072 tokens where bucket[g] is 1 and 6 sequences of 512 tokens where it is 0; both values occur in every draw.
All inputs are finite; a program needn't handle non-finite values.
Results may differ from a plain program's by a relative error of at most 0.017.
Values may be sent and summed in bfloat16 or wider, within the bound.
A program may use at most 256 MiB of HBM per device.

v0:
```python
import jax
import jax.numpy as jnp
from jax import lax
from jax.sharding import PartitionSpec as P

HEADS = 8
HEAD_DIM = 128
SHORT = 512


eps = 1e-05
masked_value = -1e30


def layer_norm(values, gain, shift):
    center = values - jnp.mean(values, axis=-1, keepdims=True)
    spread = jnp.mean(center * center, axis=-1, keepdims=True)
    return center * lax.rsqrt(spread + eps) * gain + shift


def norm_back(values, gain, shift, cotangent):
    _, pullback = jax.vjp(layer_norm, values, gain, shift)
    return pullback(cotangent)


def block_scores(query_block, key_rows, query_place, key_place, slopes):
    logits = jnp.einsum(
        "qhe,khe->hqk", query_block, key_rows, preferred_element_type=jnp.float32
    ) * HEAD_DIM ** (-0.5)
    distance = (query_place[:, None] - key_place[None, :]).astype(jnp.float32)
    scores = logits - slopes[:, None, None] * distance[None]
    allowed = (key_place[None, :] <= query_place[:, None])[None]
    return jnp.where(allowed, scores, masked_value)


def block_forward(query_block, key_rows, value_rows, query_place, key_place, slopes):
    scores = block_scores(query_block, key_rows, query_place, key_place, slopes)
    largest = jnp.max(scores, axis=-1, keepdims=True)
    powers = jnp.exp(scores - largest)
    total = jnp.sum(powers, axis=-1, keepdims=True)
    weights = (powers / total).astype(jnp.bfloat16)
    result = jnp.einsum(
        "hqk,khe->qhe", weights, value_rows, preferred_element_type=jnp.float32
    ).astype(jnp.bfloat16)
    return (result, (largest + jnp.log(total))[..., 0])


def block_backward(
    query_block, key_rows, value_rows, grad_block, logsum_block, query_place, key_place, slopes
):
    scores = block_scores(query_block, key_rows, query_place, key_place, slopes)
    softmax_full = jnp.exp(scores - logsum_block[..., None])
    softmax_low = softmax_full.astype(jnp.bfloat16)
    grad_weights = jnp.einsum(
        "qhe,khe->hqk", grad_block, value_rows, preferred_element_type=jnp.float32
    )
    grad_scores = softmax_full * (
        grad_weights - jnp.sum(softmax_full * grad_weights, axis=-1, keepdims=True)
    )
    grad_logits = grad_scores.astype(jnp.bfloat16)
    grad_queries = jnp.einsum(
        "hqk,khe->qhe", grad_logits, key_rows, preferred_element_type=jnp.float32
    ) * HEAD_DIM ** (-0.5)
    grad_keys = jnp.einsum(
        "hqk,qhe->khe", grad_logits, query_block, preferred_element_type=jnp.float32
    ) * HEAD_DIM ** (-0.5)
    grad_values = jnp.einsum(
        "hqk,qhe->khe", softmax_low, grad_block, preferred_element_type=jnp.float32
    )
    return (grad_queries, grad_keys, grad_values)


def attend(queries, keys, values, slopes, is_long):
    rows = queries.shape[0]
    order = jnp.arange(rows // SHORT, dtype=jnp.int32)
    local_place = jnp.arange(SHORT, dtype=jnp.int32)

    def short_path(queries, keys, values):

        def single_block(block_index):
            start = block_index * SHORT
            query_block = lax.dynamic_slice_in_dim(queries, start, SHORT, 0)
            key_block = lax.dynamic_slice_in_dim(keys, start, SHORT, 0)
            value_block = lax.dynamic_slice_in_dim(values, start, SHORT, 0)
            return block_forward(
                query_block, key_block, value_block, local_place, local_place, slopes
            )

        return lax.map(single_block, order)

    def long_path(queries, keys, values):
        key_place = jnp.arange(rows, dtype=jnp.int32)

        def single_block(block_index):
            start = block_index * SHORT
            query_block = lax.dynamic_slice_in_dim(queries, start, SHORT, 0)
            return block_forward(query_block, keys, values, start + local_place, key_place, slopes)

        return lax.map(single_block, order)

    result, logsum = lax.cond(is_long, long_path, short_path, queries, keys, values)
    return (result.reshape(queries.shape), logsum)


def attend_back(queries, keys, values, grad_heads, logsum, slopes, is_long):
    rows = queries.shape[0]
    order = jnp.arange(rows // SHORT, dtype=jnp.int32)
    local_place = jnp.arange(SHORT, dtype=jnp.int32)

    def short_path(queries, keys, values, grad_heads, logsum):

        def single_block(block_index):
            start = block_index * SHORT
            query_block = lax.dynamic_slice_in_dim(queries, start, SHORT, 0)
            key_block = lax.dynamic_slice_in_dim(keys, start, SHORT, 0)
            value_block = lax.dynamic_slice_in_dim(values, start, SHORT, 0)
            grad_block = lax.dynamic_slice_in_dim(grad_heads, start, SHORT, 0)
            return block_backward(
                query_block,
                key_block,
                value_block,
                grad_block,
                logsum[block_index],
                local_place,
                local_place,
                slopes,
            )

        grad_queries, grad_keys, grad_values = lax.map(single_block, order)
        return (
            grad_queries.reshape(queries.shape),
            grad_keys.reshape(queries.shape),
            grad_values.reshape(queries.shape),
        )

    def long_path(queries, keys, values, grad_heads, logsum):
        key_place = jnp.arange(rows, dtype=jnp.int32)

        def single_block(carry, block_index):
            start = block_index * SHORT
            query_block = lax.dynamic_slice_in_dim(queries, start, SHORT, 0)
            grad_block = lax.dynamic_slice_in_dim(grad_heads, start, SHORT, 0)
            grad_queries, grad_keys, grad_values = block_backward(
                query_block,
                keys,
                values,
                grad_block,
                logsum[block_index],
                start + local_place,
                key_place,
                slopes,
            )
            return ((carry[0] + grad_keys, carry[1] + grad_values), grad_queries)

        zeros = jnp.zeros(queries.shape, jnp.float32)
        (grad_keys, grad_values), grad_queries = lax.scan(single_block, (zeros, zeros), order)
        return (grad_queries.reshape(queries.shape), grad_keys, grad_values)

    grad_queries, grad_keys, grad_values = lax.cond(
        is_long, long_path, short_path, queries, keys, values, grad_heads, logsum
    )
    return (
        grad_queries.astype(jnp.bfloat16),
        grad_keys.astype(jnp.bfloat16),
        grad_values.astype(jnp.bfloat16),
    )


def shards(
    layer_in,
    bucket,
    w_query,
    w_key,
    w_value,
    w_proj,
    attn_gain,
    attn_shift,
    ffn_gain,
    ffn_shift,
    w_expand,
    bias_expand,
    w_reduce,
    bias_reduce,
    grad_out,
):
    rank = lax.axis_index("head")
    rows = layer_in.shape[0]
    slice_width = layer_in.shape[1]
    heads_here = w_query.shape[1] // HEAD_DIM
    all_slopes = jnp.exp2(-8.0 * (jnp.arange(HEADS, dtype=jnp.float32) + 1.0) / HEADS)
    slopes = lax.dynamic_slice_in_dim(all_slopes, rank * heads_here, heads_here)
    is_long = bucket[0] == 1
    whole_in = lax.all_gather(layer_in, "head", axis=1, tiled=True)
    normed_attn = layer_norm(whole_in, attn_gain, attn_shift).astype(jnp.bfloat16)

    def project(weight):
        product = jnp.dot(normed_attn, weight, preferred_element_type=jnp.float32)
        return product.astype(jnp.bfloat16).reshape(rows, heads_here, HEAD_DIM)

    queries = project(w_query)
    keys = project(w_key)
    values = project(w_value)
    attended, logsum = attend(queries, keys, values, slopes, is_long)
    attn_flat = attended.reshape(rows, heads_here * HEAD_DIM)
    attn_partial = jnp.dot(attn_flat, w_proj, preferred_element_type=jnp.float32)
    hidden = layer_in + lax.psum_scatter(
        attn_partial.astype(jnp.bfloat16), "head", scatter_dimension=1, tiled=True
    ).astype(jnp.float32)
    hidden_rows, grad_rows = (
        lax.all_to_all(
            hidden.astype(jnp.bfloat16), "head", split_axis=0, concat_axis=1, tiled=True
        ).astype(hidden.dtype),
        lax.all_to_all(
            grad_out.astype(jnp.bfloat16), "head", split_axis=0, concat_axis=1, tiled=True
        ).astype(grad_out.dtype),
    )
    normed_ffn = layer_norm(hidden_rows, ffn_gain, ffn_shift).astype(jnp.bfloat16)
    grad_low = grad_rows.astype(jnp.bfloat16)

    def expand(expand_cols, bias_cols):
        preact = jnp.dot(
            normed_ffn, expand_cols, preferred_element_type=jnp.float32
        ) + bias_cols.astype(jnp.float32)
        return (preact, jax.nn.gelu(preact).astype(jnp.bfloat16))

    pieces = (
        lax.all_gather(w_expand, ("dp", "head"), axis=1, tiled=True),
        lax.all_gather(bias_expand, ("dp", "head"), axis=1, tiled=True),
        lax.all_gather(w_reduce, ("dp", "head"), axis=1, tiled=True),
    )
    preact, activated = expand(pieces[0], pieces[1])
    ffn_result = lax.dot_general(
        activated, pieces[2], (((1,), (1,)), ((), ())), preferred_element_type=jnp.float32
    )
    pieces = (
        lax.all_gather(w_expand, ("dp", "head"), axis=1, tiled=True),
        lax.all_gather(bias_expand, ("dp", "head"), axis=1, tiled=True),
        lax.all_gather(w_reduce, ("dp", "head"), axis=1, tiled=True),
    )
    preact, activated = expand(pieces[0], pieces[1])
    grad_activated = jnp.dot(grad_low, pieces[2], preferred_element_type=jnp.float32)
    _, gelu_back = jax.vjp(jax.nn.gelu, preact)
    grad_preact = gelu_back(grad_activated)[0].astype(jnp.bfloat16)
    grad_norm = lax.dot_general(
        grad_preact, pieces[0], (((1,), (1,)), ((), ())), preferred_element_type=jnp.float32
    )
    expand_part = lax.dot_general(
        normed_ffn, grad_preact, (((0,), (0,)), ((), ())), preferred_element_type=jnp.float32
    )
    reduce_part = lax.dot_general(
        grad_low, activated, (((0,), (0,)), ((), ())), preferred_element_type=jnp.float32
    )
    bias_part = jnp.sum(grad_preact, axis=0, keepdims=True, dtype=jnp.float32)
    grad_wide = expand_part
    grad_bias = bias_part
    grad_narrow = reduce_part
    backed = (grad_norm, grad_wide, grad_bias, grad_narrow)
    grad_norm, grad_wide, grad_bias, grad_narrow = backed
    grad_expand, grad_bias_expand, grad_reduce = (
        lax.psum_scatter(grad_wide, ("dp", "head"), scatter_dimension=1, tiled=True),
        lax.psum_scatter(grad_bias, ("dp", "head"), scatter_dimension=1, tiled=True),
        lax.psum_scatter(grad_narrow, ("dp", "head"), scatter_dimension=1, tiled=True),
    )
    grad_hidden_rows, grad_ffn_gain, grad_ffn_shift = norm_back(
        hidden_rows, ffn_gain, ffn_shift, grad_norm
    )
    grad_ffn_gain, grad_ffn_shift = lax.psum((grad_ffn_gain, grad_ffn_shift), ("dp", "head"))
    ffn_features, back_features = (
        lax.all_to_all(
            ffn_result.astype(jnp.bfloat16), "head", split_axis=1, concat_axis=0, tiled=True
        ).astype(ffn_result.dtype),
        lax.all_to_all(
            grad_hidden_rows.astype(jnp.bfloat16), "head", split_axis=1, concat_axis=0, tiled=True
        ).astype(grad_hidden_rows.dtype),
    )
    layer_out = hidden + ffn_features + bias_reduce
    grad_hidden = grad_out + back_features
    grad_attn = lax.all_gather(grad_hidden.astype(jnp.bfloat16), "head", axis=1, tiled=True)
    grad_proj = lax.dot_general(
        attn_flat, grad_attn, (((0,), (0,)), ((), ())), preferred_element_type=jnp.float32
    )
    grad_flat = lax.dot_general(
        grad_attn, w_proj, (((1,), (1,)), ((), ())), preferred_element_type=jnp.float32
    )
    grad_heads = grad_flat.astype(jnp.bfloat16).reshape(rows, heads_here, HEAD_DIM)
    grad_queries, grad_keys, grad_values = attend_back(
        queries, keys, values, grad_heads, logsum, slopes, is_long
    )

    def weight_grad(grad_part):
        return lax.dot_general(
            normed_attn,
            grad_part.reshape(rows, heads_here * HEAD_DIM),
            (((0,), (0,)), ((), ())),
            preferred_element_type=jnp.float32,
        )

    def input_part(grad_part, weight):
        return lax.dot_general(
            grad_part.reshape(rows, heads_here * HEAD_DIM),
            weight,
            (((1,), (1,)), ((), ())),
            preferred_element_type=jnp.float32,
        )

    local_first = (
        input_part(grad_queries, w_query)
        + input_part(grad_keys, w_key)
        + input_part(grad_values, w_value)
    )
    grad_first = lax.psum(local_first.astype(jnp.bfloat16), "head").astype(jnp.float32)
    grad_whole, grad_attn_gain, grad_attn_shift = norm_back(
        whole_in, attn_gain, attn_shift, grad_first
    )
    grad_in = grad_hidden + lax.dynamic_slice_in_dim(grad_whole, rank * slice_width, slice_width, 1)
    grad_bias_reduce = jnp.sum(grad_out, axis=0)
    (
        grad_query,
        grad_key,
        grad_value,
        grad_proj,
        grad_attn_gain,
        grad_attn_shift,
        grad_bias_reduce,
    ) = lax.psum(
        (
            weight_grad(grad_queries),
            weight_grad(grad_keys),
            weight_grad(grad_values),
            grad_proj,
            grad_attn_gain,
            grad_attn_shift,
            grad_bias_reduce,
        ),
        "dp",
    )
    return (
        layer_out,
        grad_in,
        grad_query,
        grad_key,
        grad_value,
        grad_proj,
        grad_attn_gain,
        grad_attn_shift,
        grad_ffn_gain,
        grad_ffn_shift,
        grad_expand,
        grad_bias_expand,
        grad_reduce,
        grad_bias_reduce,
    )


def solution(mesh):
    placed = (
        P("dp", "head"),
        P("dp"),
        P(None, "head"),
        P(None, "head"),
        P(None, "head"),
        P("head", None),
        P(),
        P(),
        P(),
        P(),
        P(None, ("dp", "head")),
        P(None, ("dp", "head")),
        P(None, ("dp", "head")),
        P("head"),
        P("dp", "head"),
    )
    return jax.shard_map(
        shards,
        mesh=mesh,
        in_specs=placed,
        out_specs=(
            P("dp", "head"),
            P("dp", "head"),
            P(None, "head"),
            P(None, "head"),
            P(None, "head"),
            P("head", None),
            P(),
            P(),
            P(),
            P(),
            P(None, ("dp", "head")),
            P(None, ("dp", "head")),
            P(None, ("dp", "head")),
            P("head"),
        ),
        check_vma=False,
    )
```

profile of v0, /device:TPU:0, one launch (start us, length us, event | category | flops | bytes accessed | tf_op | source)
XLA Modules:
  0.0 1509.8 jit_solution(17025491534814780240)
XLA Ops:
  9.6 85.7 %all-gather.5.cloned.1.call-done = f32[3072,1024]{1,0:T(8,128)} async-done(((f32[3072,256]{1,0:T(8,128)}), f32[3072,1024]{1,0:T(8,128)}) %all-gather.5.cloned.1.call-update) | async-done | bytes 12582928 | tf_op jit(solution)/shard_map/all_gather | solution.py:193
  100.5 7.3 multiply_reduce_fusion.2
  120.3 133.5 %conditional.2 = (bf16[6,512,2,128]{1,3,2,0:T(8,128)(2,1)}, f32[6,2,512]{2,1,0:T(2,128)}) conditional(s32[]{:T(128)} %bitcast.14, (s32[6]{0:T(128)S(1)}, bf16[3072,2,128]{0,2,1:T(8,128)(2,1)}, s32[512]{0:T(512)S(1)}, s32[512]{0:T(512)S(1)}, bf16[3072,2,128]{0,2,1:T(8,128)(2,1)}, /*index=5*/bf16[3072,2,128]{0,2,1:T(8,128)(2,1)S(1)}, ...), branch_computations={%region_2.7_spmd, %region_7.12_spmd} | conditional | flops 1672084992 | bytes 86557200 | solution.py:101
  126.0 127.7 %while.54 = (s32[]{:T(128)}, bf16[6,512,2,128]{1,3,2,0:T(8,128)(2,1)}, f32[6,2,512]{2,1,0:T(2,128)}, s32[6]{0:T(128)S(1)}, s32[512]{0:T(512)S(1)}, /*index=5*/bf...) while((s32[]{:T(128)}, ...), condition=%wide.region_11.11_spmd.clone.clone, body=%wide.region_8.10_spmd.clone.clone.sunk | while | flops 1672084992 | bytes 73965792 | solution.py:99
  129.4 5.9 fusion.203
  172.0 5.9 fusion.203
  269.8 58.2 %reduce-scatter.7.cloned.1.call-done = bf16[3072,256]{1,0:T(8,128)(2,1)} async-done(((bf16[3072,1024]{1,0:T(8,128)(2,1)}), bf16[3072,256]{1,0:T(8,128)(2,1)}) %reduce-scatter.7.cloned.1.call-update) | async-done | bytes 1572880 | tf_op jit(solution)/shard_map/reduce_scatter | solution.py:206
  336.7 52.6 %all_gather.20 = bf16[1,4096]{1,0:T(2,128)(2,1)S(1)} all-gather(bf16[1,128]{1,0:T(2,128)(2,1)S(1)} %copy-done.62), channel_id=1, replica_groups=mesh['dp'=8,'head'=4] {'dp','head'}, dimensions={1}, use_global_device_ids=true | all-gather | bytes 8448 | tf_op jit(solution)/shard_map/all_gather | solution.py:228
  395.3 13.8 fusion.88
  409.1 77.7 %all-gather.9.cloned.1.call-done = bf16[1024,4096]{1,0:T(8,128)(2,1)} async-done(((bf16[1024,128]{1,0:T(8,128)(2,1)}), bf16[1024,4096]{1,0:T(8,128)(2,1)}) %all-gather.9.cloned.1.call-update) | async-done | bytes 8388624 | tf_op jit(solution)/shard_map/all_gather | solution.py:229
  486.8 19.8 %convert_reduce_fusion.1 = (f32[4096]{0:T(1024)S(1)}, bf16[768,4096]{1,0:T(8,128)(2,1)S(1)}) fusion(f32[768,4096]{1,0:T(8,128)} %fusion.88, f32[4096]{0:T(1024)S(1)} %bitcast.247, bf16[768,1024]{0,1:T(8,128)(2,1)S(1)} %bitcast.243, bf16[1024,4096]{1,0:T(8,128)(2,1)} %all-gather.9.cloned.1.call-done), kind=kOutput, calls=%fused_computation.110 | convolution fusion | flops 6514798592 | bytes 28868608 | tf_op jit(solution)/shard_map/dot_general | solution.py:241
  506.6 13.2 multiply_reduce_fusion.3
  521.3 22.9 %all_to_all.58 = bf16[768,4,256]{2,0,1:T(8,128)(2,1)S(1)} all-to-all(bf16[768,4,256]{2,0,1:T(8,128)(2,1)S(1)} %bitcast.236), channel_id=1, replica_groups=mesh['dp'=8,'head'=4] {'head'}, dimensions={1} | all-to-all | bytes 3145728 | tf_op jit(solution)/shard_map/all_to_all | solution.py:272
  549.0 44.0 %all-gather.11.cloned.1.call-done = bf16[3072,1024]{1,0:T(8,128)(2,1)} async-done(((bf16[3072,256]{1,0:T(8,128)(2,1)}), bf16[3072,1024]{1,0:T(8,128)(2,1)}) %all-gather.11.cloned.1.call-update) | async-done | bytes 6291472 | tf_op jit(solution)/shard_map/all_gather | solution.py:278
  598.7 306.3 %conditional.3 = (bf16[3072,256]{0,1:T(8,128)(2,1)}, bf16[3072,256]{0,1:T(8,128)(2,1)S(1)}, bf16[3072,256]{1,0:T(8,128)(2,1)}) conditional(s32[]{:T(128)} %bitcast.14, (s32[6]{0:T(128)S(1)}, bf16[3072,2,128]{0,2,1:T(8,128)(2,1)}, s32[512]{0:T(512)S(1)}, s32[512]{0:T(512)S(1)}, bf16[3072,2,128]{0,2,1:T(8,128)(2,1)}, /*index=5*/f32[2]{0:T(128)S(1)}, ...), branch_computations={%region_17.21_spmd, %region_21.25_spmd} | conditional | flops 4071489024 | bytes 289444704 | solution.py:159
  604.6 293.0 %while.55 = (s32[]{:T(128)}, f32[3072,2,128]{0,2,1:T(8,128)}, f32[3072,2,128]{0,2,1:T(8,128)}, bf16[6,512,2,128]{3,1,2,0:T(8,128)(2,1)}, s32[6]{0:T(128)S(1)}, /...) while((s32[]{:T(128)}, f32[3072,2,128]{0,2,1:T(8,128)}, ...), condition=%wide.region_24.24_spmd.clone.clone, body=%wide.region_22.23_spmd.clone.clone.sunk | while | flops 4069916160 | bytes 235958736 | solution.py:156
  611.2 7.3 fusion.183
  618.5 11.9 multiply_reduce_fusion.7
  630.4 9.2 multiply_convert_fusion.7
  660.1 7.3 fusion.183
  667.4 11.9 multiply_reduce_fusion.7
  679.4 9.2 multiply_convert_fusion.7
  709.0 7.3 fusion.183
  716.3 11.9 multiply_reduce_fusion.7
  728.3 9.1 multiply_convert_fusion.7
  757.8 7.3 fusion.183
  765.1 11.9 multiply_reduce_fusion.7
  777.0 9.1 multiply_convert_fusion.7
  806.6 7.3 fusion.183
  813.9 11.9 multiply_reduce_fusion.7
  825.8 9.1 multiply_convert_fusion.7
  855.4 7.3 fusion.183
  862.7 11.9 multiply_reduce_fusion.7
  874.6 9.1 multiply_convert_fusion.7
  905.1 8.5 fusion.95
  913.6 7.9 fusion.94
  921.5 12.2 add_convert_fusion
  934.4 16.2 %convolution_bitcast_fusion.1 = f32[1024,4096]{0,1:T(8,128)} fusion(bf16[768,1024]{0,1:T(8,128)(2,1)} %bitcast.242, f32[768,4096]{1,0:T(8,128)} %fusion.88, f32[4096]{0:T(1024)S(1)} %bitcast.248), kind=kOutput, calls=%fused_computation.115 | convolution fusion | flops 6473908224 | bytes 30949376 | tf_op jit(solution)/shard_map/dot_general | solution.py:250
  951.0 6.1 fusion.97
  973.7 13.6 fusion.87
  987.3 13.6 convolution_convert_fusion.6
  1006.6 77.2 %all-reduce = (f32[1024]{0:T(1024)}, f32[1024]{0:T(1024)}) all-reduce(f32[1024]{0:T(1024)S(1)} %copy-done.59, f32[1024]{0:T(1024)S(1)} %copy-done.60), channel_id=1, replica_groups=mesh['dp'=8,'head'=4] {'dp','head'}, use_global_device_ids=true, to_apply=%region_37.38 | all-reduce | flops 2048 | bytes 16384 | tf_op jit(solution)/shard_map/psum | solution.py:267
  1089.8 10.1 all-reduce.6.cloned.1.call-done
  1099.9 9.0 fusion.73
  1108.9 9.1 fusion.90
  1120.7 23.4 %all-reduce.1 = (f32[1024]{0:T(1024)}, f32[1024]{0:T(1024)}, f32[256]{0:T(256)}) all-reduce(f32[1024]{0:T(1024)S(1)} %get-tuple-element.676, f32[1024]{0:T(1024)S(1)} %get-tuple-element.680, f32[256]{0:T(256)S(1)} %get-tuple-element.793), channel_id=1, replica_groups=mesh['dp'=8,'head'=4] {'dp'}, use_global_device_ids=true, to_apply=%region_33.34 | all-reduce | flops 2304 | bytes 18432 | tf_op jit(solution)/shard_map/psum | solution.py:325
  1144.1 167.4 %reduce-scatter.11.cloned.1.call-done = f32[1024,128]{0,1:T(8,128)} async-done(((f32[1024,4096]{0,1:T(8,128)}), f32[1024,128]{0,1:T(8,128)}) %reduce-scatter.11.cloned.1.call-update) | async-done | bytes 524304 | tf_op jit(solution)/shard_map/reduce_scatter | solution.py:262
  1313.5 182.1 %reduce-scatter.9.cloned.1.call-done = f32[1024,128]{1,0:T(8,128)} async-done(((f32[1024,4096]{1,0:T(8,128)}), f32[1024,128]{1,0:T(8,128)}) %reduce-scatter.9.cloned.1.call-update) | async-done | bytes 524304 | tf_op jit(solution)/shard_map/reduce_scatter | solution.py:260
  (390 shorter events, 337.5 us)
Async XLA Ops:
  8.0 249.4 %copy-start = (bf16[256,1024]{1,0:T(8,128)(2,1)S(1)}, bf16[256,1024]{1,0:T(8,128)(2,1)}, u32[]{:S(2)}) copy-start(bf16[256,1024]{1,0:T(8,128)(2,1)} %param.32) | copy-start | bytes 1572868
  8.0 87.2 %all-gather.5.cloned.1.call-start = ((), (), s32[]{:S(2)}) async-start(), calls=%async_computation.8 | async-start | bytes 15728640 | tf_op jit(solution)/shard_map/all_gather | solution.py:193
  8.8 319.3 %reduce-scatter.7.cloned.1.call-start = ((), (), s32[]{:S(2)}) async-start(), calls=%async_computation.9 | async-start | bytes 7864320 | tf_op jit(solution)/shard_map/reduce_scatter | solution.py:206
  100.5 8.5 copy-start.6
  100.5 8.5 copy-start.54
  100.5 8.5 copy-start.58
  261.9 133.4 %all-gather.7.cloned.1.call-start = ((), (), s32[]{:S(2)}) async-start(), calls=%async_computation.10 | async-start | bytes 8650752 | tf_op jit(solution)/shard_map/all_gather | solution.py:227
  262.5 224.4 %all-gather.9.cloned.1.call-start = ((), (), s32[]{:S(2)}) async-start(), calls=%async_computation.11 | async-start | bytes 8650752 | tf_op jit(solution)/shard_map/all_gather | solution.py:229
  266.2 65.7 %all-to-all-start.2 = ((bf16[4,768,256]{2,1,0:T(8,128)(2,1)}), bf16[4,768,256]{2,1,0:T(8,128)(2,1)S(1)}, u32[]{:S(2)}, u32[]{:S(2)}) async-start(bf16[4,768,256]{2,1,0:T(8,128)(2,1)} %bitcast.240), calls=%async_computation.3 | async-start | bytes 3145728 | tf_op jit(solution)/shard_map/all_to_all | solution.py:213
  333.1 58.9 %all-to-all-start = ((bf16[4,768,256]{2,1,0:T(8,128)(2,1)}), bf16[4,768,256]{2,1,0:T(8,128)(2,1)S(1)}, u32[]{:S(2)}, u32[]{:S(2)}) async-start(bf16[4,768,256]{2,1,0:T(8,128)(2,1)} %bitcast.239), calls=%async_computation.1 | async-start | bytes 3145728 | tf_op jit(solution)/shard_map/all_to_all | solution.py:210
  336.6 256.3 %all-gather.11.cloned.1.call-start = ((), (), s32[]{:S(2)}) async-start(), calls=%async_computation.12 | async-start | bytes 7864320 | tf_op jit(solution)/shard_map/all_gather | solution.py:278
  389.3 97.5 %copy-start.56 = (f32[1,4096]{1,0:T(1,128)}, f32[1,4096]{1,0:T(1,128)S(1)}, u32[]{:S(2)}) copy-start(f32[1,4096]{1,0:T(1,128)S(1)} %add.257) | copy-start | bytes 49156
  394.6 125.2 %copy-start.38 = (f32[768]{0:T(1024)}, f32[768]{0:T(1024)S(1)}, u32[]{:S(2)}) copy-start(f32[768]{0:T(1024)S(1)} %broadcast_multiply_fusion.1) | copy-start | bytes 9220
  395.2 124.7 %copy-start.40 = (f32[768]{0:T(1024)}, f32[768]{0:T(1024)S(1)}, u32[]{:S(2)}) copy-start(f32[768]{0:T(1024)S(1)} %fusion.86) | copy-start | bytes 9220
  395.3 91.5 %copy-start.29 = (bf16[768,4,256]{0,2,1:T(8,128)(2,1)S(1)}, bf16[768,4,256]{0,2,1:T(8,128)(2,1)}, u32[]{:S(2)}) copy-start(bf16[768,4,256]{0,2,1:T(8,128)(2,1)} %copy.151) | copy-start | bytes 4718596
  486.8 19.8 %copy-start.15 = (f32[4,96,8,256]{3,2,0,1:T(8,128)S(1)}, f32[4,96,8,256]{3,2,0,1:T(8,128)}, u32[]{:S(2)}) copy-start(f32[4,96,8,256]{3,2,0,1:T(8,128)} %copy.199) | copy-start | bytes 9437188
  506.6 13.3 copy-start.27
  521.1 24.2 %copy-start.16 = (f32[3072,256]{1,0:T(8,128)S(1)}, f32[3072,256]{1,0:T(8,128)}, u32[]{:S(2)}) copy-start(f32[3072,256]{1,0:T(8,128)} %param.41) | copy-start | bytes 9437188
  546.9 536.9 %reduce-scatter.13.cloned.1.call-start = ((), (), s32[]{:S(2)}) async-start(), calls=%async_computation.16 | async-start | bytes 2162688
  549.0 551.0 %all-reduce.6.cloned.1.call-start = ((), (), s32[]{:S(2)}) async-start(), calls=%async_computation.13 | async-start | bytes 12582912 | tf_op jit(solution)/shard_map/psum | solution.py:311
  630.4 11.9 copy-start.2
  630.4 12.8 copy-start.7
  679.4 12.0 copy-start.2
  679.4 12.8 copy-start.7
  728.3 11.9 copy-start.2
  728.3 12.7 copy-start.7
  777.0 11.9 copy-start.2
  777.0 12.7 copy-start.7
  825.8 11.9 copy-start.2
  825.8 12.7 copy-start.7
  874.6 11.9 copy-start.2
  874.6 12.7 copy-start.7
  905.0 8.5 copy-start.23
  933.7 377.8 %reduce-scatter.11.cloned.1.call-start = ((), (), s32[]{:S(2)}) async-start(), calls=%async_computation.15 | async-start | bytes 17301504 | tf_op jit(solution)/shard_map/reduce_scatter | solution.py:262
  950.6 362.9 %all-reduce.8.cloned.1.call-start = ((), (), s32[]{:S(2)}) async-start(), calls=%async_computation.17 | async-start | bytes 8388608 | tf_op jit(solution)/shard_map/psum | solution.py:325
  957.1 11.6 slice-start
  973.0 522.6 %reduce-scatter.9.cloned.1.call-start = ((), (), s32[]{:S(2)}) async-start(), calls=%async_computation.14 | async-start | bytes 17301504 | tf_op jit(solution)/shard_map/reduce_scatter | solution.py:260
  1000.9 84.3 %copy-start.25 = (bf16[3072,256]{1,0:T(8,128)(2,1)S(1)}, bf16[3072,256]{1,0:T(8,128)(2,1)}, u32[]{:S(2)}) copy-start(bf16[3072,256]{1,0:T(8,128)(2,1)} %reduce-scatter.7.cloned.1.call-done) | copy-start | bytes 4718596
  1000.9 84.3 %copy-start.61 = (f32[256]{0:T(256)S(1)}, f32[256]{0:T(256)}, u32[]{:S(2)}) copy-start(f32[256]{0:T(256)} %param.40) | copy-start | bytes 3076
  1002.2 83.1 %all-to-all-start.1 = ((bf16[768,4,256]{2,0,1:T(8,128)(2,1)}), bf16[768,4,256]{2,0,1:T(8,128)(2,1)}, u32[]{:S(2)}, u32[]{:S(2)}) async-start(bf16[768,4,256]{2,0,1:T(8,128)(2,1)} %bitcast.234), calls=%async_computation.2 | async-start | bytes 3145728 | tf_op jit(solution)/shard_map/all_to_all | solution.py:269
  1085.2 14.7 copy-start.45
  1085.2 14.7 copy-start.49
  1085.2 14.7 copy-start.55
  1089.8 19.1 %copy-start.51 = (f32[3072]{0:T(1024)S(1)}, f32[3072]{0:T(1024)}, u32[]{:S(2)}) copy-start(f32[3072]{0:T(1024)} %copy-done.50) | copy-start | bytes 36868
  1099.9 9.0 copy-start.19
  1108.9 9.2 copy-start.17
  1108.9 9.2 copy-start.22
  1313.5 186.7 %copy-start.32 = (f32[1024,256]{1,0:T(8,128)S(1)}, f32[1024,256]{1,0:T(8,128)}, u32[]{:S(2)}) copy-start(f32[1024,256]{1,0:T(8,128)} %get-tuple-element.1280) | copy-start | bytes 3145732
  (60 other events, 187.5 us)
Sparse Core Ops, SparseCore 0:
  10.4 84.7 all-gather.4
  262.0 66.0 reduce-scatter.6
  547.0 45.8 all-gather.10
  933.8 166.0 all-reduce.5
  1104.9 185.6 all-reduce.7
Sparse Core Ops, SparseCore 1:
  265.6 127.8 all-gather.6
  396.6 90.2 all-gather.8
  549.8 159.3 reduce-scatter.12
  950.7 360.8 reduce-scatter.10
  1314.4 181.2 reduce-scatter.8
where the time goes:
time: 1520 us; the launch traced here: 1510 us
  waiting for transfers between devices  627 us (41%)
  matrix products  391 us (26%)
  blocking collectives  176 us (12%)
  other arithmetic  165 us (11%)
  local copies, waits for them, and re-layouts  99.9 us (7%)
  loops' own time  21.5 us (1%)
  between operations  17 us (1%)
    reduce_scatter x1, waiting for transfers between devices, shards(): lax.psum_scatter(grad_wide, ('dp', 'head'), scatter_dimension=1, tiled=True)  182 us
    reduce_scatter x1, waiting for transfers between devices, shards(): lax.psum_scatter(grad_narrow, ('dp', 'head'), scatter_dimension=1, tiled=...  167 us
    dot_general x12, matrix products, block_scores(): jnp.einsum('qhe,khe->hqk', query_block, key_rows, preferred_element_type=...  107 us
    all_gather x1, waiting for transfers between devices, shards(): whole_in = lax.all_gather(layer_in, 'head', axis=1, tiled=True)  85.7 us
    all_gather x1, waiting for transfers between devices, shards(): lax.all_gather(w_reduce, ('dp', 'head'), axis=1, tiled=True)  77.7 us
    psum x1, blocking collectives, shards(): lax.psum((grad_ffn_gain, grad_ffn_shift), ('dp', 'head'))  77.2 us
    reduce_scatter x1, waiting for transfers between devices, shards(): lax.psum_scatter(attn_partial.astype(jnp.bfloat16), 'head', scatter_dimen...  58.2 us
    convert_element_type x6, other arithmetic, block_backward(): grad_logits = grad_scores.astype(jnp.bfloat16)  54.8 us
  transfers between devices with their start and end apart: 13, of which 7 were waited for; matrix products, arithmetic and copies ran while one was open for 27% of the time, Pallas kernels for 0%

commit v1 on v0

v1 whole, which is shorter than its diff:
```python
import functools

import jax
import jax.numpy as jnp
from jax import lax
from jax.experimental import pallas as pl
from jax.experimental.pallas import tpu as pltpu
from jax.sharding import PartitionSpec as P

HEADS = 8
HEAD_DIM = 128
SHORT = 512
eps = 1e-05
masked_value = -1e30
LOG2E = 1.4426950408889634
LN2 = 0.6931471805599453
SCALE = HEAD_DIM ** (-0.5)
MIB = 1024 * 1024
f32 = jnp.float32
bf16 = jnp.bfloat16

NN = (((1,), (0,)), ((), ()))
NT = (((1,), (1,)), ((), ()))
TN = (((0,), (0,)), ((), ()))


def dot(left, right, dims=NN):
    return lax.dot_general(left, right, dims, preferred_element_type=f32)


def full_spec(shape):
    return pl.BlockSpec(shape, lambda *_: (0,) * len(shape))


def project_kernel(x0, x1, x2, x3, gain, shift, weight, normed, qkv):
    parts = [ref[...].astype(f32) for ref in (x0, x1, x2, x3)]
    width = parts[0].shape[1]
    features = 4 * width
    mean = sum(jnp.sum(p, axis=1, keepdims=True) for p in parts) * (1.0 / features)
    parts = [p - mean for p in parts]
    spread = sum(jnp.sum(p * p, axis=1, keepdims=True) for p in parts) * (1.0 / features)
    scale = lax.rsqrt(spread + eps)
    for k, p in enumerate(parts):
        cols = slice(k * width, (k + 1) * width)
        normed[:, cols] = (p * scale * gain[:, cols] + shift[:, cols]).astype(bf16)
    qkv[...] = dot(normed[...], weight[...]).astype(bf16)


def project(pieces, gain, shift, weight):
    rows, width = pieces[0].shape
    block = SHORT
    out = weight.shape[1]
    return pl.pallas_call(
        project_kernel,
        grid=(rows // block,),
        in_specs=[pl.BlockSpec((block, width), lambda i: (i, 0))] * 4
        + [full_spec(gain.shape), full_spec(shift.shape), full_spec(weight.shape)],
        out_specs=[
            pl.BlockSpec((block, 4 * width), lambda i: (i, 0)),
            pl.BlockSpec((block, out), lambda i: (i, 0)),
        ],
        out_shape=[
            jax.ShapeDtypeStruct((rows, 4 * width), bf16),
            jax.ShapeDtypeStruct((rows, out), bf16),
        ],
        compiler_params=pltpu.CompilerParams(vmem_limit_bytes=40 * MIB),
        cost_estimate=pl.CostEstimate(
            flops=2 * rows * 4 * width * out, bytes_accessed=rows * 4 * width * 4, transcendentals=0
        ),
    )(*pieces, gain, shift, weight)


def positions(block):
    return lax.broadcasted_iota(jnp.int32, (block, block), 0)


def attend_kernel(heads, kind, slopes, qkv, out, logsum, total):
    block = SHORT
    i = pl.program_id(0)
    low = jnp.where(kind[0] == 1, 0, i)
    start = pl.multiple_of(i * block, block)
    key_place = lax.broadcasted_iota(jnp.int32, (block, block), 0)
    query_place = lax.broadcasted_iota(jnp.int32, (block, block), 1)
    width = heads * HEAD_DIM

    def scores(h, j):
        at = pl.multiple_of(j * block, block)
        q = qkv[pl.ds(start, block), h * HEAD_DIM : (h + 1) * HEAD_DIM]
        k = qkv[pl.ds(at, block), width + h * HEAD_DIM : width + (h + 1) * HEAD_DIM]
        v = qkv[pl.ds(at, block), 2 * width + h * HEAD_DIM : 2 * width + (h + 1) * HEAD_DIM]
        place = (key_place + (j - i) * block).astype(f32) * (slopes[h] * LOG2E)
        return dot(k, q, NT) * (SCALE * LOG2E) + place, v

    carry = []
    for h in range(heads):
        s, v = scores(h, i)
        s = jnp.where(key_place <= query_place, s, masked_value)
        m = jnp.max(s, axis=0, keepdims=True)
        p = jnp.exp2(s - m)
        carry += [m, jnp.sum(p, axis=0, keepdims=True)]
        total[h] = dot(v, p.astype(bf16), TN)

    def step(j, carry):
        new = []
        for h in range(heads):
            m, l = carry[2 * h], carry[2 * h + 1]
            s, v = scores(h, j)
            m_new = jnp.maximum(m, jnp.max(s, axis=0, keepdims=True))
            p = jnp.exp2(s - m_new)
            fade = jnp.exp2(m - m_new)
            new += [m_new, l * fade + jnp.sum(p, axis=0, keepdims=True)]
            total[h] = total[h] * fade + dot(v, p.astype(bf16), TN)
        return tuple(new)

    carry = lax.fori_loop(low, i, step, tuple(carry))
    for h in range(heads):
        m, l = carry[2 * h], carry[2 * h + 1]
        out[:, h * HEAD_DIM : (h + 1) * HEAD_DIM] = (total[h] * (1.0 / l)).T.astype(bf16)
        logsum[0, h : h + 1, :] = m + jnp.log(l) * LOG2E


def attend(qkv, slopes, kind):
    rows = qkv.shape[0]
    width = qkv.shape[1] // 3
    heads = width // HEAD_DIM
    block = SHORT
    n = rows // block
    return pl.pallas_call(
        functools.partial(attend_kernel, heads),
        grid=(n,),
        in_specs=[
            pl.BlockSpec(memory_space=pltpu.SMEM),
            pl.BlockSpec(memory_space=pltpu.SMEM),
            full_spec(qkv.shape),
        ],
        out_specs=[
            pl.BlockSpec((block, width), lambda i: (i, 0)),
            pl.BlockSpec((1, heads, block), lambda i: (i, 0, 0)),
        ],
        out_shape=[
            jax.ShapeDtypeStruct((rows, width), bf16),
            jax.ShapeDtypeStruct((n, heads, block), f32),
        ],
        scratch_shapes=[pltpu.VMEM((heads, HEAD_DIM, block), f32)],
        compiler_params=pltpu.CompilerParams(vmem_limit_bytes=48 * MIB),
        cost_estimate=pl.CostEstimate(
            flops=8 * rows * rows * width, bytes_accessed=rows * width * 8, transcendentals=0
        ),
    )(kind, slopes, qkv)


def attend_back_kernel(heads, kind, slopes, qkv, grad, attended, logsum, grad_qkv, total_q, delta):
    block = SHORT
    j = pl.program_id(0)
    n = pl.num_programs(0)
    high = jnp.where(kind[0] == 1, n, j + 1)
    at = pl.multiple_of(j * block, block)
    key_place = lax.broadcasted_iota(jnp.int32, (block, block), 0)
    query_place = lax.broadcasted_iota(jnp.int32, (block, block), 1)
    width = heads * HEAD_DIM

    @pl.when(j == 0)
    def _():
        total_q[...] = jnp.zeros_like(total_q)

        def fill(i, _):
            here = pl.ds(pl.multiple_of(i * block, block), block)
            for h in range(heads):
                cols = slice(h * HEAD_DIM, (h + 1) * HEAD_DIM)
                both = grad[here, cols].astype(f32) * attended[here, cols].astype(f32)
                delta[i, h : h + 1, :] = jnp.sum(both.T, axis=0, keepdims=True)
            return 0

        lax.fori_loop(0, n, fill, 0)

    def pair(h, i, masked):
        start = pl.multiple_of(i * block, block)
        cols = slice(h * HEAD_DIM, (h + 1) * HEAD_DIM)
        q = qkv[pl.ds(start, block), h * HEAD_DIM : (h + 1) * HEAD_DIM]
        k = qkv[pl.ds(at, block), width + h * HEAD_DIM : width + (h + 1) * HEAD_DIM]
        v = qkv[pl.ds(at, block), 2 * width + h * HEAD_DIM : 2 * width + (h + 1) * HEAD_DIM]
        g = grad[pl.ds(start, block), cols]
        place = (key_place + (j - i) * block).astype(f32) * (slopes[h] * LOG2E)
        s = dot(k, q, NT) * (SCALE * LOG2E) + place
        if masked:
            s = jnp.where(key_place <= query_place, s, masked_value)
        p = jnp.exp2(s - logsum[i, h : h + 1, :])
        ds = (p * (dot(v, g, NT) - delta[i, h : h + 1, :])).astype(bf16)
        dv = dot(p.astype(bf16), g)
        dk = dot(ds, q)
        total_q[pl.ds(start, block), cols] += dot(ds, k, TN)
        return dk, dv

    first = [pair(h, j, True) for h in range(heads)]
    carry = tuple(x for both in first for x in both)

    def step(i, carry):
        new = []
        for h in range(heads):
            dk, dv = pair(h, i, False)
            new += [carry[2 * h] + dk, carry[2 * h + 1] + dv]
        return tuple(new)

    carry = lax.fori_loop(j + 1, high, step, carry)
    for h in range(heads):
        cols = slice(h * HEAD_DIM, (h + 1) * HEAD_DIM)
        grad_qkv[:, cols] = (total_q[pl.ds(at, block), cols] * SCALE).astype(bf16)
        grad_qkv[:, width + h * HEAD_DIM : width + (h + 1) * HEAD_DIM] = (
            carry[2 * h] * SCALE
        ).astype(bf16)
        grad_qkv[:, 2 * width + h * HEAD_DIM : 2 * width + (h + 1) * HEAD_DIM] = carry[
            2 * h + 1
        ].astype(bf16)


def attend_back(qkv, grad, attended, logsum, slopes, kind):
    rows = qkv.shape[0]
    width = qkv.shape[1] // 3
    heads = width // HEAD_DIM
    block = SHORT
    n = rows // block
    return pl.pallas_call(
        functools.partial(attend_back_kernel, heads),
        grid=(n,),
        in_specs=[
            pl.BlockSpec(memory_space=pltpu.SMEM),
            pl.BlockSpec(memory_space=pltpu.SMEM),
            full_spec(qkv.shape),
            full_spec(grad.shape),
            full_spec(attended.shape),
            full_spec(logsum.shape),
        ],
        out_specs=pl.BlockSpec((block, 3 * width), lambda j: (j, 0)),
        out_shape=jax.ShapeDtypeStruct((rows, 3 * width), bf16),
        scratch_shapes=[pltpu.VMEM((rows, width), f32), pltpu.VMEM((n, heads, block), f32)],
        compiler_params=pltpu.CompilerParams(vmem_limit_bytes=56 * MIB),
        cost_estimate=pl.CostEstimate(
            flops=20 * rows * rows * width, bytes_accessed=rows * width * 20, transcendentals=0
        ),
    )(kind, slopes, qkv, grad, attended, logsum)


def middle_kernel(
    x0, x1, x2, x3, a0, a1, a2, a3, g0, g1, g2, g3,
    w_proj, gain, shift, w_expand, bias, w_reduce,
    normed, activated, grad_pre, grad_hid, heads_keep, heads_send, attn_out, sums, grad_bias,
):
    step = pl.program_id(0)
    width = x0.shape[1]
    features = 4 * width
    attn = dot(a0[...], w_proj[0:width, :])
    for k, ref in enumerate((a1, a2, a3), 1):
        attn += dot(ref[...], w_proj[k * width : (k + 1) * width, :])
    attn_out[...] = attn[:, 0:width].astype(attn_out.dtype)
    hidden = attn + jnp.concatenate([ref[...] for ref in (x0, x1, x2, x3)], axis=1).astype(f32)
    centre = hidden - jnp.sum(hidden, axis=1, keepdims=True) * (1.0 / features)
    spread = jnp.sum(centre * centre, axis=1, keepdims=True) * (1.0 / features)
    scale = lax.rsqrt(spread + eps)
    centred = centre * scale
    low = (centred * gain[...] + shift[...]).astype(bf16)
    normed[...] = low
    z = dot(low, w_expand[...]) + bias[...]
    c = 0.7978845608028654
    z2 = z * z
    t = jnp.tanh(z * (c + (c * 0.044715) * z2))
    half = 0.5 + 0.5 * t
    activated[...] = (z * half).astype(bf16)
    slope = half + (0.5 * z) * (1.0 - t * t) * (c + (3.0 * c * 0.044715) * z2)
    grads = jnp.concatenate([ref[...] for ref in (g0, g1, g2, g3)], axis=1)
    gp = slope * dot(grads, w_reduce[...])
    gp_low = gp.astype(bf16)
    grad_pre[...] = gp_low
    gn = dot(gp_low, w_expand[...], NT)
    scaled = gn * gain[...]
    mean_scaled = jnp.sum(scaled, axis=1, keepdims=True) * (1.0 / features)
    mean_both = jnp.sum(scaled * centred, axis=1, keepdims=True) * (1.0 / features)
    back = (scaled - mean_scaled - centred * mean_both) * scale
    back_low = (back + 0.25 * grads.astype(f32)).astype(bf16)
    grad_hid[...] = back_low
    gh = dot(back_low, w_proj[...], NT).astype(bf16)
    heads_keep[:, 0:width] = gh[:, 0:width]
    heads_keep[:, width:] = gh[:, 2 * width : 3 * width]
    heads_send[:, 0:width] = gh[:, width : 2 * width]
    heads_send[:, width:] = gh[:, 3 * width :]

    @pl.when(step == 0)
    def _():
        sums[...] = jnp.zeros_like(sums)
        grad_bias[...] = jnp.zeros_like(grad_bias)

    sums[0:1, :] += jnp.sum(gn * centred, axis=0, keepdims=True)
    sums[1:2, :] += jnp.sum(gn, axis=0, keepdims=True)
    grad_bias[...] += jnp.sum(gp_low.astype(f32), axis=0, keepdims=True)


def middle(x, a, g, w_proj, gain, shift, w_expand, bias, w_reduce):
    rows, width = x[0].shape
    hidden_units = w_expand.shape[1]
    features = 4 * width
    block = SHORT

    def rows_of(columns):
        return pl.BlockSpec((block, columns), lambda i: (i, 0))

    def out(columns, kind=bf16):
        return jax.ShapeDtypeStruct((rows, columns), kind)

    return pl.pallas_call(
        middle_kernel,
        grid=(rows // block,),
        in_specs=[rows_of(width)] * 12
        + [full_spec(v.shape) for v in (w_proj, gain, shift, w_expand, bias, w_reduce)],
        out_specs=[
            rows_of(features),
            rows_of(hidden_units),
            rows_of(hidden_units),
            rows_of(features),
            rows_of(2 * width),
            rows_of(2 * width),
            rows_of(width),
            full_spec((2, features)),
            full_spec((1, hidden_units)),
        ],
        out_shape=[
            out(features),
            out(hidden_units),
            out(hidden_units),
            out(features),
            out(2 * width),
            out(2 * width),
            out(width, f32),
            jax.ShapeDtypeStruct((2, features), f32),
            jax.ShapeDtypeStruct((1, hidden_units), f32),
        ],
        compiler_params=pltpu.CompilerParams(vmem_limit_bytes=60 * MIB),
        cost_estimate=pl.CostEstimate(
            flops=10 * rows * features * hidden_units,
            bytes_accessed=rows * features * 16,
            transcendentals=0,
        ),
    )(*x, *a, *g, w_proj, gain, shift, w_expand, bias, w_reduce)


def finish_kernel(x0, x1, x2, x3, grad_qkv, weight, gain, grad_hid, keep, send, sums):
    step = pl.program_id(0)
    width = x0.shape[1]
    features = 4 * width
    gf = dot(grad_qkv[...], weight[...], NT)
    x = jnp.concatenate([ref[...] for ref in (x0, x1, x2, x3)], axis=1).astype(f32)
    centre = x - jnp.sum(x, axis=1, keepdims=True) * (1.0 / features)
    spread = jnp.sum(centre * centre, axis=1, keepdims=True) * (1.0 / features)
    scale = lax.rsqrt(spread + eps)
    centred = centre * scale
    scaled = gf * gain[...]
    mean_scaled = jnp.sum(scaled, axis=1, keepdims=True) * (1.0 / features)
    mean_both = jnp.sum(scaled * centred, axis=1, keepdims=True) * (1.0 / features)
    back = (scaled - mean_scaled - centred * mean_both) * scale
    total = (back + grad_hid[...].astype(f32)).astype(bf16)
    keep[:, 0:width] = total[:, 0:width]
    keep[:, width:] = total[:, 2 * width : 3 * width]
    send[:, 0:width] = total[:, width : 2 * width]
    send[:, width:] = total[:, 3 * width :]

    @pl.when(step == 0)
    def _():
        sums[...] = jnp.zeros_like(sums)

    sums[0:1, :] += jnp.sum(gf * centred, axis=0, keepdims=True)
    sums[1:2, :] += jnp.sum(gf, axis=0, keepdims=True)


def finish(x, grad_qkv, weight, gain, grad_hid):
    rows, width = x[0].shape
    features = 4 * width
    block = SHORT

    def rows_of(columns):
        return pl.BlockSpec((block, columns), lambda i: (i, 0))

    return pl.pallas_call(
        finish_kernel,
        grid=(rows // block,),
        in_specs=[rows_of(width)] * 4
        + [rows_of(grad_qkv.shape[1]), full_spec(weight.shape), full_spec(gain.shape), rows_of(features)],
        out_specs=[rows_of(2 * width), rows_of(2 * width), full_spec((2, features))],
        out_shape=[
            jax.ShapeDtypeStruct((rows, 2 * width), bf16),
            jax.ShapeDtypeStruct((rows, 2 * width), bf16),
            jax.ShapeDtypeStruct((2, features), f32),
        ],
        compiler_params=pltpu.CompilerParams(vmem_limit_bytes=48 * MIB),
        cost_estimate=pl.CostEstimate(
            flops=2 * rows * features * grad_qkv.shape[1],
            bytes_accessed=rows * features * 8,
            transcendentals=0,
        ),
    )(*x, grad_qkv, weight, gain, grad_hid)


def flip(value, axis, size, mask):
    return lax.ppermute(value, axis, [(k, k ^ mask) for k in range(size)])


def gather_head(piece):
    other_core = flip(piece, "head", 4, 1)
    other_chip = flip(piece, "head", 4, 2)
    return [piece, other_core, other_chip, flip(other_chip, "head", 4, 1)]


def scatter_head(keep, send):
    width = keep.shape[1] // 2
    got = flip(send, "head", 4, 1)
    far = keep[:, width:].astype(f32) + got[:, width:].astype(f32)
    near = keep[:, :width].astype(f32) + got[:, :width].astype(f32)
    return near + flip(far.astype(bf16), "head", 4, 2).astype(f32)


def reorder(value, rank, axis=0, size=4):
    width = value.shape[axis] // size
    return jnp.concatenate(
        [lax.dynamic_slice_in_dim(value, (rank ^ k) * width, width, axis) for k in range(size)], axis
    )


def masks_of(size):
    return [1 << k for k in range(size.bit_length() - 1)]


def gather_dp(value, size):
    blocks = {0: value}
    for mask in reversed(masks_of(size)):
        order = sorted(blocks)
        got = flip(jnp.stack([blocks[k] for k in order]), "dp", size, mask)
        for k, at in enumerate(order):
            blocks[at ^ mask] = got[k]
    return [blocks[k] for k in range(size)]


def scatter_dp(blocks, size):
    held = {k: blocks[k] for k in range(size)}
    for mask in masks_of(size):
        mine = [k for k in sorted(held) if not k & mask]
        got = flip(jnp.stack([held[k ^ mask] for k in mine]).astype(bf16), "dp", size, mask)
        held = {k: held[k] + got[p].astype(f32) for p, k in enumerate(mine)}
    return held[0]


def sum_small(value, dp_size):
    for mask in (1, 2):
        value = value + flip(value, "head", 4, mask)
    return sum_dp(value, dp_size)


def sum_dp(value, dp_size):
    for mask in masks_of(dp_size):
        value = value + flip(value, "dp", dp_size, mask)
    return value


def all_sum_dp(value, dp_size):
    parts = value.reshape(dp_size, value.shape[0] // dp_size, value.shape[1])
    me = lax.axis_index("dp")
    own = scatter_dp(reorder(parts, me, 0, dp_size), dp_size)
    blocks = gather_dp(own.astype(bf16), dp_size)
    return reorder(jnp.concatenate(blocks, 0), me, 0, dp_size).astype(f32)


def shards(
    dp_size,
    layer_in,
    bucket,
    w_query,
    w_key,
    w_value,
    w_proj,
    attn_gain,
    attn_shift,
    ffn_gain,
    ffn_shift,
    w_expand,
    bias_expand,
    w_reduce,
    bias_reduce,
    grad_out,
):
    rank = lax.axis_index("head")
    rows, width = layer_in.shape
    features = 4 * width
    heads_here = w_query.shape[1] // HEAD_DIM
    head_index = rank * heads_here + jnp.arange(heads_here)
    slopes = jnp.exp2(-8.0 * (head_index.astype(f32) + 1.0) / HEADS)

    gain_1 = reorder(attn_gain, rank)[None]
    shift_1 = reorder(attn_shift, rank)[None]
    gain_2 = reorder(ffn_gain, rank)[None]
    shift_2 = reorder(ffn_shift, rank)[None]
    w_qkv = reorder(jnp.concatenate([w_query, w_key, w_value], 1), rank)

    x = gather_head(layer_in.astype(bf16))
    proj = reorder(jnp.concatenate(gather_head(w_proj), 0), rank, 1)
    expand = jnp.concatenate(gather_dp(reorder(w_expand, rank), dp_size), 1)
    reduce = jnp.concatenate(gather_dp(reorder(w_reduce, rank), dp_size), 1)
    bias = jnp.concatenate(gather_dp(bias_expand, dp_size), 1).astype(f32)

    normed_attn, qkv = project(x, gain_1, shift_1, w_qkv)
    g = gather_head(grad_out.astype(bf16))
    attended, logsum = attend(qkv, slopes, bucket)
    a = gather_head(attended)

    normed_ffn, activated, grad_pre, grad_hid, heads_keep, heads_send, attn_out, sums_2, grad_bias = middle(
        x, a, g, proj, gain_2, shift_2, expand, bias, reduce
    )
    grad_heads = scatter_head(heads_keep, heads_send).astype(bf16)

    ffn_partial = dot(activated, reduce, NT).astype(bf16)
    ffn_out = scatter_head(
        jnp.concatenate([ffn_partial[:, :width], ffn_partial[:, 2 * width : 3 * width]], 1),
        jnp.concatenate([ffn_partial[:, width : 2 * width], ffn_partial[:, 3 * width :]], 1),
    )
    layer_out = layer_in + attn_out + ffn_out + bias_reduce

    grad_all = jnp.concatenate(g, 1)
    grad_wide = dot(normed_ffn, grad_pre, TN)
    grad_narrow = dot(grad_all, activated, TN)
    local = w_expand.shape[1]

    def columns_home(value):
        blocks = [value[:, k * local : (k + 1) * local] for k in range(dp_size)]
        return scatter_dp(blocks, dp_size)

    grad_expand = reorder(columns_home(grad_wide), rank)
    grad_reduce = reorder(columns_home(grad_narrow), rank)
    grad_bias_expand = columns_home(grad_bias)

    proj_part = reorder(dot(jnp.concatenate(a, 1), grad_hid, TN), rank, 1).astype(bf16)
    proj_sum = scatter_head(
        jnp.concatenate([proj_part[:width].T, proj_part[2 * width : 3 * width].T], 1),
        jnp.concatenate([proj_part[width : 2 * width].T, proj_part[3 * width :].T], 1),
    ).T
    grad_proj = all_sum_dp(proj_sum, dp_size)

    grad_qkv = attend_back(qkv, grad_heads, attended, logsum, slopes, bucket)
    weight_grad = reorder(dot(normed_attn, grad_qkv, TN), rank)
    weight_grad = all_sum_dp(weight_grad, dp_size)
    grad_query, grad_key, grad_value = (
        weight_grad[:, k * heads_here * HEAD_DIM : (k + 1) * heads_here * HEAD_DIM] for k in range(3)
    )
    keep, send, sums_1 = finish(x, grad_qkv, w_qkv, gain_1, grad_hid)
    grad_in = scatter_head(keep, send)

    small = sum_small(
        reorder(jnp.concatenate([sums_2, sums_1], 0), rank, 1), dp_size
    )
    grad_bias_reduce = sum_dp(jnp.sum(grad_out, axis=0), dp_size)
    return (
        layer_out,
        grad_in,
        grad_query,
        grad_key,
        grad_value,
        grad_proj,
        small[2],
        small[3],
        small[0],
        small[1],
        grad_expand,
        grad_bias_expand,
        grad_reduce,
        grad_bias_reduce,
    )


def solution(mesh):
    placed = (
        P("dp", "head"),
        P("dp"),
        P(None, "head"),
        P(None, "head"),
        P(None, "head"),
        P("head", None),
        P(),
        P(),
        P(),
        P(),
        P(None, ("dp", "head")),
        P(None, ("dp", "head")),
        P(None, ("dp", "head")),
        P("head"),
        P("dp", "head"),
    )
    return jax.shard_map(
        functools.partial(shards, mesh.shape["dp"]),
        mesh=mesh,
        in_specs=placed,
        out_specs=(
            P("dp", "head"),
            P("dp", "head"),
            P(None, "head"),
            P(None, "head"),
            P(None, "head"),
            P("head", None),
            P(),
            P(),
            P(),
            P(),
            P(None, ("dp", "head")),
            P(None, ("dp", "head")),
            P(None, ("dp", "head")),
            P("head"),
        ),
        check_vma=False,
    )
```

time: 1520 us -> 565 us (0.37)
  waiting for transfers between devices: 627 us -> 229 us
  matrix products: 391 us -> 53.2 us
  blocking collectives: 176 us -> 0 us
  other arithmetic: 165 us -> 47 us
  Pallas kernels: 0 us -> 104 us
  starting transfers between devices: 12.5 us -> 93.6 us
  local copies, waits for them, and re-layouts: 99.9 us -> 31.7 us
  loops' own time: 21.5 us -> 0 us
    reduce_scatter x3 -> x0, waiting for transfers between devices: 408 us -> none  [the longest x1 182 us: shards(): lax.psum_scatter(grad_wide, ('dp', 'head'), scatter_dimension=1, tiled=True)]
    dot_general x60 -> x5, matrix products: 391 us -> 53.2 us  [dot(): return lax.dot_general(left, right, dims, preferred_element_type=f32)]
    ppermute x0 -> x58, waiting for transfers between devices: none -> 229 us  [flip(): return lax.ppermute(value, axis, [(k, k ^ mask) for k in range(size)])]
    all_gather x4 -> x0, waiting for transfers between devices: 207 us -> none  [the longest x1 85.7 us: shards(): whole_in = lax.all_gather(layer_in, 'head', axis=1, tiled=True)]
    pallas_call x0 -> x5, Pallas kernels: none -> 104 us  [the longest x1 50.7 us: middle(): pl.pallas_call(middle_kernel, grid=(rows // block,), in_specs=[rows_of(wi...]
    psum x2 -> x0, blocking collectives: 101 us -> none  [the longest x1 77.2 us: shards(): lax.psum((grad_ffn_gain, grad_ffn_shift), ('dp', 'head'))]
    ppermute x0 -> x58, starting transfers between devices: none -> 93.6 us  [flip(): return lax.ppermute(value, axis, [(k, k ^ mask) for k in range(size)])]
    convert_element_type x25 -> x13, other arithmetic: 78.1 us -> 14.9 us  [the longest x4 5.73 us: scatter_head(): return near + flip(far.astype(bf16), 'head', 4, 2).astype(f32)]
  transfers between devices with their start and end apart: 13 -> 58, of which waited for: 7 -> 27; matrix products, arithmetic and copies ran while one was open for 27% -> 16% of each run, Pallas kernels for 0% -> 10%
where the time goes in v1:
time: 565 us; the launch traced here: 562 us
  waiting for transfers between devices  229 us (41%)
  Pallas kernels  104 us (18%)
  starting transfers between devices  93.6 us (17%)
  matrix products  53.2 us (9%)
  other arithmetic  47 us (8%)
  local copies, waits for them, and re-layouts  31.7 us (6%)
    ppermute x58, waiting for transfers between devices, flip(): return lax.ppermute(value, axis, [(k, k ^ mask) for k in range(size)])  229 us
    ppermute x58, starting transfers between devices, flip(): return lax.ppermute(value, axis, [(k, k ^ mask) for k in range(size)])  93.6 us
    dot_general x5, matrix products, dot(): return lax.dot_general(left, right, dims, preferred_element_type=f32)  53.2 us
    pallas_call x1, Pallas kernels, middle(): pl.pallas_call(middle_kernel, grid=(rows // block,), in_specs=[rows_of(wi...  50.7 us
    unnamed x150, local copies, waits for them, and re-layouts  22.2 us
    pallas_call x1, Pallas kernels, attend_back(): pl.pallas_call(functools.partial(attend_back_kernel, heads), grid=(n,), i...  16.8 us
    pallas_call x1, Pallas kernels, finish(): pl.pallas_call(finish_kernel, grid=(rows // block,), in_specs=[rows_of(wi...  15.8 us
    pallas_call x1, Pallas kernels, project(): pl.pallas_call(project_kernel, grid=(rows // block,), in_specs=[pl.BlockS...  11.7 us
  transfers between devices with their start and end apart: 58, of which 27 were waited for; matrix products, arithmetic and copies ran while one was open for 16% of the time, Pallas kernels for 10%

profile of v1, /device:TPU:0, one launch (start us, length us, event | category | flops | bytes accessed | tf_op | source)
XLA Modules:
  0.0 561.5 jit_solution(9875445622390868789)
XLA Ops:
  1.2 2.6 collective-permute-start.10
  3.8 2.6 collective-permute-start.15
  6.4 4.5 fusion.78
  13.2 2.2 constant_dynamic-update-slice_fusion.6
  24.8 2.5 collective-permute-done.17
  29.0 1.9 collective-permute-done.56
  30.9 3.3 collective-permute-start.12
  34.2 10.3 %collective-permute-done.18 = bf16[1,1024,128]{2,1,0:T(8,128)(2,1)S(1)} collective-permute-done((bf16[1,1024,128]{2,1,0:T(8,128)(2,1)}, bf16[1,1024,128]{2,1,0:T(8,128)(2,1)S(1)}, u32[]{:S(2)}, u32[]{:S(2)}) %collective-permute-start.18) | collective-permute-done | bytes 262176 | tf_op jit(solution)/shard_map/ppermute | solution.py:401
  45.6 3.5 collective-permute-done.57
  51.6 2.1 collective-permute-start.13
  56.0 8.0 %collective-permute-done.19 = bf16[2,1024,128]{2,1,0:T(8,128)(2,1)S(1)} collective-permute-done((bf16[2,1024,128]{2,1,0:T(8,128)(2,1)S(1)}, bf16[2,1024,128]{2,1,0:T(8,128)(2,1)S(1)}, u32[]{:S(2)}, u32[]{:S(2)}) %collective-permute-start.19) | collective-permute-done | bytes 524320 | tf_op jit(solution)/shard_map/ppermute | solution.py:401
  65.1 7.9 %collective-permute-done.13 = bf16[2,1024,128]{2,1,0:T(8,128)(2,1)S(1)} collective-permute-done((bf16[2,1024,128]{2,1,0:T(8,128)(2,1)S(1)}, bf16[2,1024,128]{2,1,0:T(8,128)(2,1)S(1)}, u32[]{:S(2)}, u32[]{:S(2)}) %collective-permute-start.13) | collective-permute-done | bytes 524320 | tf_op jit(solution)/shard_map/ppermute | solution.py:401
  77.7 9.8 %collective-permute-done.7.g2 = bf16[3072,256]{1,0:T(8,128)(2,1)} collective-permute-done((bf16[3072,256]{1,0:T(8,128)(2,1)}, bf16[3072,256]{1,0:T(8,128)(2,1)}, u32[]{:S(2)}, u32[]{:S(2)}) %collective-permute-start.7) | collective-permute-done | bytes 1572896 | tf_op jit(solution)/shard_map/ppermute | solution.py:401
  89.0 11.7 %shard_map.254 = (bf16[3072,1024]{1,0:T(8,128)(2,1)}, bf16[3072,768]{1,0:T(8,128)(2,1)S(1)}) custom-call(bf16[3072,256]{1,0:T(8,128)(2,1)S(1)} %convert_element_type.413.x0, bf16[3072,256]{1,0:T(8,128)(2,1)S(1)} %collective-permute-done.x1, bf16[3072,256]{1,0:T(8,128)(2,1)} %collective-permute-done.1.x2, bf16[3072,256]{1,0:T(8,128)(2,1)S(1)} %collective-permute-done.2.x3, ...), custom_call_target="tpu_custom_call" | custom-call | flops 4831838208 | bytes 12582912 | tf_op jit(solution)/shard_map/pallas_call | solution.py:53
  100.7 2.2 copy-done.9
  102.8 9.4 %shard_map.255 = (bf16[3072,256]{1,0:T(8,128)(2,1)S(1)}, f32[6,2,512]{2,1,0:T(2,128)S(1)}) custom-call(s32[1]{0:T(128)S(6)} %copy.95.kind, f32[2]{0:T(128)S(1)} %multiply_exponential_fusion.slopes, bf16[3072,768]{1,0:T(8,128)(2,1)} %copy-done.9), custom_call_target="tpu_custom_call" | custom-call | flops 19327352832 | bytes 6291456 | tf_op jit(solution)/shard_map/pallas_call | solution.py:128
  118.3 30.6 %collective-permute-done.4.a2 = bf16[3072,256]{1,0:T(8,128)(2,1)S(1)} collective-permute-done((bf16[3072,256]{1,0:T(8,128)(2,1)S(1)}, bf16[3072,256]{1,0:T(8,128)(2,1)S(1)}, u32[]{:S(2)}, u32[]{:S(2)}) %collective-permute-start.4) | collective-permute-done | bytes 1572896 | tf_op jit(solution)/shard_map/ppermute | solution.py:401
  155.9 50.7 %shard_map.256 = (bf16[3072,1024]{1,0:T(8,128)(2,1)}, bf16[3072,1024]{1,0:T(8,128)(2,1)}, bf16[3072,1024]{1,0:T(8,128)(2,1)}, bf16[3072,1024]{1,0:T(8,128)(2,1)}...) custom-call(bf16[3072,256]{1,0:T(8,128)(2,1)} %copy-done, ...), custom_call_target="tpu_custom_call" | custom-call | flops 32212254720 | bytes 50331648 | tf_op jit(solution)/shard_map/pallas_call | solution.py:308
  206.6 10.7 %fusion = bf16[1024,1024]{0,1:T(8,128)(2,1)S(1)} fusion(bf16[3072,1024]{1,0:T(8,128)(2,1)} %get-tuple-element.37.grad_hid, bf16[3072,256]{1,0:T(8,128)(2,1)} %copy-done.47, bf16[3072,256]{1,0:T(8,128)(2,1)} %copy-done.45, bf16[3072,256]{1,0:T(8,128)(2,1)} %copy-done.46, bf16[3072,256]{1,0:T(8,128)(2,1)S(1)} %copy-done.7), kind=kOutput, calls=%fused_computation | convolution fusion | flops 6467616768 | bytes 14680064 | tf_op jit(solution)/shard_map/dot_general | solution.py:28
  219.0 9.9 %convolution_convert_fusion = bf16[3072,1024]{1,0:T(8,128)(2,1)S(1)} fusion(bf16[3072,1024]{1,0:T(8,128)(2,1)} %get-tuple-element.33, bf16[1024,1024]{1,0:T(8,128)(2,1)S(1)} %copy-done.36), kind=kOutput, calls=%fused_computation.16 | convolution fusion | flops 6445596672 | bytes 14680064 | tf_op jit(solution)/shard_map/dot_general | solution.py:28
  228.9 12.8 %fusion.91 = (bf16[1024,1024]{1,0:T(8,128)(2,1)S(1)}, f32[1024,1024]{1,0:T(8,128)S(1)}) fusion(bf16[3072,1024]{1,0:T(8,128)(2,1)} %get-tuple-element.33, bf16[3072,256]{1,0:T(8,128)(2,1)} %collective-permute-done.8.g3, bf16[3072,256]{1,0:T(8,128)(2,1)} %collective-permute-done.7.g2, bf16[3072,256]{1,0:T(8,128)(2,1)} %collective-permute-done.6.g1, ...), kind=kOutput, calls=%fused_computation.303 | convolution fusion | flops 6468665344 | bytes 18874368 | tf_op jit(solution)/shard_map/dot_general | solution.py:28
  242.4 17.4 %collective-permute-start.49 = (bf16[4,1,128]{2,1,0:T(2,128)(2,1)S(1)}, bf16[4,1,128]{2,1,0:T(2,128)(2,1)S(1)}, u32[]{:S(2)}, u32[]{:S(2)}) collective-permute-start(bf16[4,1,128]{2,1,0:T(2,128)(2,1)S(1)} %pad_maximum_fusion.32), channel_id=1, source_target_pairs={{0,4},{4,0},{8,12},{12,8},{16,20},{20,16},{24,28},{28,24},{1,5},{5... | collective-permute-start | bytes 3080 | tf_op jit(solution)/shard_map/ppermute | solution.py:401
  260.9 10.9 %fusion.90 = (bf16[1024,1024]{1,0:T(8,128)(2,1)S(1)}, f32[1024,1024]{1,0:T(8,128)S(1)}) fusion(bf16[3072,1024]{1,0:T(8,128)(2,1)} %get-tuple-element.43, bf16[3072,1024]{1,0:T(8,128)(2,1)} %get-tuple-element.44), kind=kOutput, calls=%fused_computation.302 | convolution fusion | flops 6443499520 | bytes 18874368 | tf_op jit(solution)/shard_map/dot_general | solution.py:28
  276.8 1.9 pad_maximum_fusion
  281.9 4.5 collective-permute-done.52
  287.4 21.0 %collective-permute-done.46 = bf16[4,1024,128]{2,1,0:T(8,128)(2,1)S(1)} collective-permute-done((bf16[4,1024,128]{2,1,0:T(8,128)(2,1)S(1)}, bf16[4,1024,128]{2,1,0:T(8,128)(2,1)S(1)}, u32[]{:S(2)}, u32[]{:S(2)}) %collective-permute-start.46) | collective-permute-done | bytes 1048608 | tf_op jit(solution)/shard_map/ppermute | solution.py:401
  312.8 3.2 collective-permute-start.54
  316.0 2.1 collective-permute-done.35
  318.3 13.7 %collective-permute-done.47 = bf16[2,1024,128]{2,1,0:T(8,128)(2,1)S(1)} collective-permute-done((bf16[2,1024,128]{2,1,0:T(8,128)(2,1)S(1)}, bf16[2,1024,128]{2,1,0:T(8,128)(2,1)S(1)}, u32[]{:S(2)}, u32[]{:S(2)}) %collective-permute-start.47) | collective-permute-done | bytes 524320 | tf_op jit(solution)/shard_map/ppermute | solution.py:401
  333.8 2.4 collective-permute-start.37
  337.5 10.4 %collective-permute-done.37 = bf16[1,32,1024]{2,1,0:T(8,128)(2,1)S(1)} collective-permute-done((bf16[1,32,1024]{2,1,0:T(8,128)(2,1)S(1)}, bf16[1,32,1024]{2,1,0:T(8,128)(2,1)S(1)}, u32[]{:S(2)}, u32[]{:S(2)}) %collective-permute-start.37) | collective-permute-done | bytes 65568 | tf_op jit(solution)/shard_map/ppermute | solution.py:401
  349.3 3.9 collective-permute-done.38
  353.4 4.9 collective-permute-done.39
  365.0 31.1 %collective-permute-done.24 = bf16[3072,256]{1,0:T(8,128)(2,1)S(1)} collective-permute-done((bf16[3072,256]{1,0:T(8,128)(2,1)S(1)}, bf16[3072,256]{1,0:T(8,128)(2,1)S(1)}, u32[]{:S(2)}, u32[]{:S(2)}) %collective-permute-start.24) | collective-permute-done | bytes 1572896 | tf_op jit(solution)/shard_map/ppermute | solution.py:401
  396.1 3.1 add_convert_fusion.1.grad
  399.2 16.8 %shard_map.257.grad_qkv = bf16[3072,768]{1,0:T(8,128)(2,1)} custom-call(s32[1]{0:T(128)S(6)} %copy.95.kind, f32[2]{0:T(128)} %copy-done.8, bf16[3072,768]{1,0:T(8,128)(2,1)} %copy-done.9, bf16[3072,256]{1,0:T(8,128)(2,1)} %add_convert_fusion.1.grad, bf16[3072,256]{1,0:T(8,128)(2,1)} %copy-done.6, f32[6,2,512]{2,1,0:T(2,128)} %copy-done.10), custom_call_target="tpu_custom_call" | custom-call | flops 48318382080 | bytes 15728640 | tf_op jit(solution)/shard_map/pallas_call | solution.py:222
  416.1 8.9 %fusion.92 = f32[1024,768]{1,0:T(8,128)S(1)} fusion(bf16[3072,1024]{1,0:T(8,128)(2,1)} %get-tuple-element.40, bf16[3072,768]{1,0:T(8,128)(2,1)} %shard_map.257.grad_qkv), kind=kOutput, calls=%fused_computation.304 | convolution fusion | flops 4831838208 | bytes 14155776 | tf_op jit(solution)/shard_map/dot_general | solution.py:28
  425.6 27.5 %collective-permute-start.27 = (bf16[4,128,768]{2,1,0:T(8,128)(2,1)S(1)}, bf16[4,128,768]{2,1,0:T(8,128)(2,1)S(1)}, u32[]{:S(2)}, u32[]{:S(2)}) collective-permute-start(bf16[4,128,768]{2,1,0:T(8,128)(2,1)S(1)} %pad_maximum_fusion.10), channel_id=1, source_target_pairs={{0,4},{4,0},{8,12},{12,8},{16,20},{20,16},{24,28},{28,24},{1,5},{5... | collective-permute-start | bytes 2359304 | tf_op jit(solution)/shard_map/ppermute | solution.py:401
  454.1 13.8 %collective-permute-done.27 = bf16[4,128,768]{2,1,0:T(8,128)(2,1)S(1)} collective-permute-done((bf16[4,128,768]{2,1,0:T(8,128)(2,1)S(1)}, bf16[4,128,768]{2,1,0:T(8,128)(2,1)S(1)}, u32[]{:S(2)}, u32[]{:S(2)}) %collective-permute-start.27) | collective-permute-done | bytes 786464 | tf_op jit(solution)/shard_map/ppermute | solution.py:401
  468.2 3.3 add_convert_fusion.3
  472.5 3.7 collective-permute-done.28
  479.0 15.8 %shard_map.258 = (bf16[3072,512]{1,0:T(8,128)(2,1)}, bf16[3072,512]{1,0:T(8,128)(2,1)}, f32[2,1024]{1,0:T(2,128)S(1)}) custom-call(bf16[3072,256]{1,0:T(8,128)(2,1)S(1)} %copy-done.1, bf16[3072,256]{1,0:T(8,128)(2,1)S(1)} %copy-done.4, bf16[3072,256]{1,0:T(8,128)(2,1)} %collective-permute-done.1.x2, bf16[3072,256]{1,0:T(8,128)(2,1)} %copy-done.5, ...), custom_call_target="tpu_custom_call" | custom-call | flops 4831838208 | bytes 25165824 | tf_op jit(solution)/shard_map/pallas_call | solution.py:380
  497.8 7.0 %collective-permute-done.30 = bf16[1,128,768]{2,1,0:T(8,128)(2,1)S(1)} collective-permute-done((bf16[1,128,768]{2,1,0:T(8,128)(2,1)S(1)}, bf16[1,128,768]{2,1,0:T(8,128)(2,1)S(1)}, u32[]{:S(2)}, u32[]{:S(2)}) %collective-permute-start.30) | collective-permute-done | bytes 196640 | tf_op jit(solution)/shard_map/ppermute | solution.py:401
  516.0 2.1 convert_element_type.462
  520.8 4.3 add_add_fusion
  525.8 5.3 collective-permute-done.32
  534.7 24.3 %collective-permute-done.26 = bf16[3072,256]{1,0:T(8,128)(2,1)S(1)} collective-permute-done((bf16[3072,256]{1,0:T(8,128)(2,1)S(1)}, bf16[3072,256]{1,0:T(8,128)(2,1)S(1)}, u32[]{:S(2)}, u32[]{:S(2)}) %collective-permute-start.26) | collective-permute-done | bytes 1572896 | tf_op jit(solution)/shard_map/ppermute | solution.py:401
  558.9 2.2 convert_add_fusion
  (337 shorter events, 93.7 us)
Async XLA Ops:
  0.6 49.7 %collective-permute-start.9 = (bf16[256,1024]{1,0:T(8,128)(2,1)}, bf16[256,1024]{1,0:T(8,128)(2,1)}, u32[]{:S(2)}, u32[]{:S(2)}) collective-permute-start(bf16[256,1024]{1,0:T(8,128)(2,1)} %param.20), channel_id=1, source_target_pairs={{0,1},{1,0},{2,3},{3,2},{4,5},{5,4},{6,7},{7,6},{8,9},{9,8},{10,11... | collective-permute-start | bytes 1572872 | tf_op jit(solution)/shard_map/ppermute | solution.py:401
  1.2 50.5 %collective-permute-start.10 = (bf16[256,1024]{1,0:T(8,128)(2,1)}, bf16[256,1024]{1,0:T(8,128)(2,1)}, u32[]{:S(2)}, u32[]{:S(2)}) collective-permute-start(bf16[256,1024]{1,0:T(8,128)(2,1)} %param.20), channel_id=1, source_target_pairs={{0,2},{1,3},{2,0},{3,1},{4,6},{5,7},{6,4},{7,5},{8,10},{9,11},{10,... | collective-permute-start | bytes 1572872 | tf_op jit(solution)/shard_map/ppermute | solution.py:401
  3.8 16.3 %collective-permute-start.15 = (bf16[1,1,128]{2,1,0:T(2,128)(2,1)}, bf16[1,1,128]{2,1,0:T(2,128)(2,1)S(1)}, u32[]{:S(2)}, u32[]{:S(2)}) collective-permute-start(bf16[1,1,128]{2,1,0:T(2,128)(2,1)} %bitcast.343), channel_id=1, source_target_pairs={{0,16},{4,20},{8,24},{12,28},{16,0},{20,4},{24,8},{28,12},{1,17},{... | collective-permute-start | bytes 776 | tf_op jit(solution)/shard_map/ppermute | solution.py:401
  10.9 13.4 %collective-permute-start.55 = (f32[256]{0:T(256)S(1)}, f32[256]{0:T(256)S(1)}, u32[]{:S(2)}, u32[]{:S(2)}) collective-permute-start(f32[256]{0:T(256)S(1)} %get-tuple-element.58), channel_id=1, source_target_pairs={{0,4},{4,0},{8,12},{12,8},{16,20},{20,16},{24,28},{28,24},{1,5},{5... | collective-permute-start | bytes 3080 | tf_op jit(solution)/shard_map/ppermute | solution.py:401
  12.6 38.8 %collective-permute-start.1 = (bf16[3072,256]{1,0:T(8,128)(2,1)S(1)}, bf16[3072,256]{1,0:T(8,128)(2,1)}, u32[]{:S(2)}, u32[]{:S(2)}) collective-permute-start(bf16[3072,256]{1,0:T(8,128)(2,1)S(1)} %convert_element_type.413.x0), channel_id=1, source_target_pairs={{0,2},{1,3},{2,0},{3,1},{4,6},{5,7},{6,4},{7,5},{8,10},{9,11},{10,... | collective-permute-start | bytes 4718600 | tf_op jit(solution)/shard_map/ppermute | solution.py:401
  24.3 20.3 %collective-permute-start.18 = (bf16[1,1024,128]{2,1,0:T(8,128)(2,1)}, bf16[1,1024,128]{2,1,0:T(8,128)(2,1)S(1)}, u32[]{:S(2)}, u32[]{:S(2)}) collective-permute-start(bf16[1,1024,128]{2,1,0:T(8,128)(2,1)} %get-tuple-element.113), channel_id=1, source_target_pairs={{0,16},{4,20},{8,24},{12,28},{16,0},{20,4},{24,8},{28,12},{1,17},{... | collective-permute-start | bytes 786440 | tf_op jit(solution)/shard_map/ppermute | solution.py:401
  30.9 19.4 %collective-permute-start.12 = (bf16[1,1024,128]{2,1,0:T(8,128)(2,1)S(1)}, bf16[1,1024,128]{2,1,0:T(8,128)(2,1)S(1)}, u32[]{:S(2)}, u32[]{:S(2)}) collective-permute-start(bf16[1,1024,128]{2,1,0:T(8,128)(2,1)S(1)} %get-tuple-element.119), channel_id=1, source_target_pairs={{0,16},{4,20},{8,24},{12,28},{16,0},{20,4},{24,8},{28,12},{1,17},{... | collective-permute-start | bytes 786440 | tf_op jit(solution)/shard_map/ppermute | solution.py:401
  49.1 14.9 %collective-permute-start.19 = (bf16[2,1024,128]{2,1,0:T(8,128)(2,1)S(1)}, bf16[2,1024,128]{2,1,0:T(8,128)(2,1)S(1)}, u32[]{:S(2)}, u32[]{:S(2)}) collective-permute-start(bf16[2,1024,128]{2,1,0:T(8,128)(2,1)S(1)} %pad_maximum_fusion.13), channel_id=1, source_target_pairs={{0,8},{4,12},{8,0},{12,4},{16,24},{20,28},{24,16},{28,20},{1,9},{5... | collective-permute-start | bytes 1572872 | tf_op jit(solution)/shard_map/ppermute | solution.py:401
  50.3 38.6 %collective-permute-start = (bf16[3072,256]{1,0:T(8,128)(2,1)S(1)}, bf16[3072,256]{1,0:T(8,128)(2,1)S(1)}, u32[]{:S(2)}, u32[]{:S(2)}) collective-permute-start(bf16[3072,256]{1,0:T(8,128)(2,1)S(1)} %convert_element_type.413.x0), channel_id=1, source_target_pairs={{0,1},{1,0},{2,3},{3,2},{4,5},{5,4},{6,7},{7,6},{8,9},{9,8},{10,11... | collective-permute-start | bytes 4718600 | tf_op jit(solution)/shard_map/ppermute | solution.py:401
  50.3 37.1 %collective-permute-start.7 = (bf16[3072,256]{1,0:T(8,128)(2,1)}, bf16[3072,256]{1,0:T(8,128)(2,1)}, u32[]{:S(2)}, u32[]{:S(2)}) collective-permute-start(bf16[3072,256]{1,0:T(8,128)(2,1)} %get-tuple-element.59.g0), channel_id=1, source_target_pairs={{0,2},{1,3},{2,0},{3,1},{4,6},{5,7},{6,4},{7,5},{8,10},{9,11},{10,... | collective-permute-start | bytes 4718600 | tf_op jit(solution)/shard_map/ppermute | solution.py:401
  51.4 37.5 %collective-permute-start.2 = (bf16[3072,256]{1,0:T(8,128)(2,1)}, bf16[3072,256]{1,0:T(8,128)(2,1)S(1)}, u32[]{:S(2)}, u32[]{:S(2)}) collective-permute-start(bf16[3072,256]{1,0:T(8,128)(2,1)} %collective-permute-done.1.x2), channel_id=1, source_target_pairs={{0,1},{1,0},{2,3},{3,2},{4,5},{5,4},{6,7},{7,6},{8,9},{9,8},{10,11... | collective-permute-start | bytes 4718600 | tf_op jit(solution)/shard_map/ppermute | solution.py:401
  51.6 21.4 %collective-permute-start.13 = (bf16[2,1024,128]{2,1,0:T(8,128)(2,1)S(1)}, bf16[2,1024,128]{2,1,0:T(8,128)(2,1)S(1)}, u32[]{:S(2)}, u32[]{:S(2)}) collective-permute-start(bf16[2,1024,128]{2,1,0:T(8,128)(2,1)S(1)} %pad_maximum_fusion.12), channel_id=1, source_target_pairs={{0,8},{4,12},{8,0},{12,4},{16,24},{20,28},{24,16},{28,20},{1,9},{5... | collective-permute-start | bytes 1572872 | tf_op jit(solution)/shard_map/ppermute | solution.py:401
  64.0 10.2 %collective-permute-start.11 = (bf16[256,1024]{1,0:T(8,128)(2,1)}, bf16[256,1024]{1,0:T(8,128)(2,1)S(1)}, u32[]{:S(2)}, u32[]{:S(2)}) collective-permute-start(bf16[256,1024]{1,0:T(8,128)(2,1)} %collective-permute-done.10), channel_id=1, source_target_pairs={{0,1},{1,0},{2,3},{3,2},{4,5},{5,4},{6,7},{7,6},{8,9},{9,8},{10,11... | collective-permute-start | bytes 1572872 | tf_op jit(solution)/shard_map/ppermute | solution.py:401
  73.1 80.6 %collective-permute-start.6 = (bf16[3072,256]{1,0:T(8,128)(2,1)S(1)}, bf16[3072,256]{1,0:T(8,128)(2,1)}, u32[]{:S(2)}, u32[]{:S(2)}) collective-permute-start(bf16[3072,256]{1,0:T(8,128)(2,1)S(1)} %copy-done.19), channel_id=1, source_target_pairs={{0,1},{1,0},{2,3},{3,2},{4,5},{5,4},{6,7},{7,6},{8,9},{9,8},{10,11... | collective-permute-start | bytes 4718600 | tf_op jit(solution)/shard_map/ppermute | solution.py:401
  74.2 39.1 %collective-permute-start.20 = (bf16[4,1024,128]{2,1,0:T(8,128)(2,1)}, bf16[4,1024,128]{2,1,0:T(8,128)(2,1)}, u32[]{:S(2)}, u32[]{:S(2)}) collective-permute-start(bf16[4,1024,128]{2,1,0:T(8,128)(2,1)} %pad_maximum_fusion.6), channel_id=1, source_target_pairs={{0,4},{4,0},{8,12},{12,8},{16,20},{20,16},{24,28},{28,24},{1,5},{5... | collective-permute-start | bytes 3145736 | tf_op jit(solution)/shard_map/ppermute | solution.py:401
  87.4 61.5 %collective-permute-start.14 = (bf16[4,1024,128]{2,1,0:T(8,128)(2,1)}, bf16[4,1024,128]{2,1,0:T(8,128)(2,1)}, u32[]{:S(2)}, u32[]{:S(2)}) collective-permute-start(bf16[4,1024,128]{2,1,0:T(8,128)(2,1)} %pad_maximum_fusion.5), channel_id=1, source_target_pairs={{0,4},{4,0},{8,12},{12,8},{16,20},{20,16},{24,28},{28,24},{1,5},{5... | collective-permute-start | bytes 3145736 | tf_op jit(solution)/shard_map/ppermute | solution.py:401
  88.9 64.7 %collective-permute-start.8 = (bf16[3072,256]{1,0:T(8,128)(2,1)}, bf16[3072,256]{1,0:T(8,128)(2,1)}, u32[]{:S(2)}, u32[]{:S(2)}) collective-permute-start(bf16[3072,256]{1,0:T(8,128)(2,1)} %collective-permute-done.7.g2), channel_id=1, source_target_pairs={{0,1},{1,0},{2,3},{3,2},{4,5},{5,4},{6,7},{7,6},{8,9},{9,8},{10,11... | collective-permute-start | bytes 4718600 | tf_op jit(solution)/shard_map/ppermute | solution.py:401
  112.2 36.7 %collective-permute-start.4 = (bf16[3072,256]{1,0:T(8,128)(2,1)S(1)}, bf16[3072,256]{1,0:T(8,128)(2,1)S(1)}, u32[]{:S(2)}, u32[]{:S(2)}) collective-permute-start(bf16[3072,256]{1,0:T(8,128)(2,1)S(1)} %get-tuple-element.31.a0.attended), channel_id=1, source_target_pairs={{0,2},{1,3},{2,0},{3,1},{4,6},{5,7},{6,4},{7,5},{8,10},{9,11},{10,... | collective-permute-start | bytes 4718600 | tf_op jit(solution)/shard_map/ppermute | solution.py:401
  117.9 35.8 %collective-permute-start.3 = (bf16[3072,256]{1,0:T(8,128)(2,1)S(1)}, bf16[3072,256]{1,0:T(8,128)(2,1)S(1)}, u32[]{:S(2)}, u32[]{:S(2)}) collective-permute-start(bf16[3072,256]{1,0:T(8,128)(2,1)S(1)} %get-tuple-element.31.a0.attended), channel_id=1, source_target_pairs={{0,1},{1,0},{2,3},{3,2},{4,5},{5,4},{6,7},{7,6},{8,9},{9,8},{10,11... | collective-permute-start | bytes 4718600 | tf_op jit(solution)/shard_map/ppermute | solution.py:401
  242.4 29.6 %collective-permute-start.49 = (bf16[4,1,128]{2,1,0:T(2,128)(2,1)S(1)}, bf16[4,1,128]{2,1,0:T(2,128)(2,1)S(1)}, u32[]{:S(2)}, u32[]{:S(2)}) collective-permute-start(bf16[4,1,128]{2,1,0:T(2,128)(2,1)S(1)} %pad_maximum_fusion.32), channel_id=1, source_target_pairs={{0,4},{4,0},{8,12},{12,8},{16,20},{20,16},{24,28},{28,24},{1,5},{5... | collective-permute-start | bytes 3080 | tf_op jit(solution)/shard_map/ppermute | solution.py:401
  260.1 20.5 %collective-permute-start.33 = (bf16[1024,512]{1,0:T(8,128)(2,1)S(1)}, bf16[1024,512]{1,0:T(8,128)(2,1)S(1)}, u32[]{:S(2)}, u32[]{:S(2)}) collective-permute-start(bf16[1024,512]{1,0:T(8,128)(2,1)S(1)} %pad_maximum_fusion.7), channel_id=1, source_target_pairs={{0,1},{1,0},{2,3},{3,2},{4,5},{5,4},{6,7},{7,6},{8,9},{9,8},{10,11... | collective-permute-start | bytes 3145736 | tf_op jit(solution)/shard_map/ppermute | solution.py:401
  260.3 26.0 %collective-permute-start.52 = (bf16[4,1024,128]{2,1,0:T(8,128)(2,1)S(1)}, bf16[4,1024,128]{2,1,0:T(8,128)(2,1)S(1)}, u32[]{:S(2)}, u32[]{:S(2)}) collective-permute-start(bf16[4,1024,128]{2,1,0:T(8,128)(2,1)S(1)} %pad_maximum_fusion.9), channel_id=1, source_target_pairs={{0,4},{4,0},{8,12},{12,8},{16,20},{20,16},{24,28},{28,24},{1,5},{5... | collective-permute-start | bytes 3145736 | tf_op jit(solution)/shard_map/ppermute | solution.py:401
  272.3 36.2 %collective-permute-start.46 = (bf16[4,1024,128]{2,1,0:T(8,128)(2,1)S(1)}, bf16[4,1024,128]{2,1,0:T(8,128)(2,1)S(1)}, u32[]{:S(2)}, u32[]{:S(2)}) collective-permute-start(bf16[4,1024,128]{2,1,0:T(8,128)(2,1)S(1)} %pad_maximum_fusion.8), channel_id=1, source_target_pairs={{0,4},{4,0},{8,12},{12,8},{16,20},{20,16},{24,28},{28,24},{1,5},{5... | collective-permute-start | bytes 3145736 | tf_op jit(solution)/shard_map/ppermute | solution.py:401
  278.8 189.4 %collective-permute-start.21 = (bf16[3072,512]{1,0:T(8,128)(2,1)}, bf16[3072,512]{1,0:T(8,128)(2,1)}, u32[]{:S(2)}, u32[]{:S(2)}) collective-permute-start(bf16[3072,512]{1,0:T(8,128)(2,1)} %pad_maximum_fusion), channel_id=1, source_target_pairs={{0,1},{1,0},{2,3},{3,2},{4,5},{5,4},{6,7},{7,6},{8,9},{9,8},{10,11... | collective-permute-start | bytes 9437192 | tf_op jit(solution)/shard_map/ppermute | solution.py:401
  280.1 79.3 %collective-permute-start.23 = (bf16[3072,512]{1,0:T(8,128)(2,1)}, bf16[3072,512]{1,0:T(8,128)(2,1)}, u32[]{:S(2)}, u32[]{:S(2)}) collective-permute-start(bf16[3072,512]{1,0:T(8,128)(2,1)} %get-tuple-element.35), channel_id=1, source_target_pairs={{0,1},{1,0},{2,3},{3,2},{4,5},{5,4},{6,7},{7,6},{8,9},{9,8},{10,11... | collective-permute-start | bytes 9437192 | tf_op jit(solution)/shard_map/ppermute | solution.py:401
  280.8 28.7 %collective-permute-start.34 = (bf16[1024,256]{1,0:T(8,128)(2,1)S(1)}, bf16[1024,256]{1,0:T(8,128)(2,1)S(1)}, u32[]{:S(2)}, u32[]{:S(2)}) collective-permute-start(bf16[1024,256]{1,0:T(8,128)(2,1)S(1)} %fusion.16), channel_id=1, source_target_pairs={{0,2},{1,3},{2,0},{3,1},{4,6},{5,7},{6,4},{7,5},{8,10},{9,11},{10,... | collective-permute-start | bytes 1572872 | tf_op jit(solution)/shard_map/ppermute | solution.py:401
  287.4 24.2 %collective-permute-start.53 = (bf16[2,1024,128]{2,1,0:T(8,128)(2,1)}, bf16[2,1024,128]{2,1,0:T(8,128)(2,1)}, u32[]{:S(2)}, u32[]{:S(2)}) collective-permute-start(bf16[2,1024,128]{2,1,0:T(8,128)(2,1)} %pad_maximum_fusion.16), channel_id=1, source_target_pairs={{0,8},{4,12},{8,0},{12,4},{16,24},{20,28},{24,16},{28,20},{1,9},{5... | collective-permute-start | bytes 1572872 | tf_op jit(solution)/shard_map/ppermute | solution.py:401
  310.2 8.0 %collective-permute-start.35 = (bf16[4,32,1024]{2,1,0:T(8,128)(2,1)S(1)}, bf16[4,32,1024]{2,1,0:T(8,128)(2,1)S(1)}, u32[]{:S(2)}, u32[]{:S(2)}) collective-permute-start(bf16[4,32,1024]{2,1,0:T(8,128)(2,1)S(1)} %pad_maximum_fusion.22), channel_id=1, source_target_pairs={{0,4},{4,0},{8,12},{12,8},{16,20},{20,16},{24,28},{28,24},{1,5},{5... | collective-permute-start | bytes 786440 | tf_op jit(solution)/shard_map/ppermute | solution.py:401
  311.5 20.5 %collective-permute-start.47 = (bf16[2,1024,128]{2,1,0:T(8,128)(2,1)S(1)}, bf16[2,1024,128]{2,1,0:T(8,128)(2,1)S(1)}, u32[]{:S(2)}, u32[]{:S(2)}) collective-permute-start(bf16[2,1024,128]{2,1,0:T(8,128)(2,1)S(1)} %pad_maximum_fusion.14), channel_id=1, source_target_pairs={{0,8},{4,12},{8,0},{12,4},{16,24},{20,28},{24,16},{28,20},{1,9},{5... | collective-permute-start | bytes 1572872 | tf_op jit(solution)/shard_map/ppermute | solution.py:401
  312.8 23.4 %collective-permute-start.54 = (bf16[1,1024,128]{2,1,0:T(8,128)(2,1)S(1)}, bf16[1,1024,128]{2,1,0:T(8,128)(2,1)S(1)}, u32[]{:S(2)}, u32[]{:S(2)}) collective-permute-start(bf16[1,1024,128]{2,1,0:T(8,128)(2,1)S(1)} %fusion.36), channel_id=1, source_target_pairs={{0,16},{4,20},{8,24},{12,28},{16,0},{20,4},{24,8},{28,12},{1,17},{... | collective-permute-start | bytes 786440 | tf_op jit(solution)/shard_map/ppermute | solution.py:401
  318.2 15.6 %collective-permute-start.36 = (bf16[2,32,1024]{2,1,0:T(8,128)(2,1)S(1)}, bf16[2,32,1024]{2,1,0:T(8,128)(2,1)S(1)}, u32[]{:S(2)}, u32[]{:S(2)}) collective-permute-start(bf16[2,32,1024]{2,1,0:T(8,128)(2,1)S(1)} %pad_maximum_fusion.24), channel_id=1, source_target_pairs={{0,8},{4,12},{8,0},{12,4},{16,24},{20,28},{24,16},{28,20},{1,9},{5... | collective-permute-start | bytes 393224 | tf_op jit(solution)/shard_map/ppermute | solution.py:401
  333.1 14.9 %collective-permute-start.48 = (bf16[1,1024,128]{2,1,0:T(8,128)(2,1)S(1)}, bf16[1,1024,128]{2,1,0:T(8,128)(2,1)S(1)}, u32[]{:S(2)}, u32[]{:S(2)}) collective-permute-start(bf16[1,1024,128]{2,1,0:T(8,128)(2,1)S(1)} %fusion.33), channel_id=1, source_target_pairs={{0,16},{4,20},{8,24},{12,28},{16,0},{20,4},{24,8},{28,12},{1,17},{... | collective-permute-start | bytes 786440 | tf_op jit(solution)/shard_map/ppermute | solution.py:401
  333.8 14.0 %collective-permute-start.37 = (bf16[1,32,1024]{2,1,0:T(8,128)(2,1)S(1)}, bf16[1,32,1024]{2,1,0:T(8,128)(2,1)S(1)}, u32[]{:S(2)}, u32[]{:S(2)}) collective-permute-start(bf16[1,32,1024]{2,1,0:T(8,128)(2,1)S(1)} %add_convert_fusion.9), channel_id=1, source_target_pairs={{0,16},{4,20},{8,24},{12,28},{16,0},{20,4},{24,8},{28,12},{1,17},{... | collective-permute-start | bytes 196616 | tf_op jit(solution)/shard_map/ppermute | solution.py:401
  347.9 5.3 collective-permute-start.38
  358.3 6.6 %collective-permute-start.40 = (bf16[4,32,1024]{2,1,0:T(8,128)(2,1)S(1)}, bf16[4,32,1024]{2,1,0:T(8,128)(2,1)S(1)}, u32[]{:S(2)}, u32[]{:S(2)}) collective-permute-start(bf16[4,32,1024]{2,1,0:T(8,128)(2,1)S(1)} %pad_maximum_fusion.23), channel_id=1, source_target_pairs={{0,4},{4,0},{8,12},{12,8},{16,20},{20,16},{24,28},{28,24},{1,5},{5... | collective-permute-start | bytes 786440 | tf_op jit(solution)/shard_map/ppermute | solution.py:401
  361.3 34.8 %collective-permute-start.24 = (bf16[3072,256]{1,0:T(8,128)(2,1)S(1)}, bf16[3072,256]{1,0:T(8,128)(2,1)S(1)}, u32[]{:S(2)}, u32[]{:S(2)}) collective-permute-start(bf16[3072,256]{1,0:T(8,128)(2,1)S(1)} %add_convert_fusion.2), channel_id=1, source_target_pairs={{0,2},{1,3},{2,0},{3,1},{4,6},{5,7},{6,4},{7,5},{8,10},{9,11},{10,... | collective-permute-start | bytes 4718600 | tf_op jit(solution)/shard_map/ppermute | solution.py:401
  425.6 42.3 %collective-permute-start.27 = (bf16[4,128,768]{2,1,0:T(8,128)(2,1)S(1)}, bf16[4,128,768]{2,1,0:T(8,128)(2,1)S(1)}, u32[]{:S(2)}, u32[]{:S(2)}) collective-permute-start(bf16[4,128,768]{2,1,0:T(8,128)(2,1)S(1)} %pad_maximum_fusion.10), channel_id=1, source_target_pairs={{0,4},{4,0},{8,12},{12,8},{16,20},{20,16},{24,28},{28,24},{1,5},{5... | collective-permute-start | bytes 2359304 | tf_op jit(solution)/shard_map/ppermute | solution.py:401
  468.1 8.2 %collective-permute-start.28 = (bf16[2,128,768]{2,1,0:T(8,128)(2,1)S(1)}, bf16[2,128,768]{2,1,0:T(8,128)(2,1)S(1)}, u32[]{:S(2)}, u32[]{:S(2)}) collective-permute-start(bf16[2,128,768]{2,1,0:T(8,128)(2,1)S(1)} %pad_maximum_fusion.18), channel_id=1, source_target_pairs={{0,8},{4,12},{8,0},{12,4},{16,24},{20,28},{24,16},{28,20},{1,9},{5... | collective-permute-start | bytes 1179656 | tf_op jit(solution)/shard_map/ppermute | solution.py:401
  471.5 49.3 %collective-permute-start.22 = (bf16[3072,256]{1,0:T(8,128)(2,1)}, bf16[3072,256]{1,0:T(8,128)(2,1)S(1)}, u32[]{:S(2)}, u32[]{:S(2)}) collective-permute-start(bf16[3072,256]{1,0:T(8,128)(2,1)} %add_convert_fusion.3), channel_id=1, source_target_pairs={{0,2},{1,3},{2,0},{3,1},{4,6},{5,7},{6,4},{7,5},{8,10},{9,11},{10,... | collective-permute-start | bytes 4718600 | tf_op jit(solution)/shard_map/ppermute | solution.py:401
  477.0 17.7 %collective-permute-start.29 = (bf16[1,128,768]{2,1,0:T(8,128)(2,1)}, bf16[1,128,768]{2,1,0:T(8,128)(2,1)}, u32[]{:S(2)}, u32[]{:S(2)}) collective-permute-start(bf16[1,128,768]{2,1,0:T(8,128)(2,1)} %add_convert_fusion.5), channel_id=1, source_target_pairs={{0,16},{4,20},{8,24},{12,28},{16,0},{20,4},{24,8},{28,12},{1,17},{... | collective-permute-start | bytes 589832 | tf_op jit(solution)/shard_map/ppermute | solution.py:401
  496.0 8.7 %collective-permute-start.30 = (bf16[1,128,768]{2,1,0:T(8,128)(2,1)S(1)}, bf16[1,128,768]{2,1,0:T(8,128)(2,1)S(1)}, u32[]{:S(2)}, u32[]{:S(2)}) collective-permute-start(bf16[1,128,768]{2,1,0:T(8,128)(2,1)S(1)} %get-tuple-element.49), channel_id=1, source_target_pairs={{0,16},{4,20},{8,24},{12,28},{16,0},{20,4},{24,8},{28,12},{1,17},{... | collective-permute-start | bytes 589832 | tf_op jit(solution)/shard_map/ppermute | solution.py:401
  497.2 8.2 %collective-permute-start.41 = (f32[4,1024]{1,0:T(4,128)S(1)}, f32[4,1024]{1,0:T(4,128)S(1)}, u32[]{:S(2)}, u32[]{:S(2)}) collective-permute-start(f32[4,1024]{1,0:T(4,128)S(1)} %pad_maximum_fusion.26), channel_id=1, source_target_pairs={{0,1},{1,0},{2,3},{3,2},{4,5},{5,4},{6,7},{7,6},{8,9},{9,8},{10,11... | collective-permute-start | bytes 49160 | tf_op jit(solution)/shard_map/ppermute | solution.py:401
  497.3 33.9 %collective-permute-start.25 = (bf16[3072,512]{1,0:T(8,128)(2,1)}, bf16[3072,512]{1,0:T(8,128)(2,1)S(1)}, u32[]{:S(2)}, u32[]{:S(2)}) collective-permute-start(bf16[3072,512]{1,0:T(8,128)(2,1)} %get-tuple-element.39), channel_id=1, source_target_pairs={{0,1},{1,0},{2,3},{3,2},{4,5},{5,4},{6,7},{7,6},{8,9},{9,8},{10,11... | collective-permute-start | bytes 9437192 | tf_op jit(solution)/shard_map/ppermute | solution.py:401
  504.8 14.1 %collective-permute-start.31 = (bf16[2,128,768]{2,1,0:T(8,128)(2,1)S(1)}, bf16[2,128,768]{2,1,0:T(8,128)(2,1)S(1)}, u32[]{:S(2)}, u32[]{:S(2)}) collective-permute-start(bf16[2,128,768]{2,1,0:T(8,128)(2,1)S(1)} %pad_maximum_fusion.19), channel_id=1, source_target_pairs={{0,8},{4,12},{8,0},{12,4},{16,24},{20,28},{24,16},{28,20},{1,9},{5... | collective-permute-start | bytes 1179656 | tf_op jit(solution)/shard_map/ppermute | solution.py:401
  513.0 5.1 collective-permute-start.44
  518.1 7.1 %collective-permute-start.45 = (f32[4,1024]{1,0:T(4,128)S(1)}, f32[4,1024]{1,0:T(4,128)S(1)}, u32[]{:S(2)}, u32[]{:S(2)}) collective-permute-start(f32[4,1024]{1,0:T(4,128)S(1)} %add.418), channel_id=1, source_target_pairs={{0,16},{4,20},{8,24},{12,28},{16,0},{20,4},{24,8},{28,12},{1,17},{... | collective-permute-start | bytes 49160 | tf_op jit(solution)/shard_map/ppermute | solution.py:401
  519.0 12.1 %collective-permute-start.32 = (bf16[4,128,768]{2,1,0:T(8,128)(2,1)S(1)}, bf16[4,128,768]{2,1,0:T(8,128)(2,1)S(1)}, u32[]{:S(2)}, u32[]{:S(2)}) collective-permute-start(bf16[4,128,768]{2,1,0:T(8,128)(2,1)S(1)} %pad_maximum_fusion.11), channel_id=1, source_target_pairs={{0,4},{4,0},{8,12},{12,8},{16,20},{20,16},{24,28},{28,24},{1,5},{5... | collective-permute-start | bytes 2359304 | tf_op jit(solution)/shard_map/ppermute | solution.py:401
  531.7 27.2 %collective-permute-start.26 = (bf16[3072,256]{1,0:T(8,128)(2,1)S(1)}, bf16[3072,256]{1,0:T(8,128)(2,1)S(1)}, u32[]{:S(2)}, u32[]{:S(2)}) collective-permute-start(bf16[3072,256]{1,0:T(8,128)(2,1)S(1)} %add_convert_fusion), channel_id=1, source_target_pairs={{0,2},{1,3},{2,0},{3,1},{4,6},{5,7},{6,4},{7,5},{8,10},{9,11},{10,... | collective-permute-start | bytes 4718600 | tf_op jit(solution)/shard_map/ppermute | solution.py:401
  (60 other events, 988.4 us)

commit v2 on v1

v2 whole, which is shorter than its diff:
```python
import functools

import jax
import jax.numpy as jnp
from jax import lax
from jax.experimental import pallas as pl
from jax.experimental.pallas import tpu as pltpu
from jax.sharding import PartitionSpec as P

HEADS = 8
HEAD_DIM = 128
SHORT = 512
eps = 1e-05
masked_value = -1e30
LOG2E = 1.4426950408889634
LN2 = 0.6931471805599453
SCALE = HEAD_DIM ** (-0.5)
MIB = 1024 * 1024
f32 = jnp.float32
bf16 = jnp.bfloat16

NN = (((1,), (0,)), ((), ()))
NT = (((1,), (1,)), ((), ()))
TN = (((0,), (0,)), ((), ()))


def dot(left, right, dims=NN):
    return lax.dot_general(left, right, dims, preferred_element_type=f32)


def full_spec(shape):
    return pl.BlockSpec(shape, lambda *_: (0,) * len(shape))


MESH = pl.DeviceIdType.MESH


def partner(index, mask):
    return index + mask - 2 * mask * ((index // mask) % 2)


def masks_of(size):
    return [1 << k for k in range(size.bit_length() - 1)]


def send_to(src, dst, send, recv, **where):
    return pltpu.make_async_remote_copy(
        src_ref=src, dst_ref=dst, send_sem=send, recv_sem=recv, device_id=where, device_id_type=MESH
    )


def greet(dp_masks):
    me, group = lax.axis_index("head"), lax.axis_index("dp")
    barrier = pltpu.get_barrier_semaphore()
    for mask in (1, 2):
        pl.semaphore_signal(
            barrier, inc=1, device_id={"head": partner(me, mask)}, device_id_type=MESH
        )
    for mask in dp_masks:
        pl.semaphore_signal(
            barrier, inc=1, device_id={"dp": partner(group, mask)}, device_id_type=MESH
        )
    pl.semaphore_wait(barrier, 2 + len(dp_masks))


def at_rows(r, block=SHORT):
    return pl.ds(pl.multiple_of(r * block, block), block)


def at_cols(k, width):
    return pl.ds(pl.multiple_of(k * width, width), width)


class HeadGather:
    def __init__(self, own, full, width, sems):
        self.own, self.full, self.width = own, full, width
        self.me = lax.axis_index("head")
        self.core, self.chip = partner(self.me, 1), partner(self.me, 2)
        self.far = partner(self.core, 2)
        self.sems = sems

    def slot(self, r, who):
        return self.full.at[at_rows(r), at_cols(who, self.width)]

    def copy(self, r, src, owner, kind, **where):
        return send_to(
            src, self.slot(r, owner), self.sems.at[2 * kind, r], self.sems.at[2 * kind + 1, r], **where
        )

    def own_src(self, r):
        return self.own(r) if self.own is not None else self.slot(r, self.me)

    def start(self, r):
        self.copy(r, self.own_src(r), self.me, 0, head=self.chip).start()
        self.copy(r, self.own_src(r), self.me, 1, head=self.core).start()

    def forward(self, r):
        self.copy(r, self.slot(r, self.chip), self.chip, 0, head=self.chip).wait_recv()
        self.copy(r, self.slot(r, self.chip), self.chip, 2, head=self.core).start()

    def arrive(self, r):
        self.copy(r, self.slot(r, self.core), self.core, 1, head=self.core).wait_recv()
        self.copy(r, self.slot(r, self.far), self.far, 2, head=self.core).wait_recv()

    def sent(self, r):
        self.copy(r, self.own_src(r), self.me, 0, head=self.chip).wait_send()
        self.copy(r, self.own_src(r), self.me, 1, head=self.core).wait_send()
        self.copy(r, self.slot(r, self.chip), self.chip, 2, head=self.core).wait_send()


class DpGather:
    def __init__(self, own, full, width, masks, send, recv):
        self.own, self.full, self.width = own, full, width
        self.masks = list(reversed(masks))
        self.group = lax.axis_index("dp")
        self.send, self.recv = send, recv
        held, self.plan, at = [0], [], 0
        for mask in self.masks:
            self.plan.append((mask, [(k, at + p) for p, k in enumerate(held)]))
            at += len(held)
            held = held + [k ^ mask for k in held]

    def block(self, k):
        who = self.group
        for mask in masks_of(1 << len(self.masks)):
            if k & mask:
                who = partner(who, mask)
        return self.full.at[:, at_cols(who, self.width)]

    def copies(self, step, there):
        mask, items = self.plan[step]
        out = []
        for k, sem in items:
            if there:
                src, at = (self.own if k == 0 else self.block(k)), self.block(k)
            else:
                src = at = self.block(k ^ mask)
            out.append(
                send_to(src, at, self.send.at[sem], self.recv.at[sem], dp=partner(self.group, mask))
            )
        return out

    def start(self, step):
        for copy in self.copies(step, True):
            copy.start()

    def arrive(self, step):
        for copy in self.copies(step, False):
            copy.wait_recv()

    def sent(self):
        for step in range(len(self.plan)):
            for copy in self.copies(step, True):
                copy.wait_send()


def head_slopes(me, heads, n_head=4):
    slopes = []
    for h in range(heads):
        value = jnp.float32(0.0)
        for k in range(n_head):
            value = jnp.where(me == k, jnp.float32(2.0 ** (-8.0 * (k * heads + h + 1) / HEADS)), value)
        slopes.append(value)
    return slopes


def first_kernel(
    masks, gather,
    kind, layer_in, wq, wk, wv, gain, shift, bias_expand, w_proj, w_expand, w_reduce,
    x_out, a_out, normed_out, qkv_out, proj_out, expand_out, reduce_out, bias_out, logsum,
    x_buf, normed_buf, qkv_buf, a_buf, bias_buf, total, x_sems, a_sems, p_sems, local_sems, copy_sems,
    e_send, e_recv, r_send, r_recv, b_send, b_recv,
):
    rows, width = layer_in.shape
    features = 4 * width
    block = SHORT
    n = rows // block
    heads = width // HEAD_DIM
    me, group = lax.axis_index("head"), lax.axis_index("dp")
    core, chip = partner(me, 1), partner(me, 2)
    greet(masks if gather else [])

    x_gather = HeadGather(None, x_buf, width, x_sems)
    a_gather = HeadGather(lambda r: a_buf.at[at_rows(r), :], a_out, width, a_sems)

    def p_copy(src, owner, k, **where):
        return send_to(src, proj_out.at[at_cols(owner, width), :], p_sems.at[2 * k], p_sems.at[2 * k + 1], **where)

    if gather:
        expand = DpGather(w_expand, expand_out, w_expand.shape[1], masks, e_send, e_recv)
        reduce = DpGather(w_reduce, reduce_out, w_reduce.shape[1], masks, r_send, r_recv)
        bias_buf[...] = jnp.broadcast_to(bias_expand[...], bias_buf.shape)
        bias = DpGather(bias_buf, bias_out, w_expand.shape[1], masks, b_send, b_recv)
        expand.start(0)
        bias.start(0)
        reduce.start(0)

    def own_chunk(r):
        x_buf[at_rows(r), at_cols(me, width)] = layer_in[at_rows(r), :].astype(bf16)
        x_gather.start(r)

    own_chunk(0)
    own_chunk(1)
    keeps = [pltpu.make_async_copy(w_proj, proj_out.at[at_cols(me, width), :], local_sems.at[0])]
    if gather:
        own_cols = at_cols(group, w_expand.shape[1])
        keeps.append(pltpu.make_async_copy(w_expand, expand_out.at[:, own_cols], local_sems.at[1]))
        keeps.append(pltpu.make_async_copy(w_reduce, reduce_out.at[:, own_cols], local_sems.at[2]))
        keeps.append(pltpu.make_async_copy(bias_buf, bias_out.at[:, own_cols], local_sems.at[3]))
    for keep in keeps:
        keep.start()

    slopes = [s * LOG2E for s in head_slopes(me, heads)]
    apart = (1 - kind[0]).astype(f32) * masked_value
    key_place = lax.broadcasted_iota(jnp.int32, (block, block), 0)
    query_place = lax.broadcasted_iota(jnp.int32, (block, block), 1)

    def normed_copy(r):
        return pltpu.make_async_copy(normed_buf.at[r % 2], normed_out.at[at_rows(r), :], copy_sems.at[0, r])

    def x_copy(r):
        return pltpu.make_async_copy(x_buf.at[at_rows(r), :], x_out.at[at_rows(r), :], copy_sems.at[1, r])

    def qkv_copy(r):
        return pltpu.make_async_copy(qkv_buf.at[at_rows(r), :], qkv_out.at[at_rows(r), :], copy_sems.at[2, r])

    def a_copy(r):
        return pltpu.make_async_copy(
            a_buf.at[at_rows(r), :], a_out.at[at_rows(r), at_cols(me, width)], copy_sems.at[3, r]
        )

    def chunk(i):
        x_gather.arrive(i)
        x_copy(i).start()
        x = x_buf[at_rows(i), :].astype(f32)
        centre = x - jnp.sum(x, axis=1, keepdims=True) * (1.0 / features)
        spread = jnp.sum(centre * centre, axis=1, keepdims=True) * (1.0 / features)
        low = (centre * lax.rsqrt(spread + eps) * gain[...] + shift[...]).astype(bf16)

        @pl.when(i >= 2)
        def _():
            normed_copy(i - 2).wait()

        normed_buf[i % 2] = low
        normed_copy(i).start()
        for k, w in enumerate((wq, wk, wv)):
            qkv_buf[at_rows(i), k * width : (k + 1) * width] = dot(low, w[...]).astype(bf16)
        qkv_copy(i).start()

        def scores(h, j):
            q = qkv_buf[at_rows(i), h * HEAD_DIM : (h + 1) * HEAD_DIM]
            k = qkv_buf[at_rows(j), width + h * HEAD_DIM : width + (h + 1) * HEAD_DIM]
            v = qkv_buf[at_rows(j), 2 * width + h * HEAD_DIM : 2 * width + (h + 1) * HEAD_DIM]
            place = (key_place + (j - i) * block).astype(f32) * slopes[h]
            return dot(k, q, NT) * (SCALE * LOG2E) + place, v

        carry = []
        for h in range(heads):
            s, v = scores(h, i)
            s = jnp.where(key_place <= query_place, s, masked_value)
            m = jnp.max(s, axis=0, keepdims=True)
            p = jnp.exp2(s - m)
            carry += [m, jnp.sum(p, axis=0, keepdims=True)]
            total[h] = dot(v, p.astype(bf16), TN)

        def step(j, carry):
            new = []
            for h in range(heads):
                m, l = carry[2 * h], carry[2 * h + 1]
                s, v = scores(h, j)
                s = s + apart
                m_new = jnp.maximum(m, jnp.max(s, axis=0, keepdims=True))
                p = jnp.exp2(s - m_new)
                fade = jnp.exp2(m - m_new)
                new += [m_new, l * fade + jnp.sum(p, axis=0, keepdims=True)]
                total[h] = total[h] * fade + dot(v, p.astype(bf16), TN)
            return tuple(new)

        carry = lax.fori_loop(0, i, step, tuple(carry))
        for h in range(heads):
            m, l = carry[2 * h], carry[2 * h + 1]
            a_buf[at_rows(i), h * HEAD_DIM : (h + 1) * HEAD_DIM] = (total[h] * (1.0 / l)).T.astype(bf16)
            logsum[i, h : h + 1, :] = m + jnp.log(l) * LOG2E
        a_gather.start(i)
        a_copy(i).start()

    steps = len(masks)

    def body(r, _):
        @pl.when(r < n)
        def _():
            x_gather.forward(r)

            @pl.when(r + 2 < n)
            def _():
                own_chunk(r + 2)

            @pl.when(r + 2 == n)
            def _():
                p_copy(w_proj, me, 0, head=chip).start()
                p_copy(w_proj, me, 1, head=core).start()

        if gather:
            for s in range(1, steps):
                @pl.when(r == min(2 * s, n - 1))
                def _(s=s):
                    expand.arrive(s - 1)
                    bias.arrive(s - 1)
                    expand.start(s)
                    bias.start(s)

                @pl.when(r == min(2 * s + 1, n))
                def _(s=s):
                    reduce.arrive(s - 1)
                    reduce.start(s)

        @pl.when(r >= 1)
        def _():
            chunk(r - 1)

        return 0

    lax.fori_loop(0, n + 1, body, 0)

    p_copy(w_proj, chip, 0, head=chip).wait_recv()
    p_forward = p_copy(proj_out.at[at_cols(chip, width), :], chip, 2, head=core)
    p_forward.start()

    def pass_on(r, _):
        a_gather.forward(r)
        return 0

    lax.fori_loop(0, n, pass_on, 0)

    def settle(r, _):
        a_gather.arrive(r)
        a_gather.sent(r)
        x_gather.sent(r)
        x_copy(r).wait()
        qkv_copy(r).wait()
        a_copy(r).wait()

        @pl.when(r >= n - 2)
        def _():
            normed_copy(r).wait()

        return 0

    lax.fori_loop(0, n, settle, 0)
    p_copy(w_proj, core, 1, head=core).wait_recv()
    p_copy(w_proj, partner(core, 2), 2, head=core).wait_recv()
    p_copy(w_proj, me, 0, head=chip).wait_send()
    p_copy(w_proj, me, 1, head=core).wait_send()
    p_forward.wait_send()
    for keep in keeps:
        keep.wait()
    if gather:
        expand.arrive(steps - 1)
        reduce.arrive(steps - 1)
        bias.arrive(steps - 1)
        expand.sent()
        reduce.sent()
        bias.sent()


def first(kind, layer_in, wq, wk, wv, gain, shift, bias_expand, w_proj, w_expand, w_reduce, dp_size):
    rows, width = layer_in.shape
    features = 4 * width
    block = SHORT
    n = rows // block
    heads = width // HEAD_DIM
    masks = masks_of(dp_size)
    local = w_expand.shape[1]
    gather = local % 128 == 0
    units = local * dp_size if gather else 128
    any_spec = pl.BlockSpec(memory_space=pl.ANY)
    vmem = pl.BlockSpec(memory_space=pltpu.VMEM)
    blocks = max(dp_size - 1, 1)
    outs = pl.pallas_call(
        functools.partial(first_kernel, masks, gather),
        in_specs=[pl.BlockSpec(memory_space=pltpu.SMEM)] + [vmem] * 7 + [any_spec] * 3,
        out_specs=[any_spec] * 8 + [vmem],
        out_shape=[
            jax.ShapeDtypeStruct((rows, features), bf16),
            jax.ShapeDtypeStruct((rows, features), bf16),
            jax.ShapeDtypeStruct((rows, features), bf16),
            jax.ShapeDtypeStruct((rows, 3 * width), bf16),
            jax.ShapeDtypeStruct((features, features), bf16),
            jax.ShapeDtypeStruct((features, units), bf16),
            jax.ShapeDtypeStruct((features, units), bf16),
            jax.ShapeDtypeStruct((16, units), bf16),
            jax.ShapeDtypeStruct((n, heads, block), f32),
        ],
        scratch_shapes=[
            pltpu.VMEM((rows, features), bf16),
            pltpu.VMEM((2, block, features), bf16),
            pltpu.VMEM((rows, 3 * width), bf16),
            pltpu.VMEM((rows, width), bf16),
            pltpu.VMEM((16, local), bf16),
            pltpu.VMEM((heads, HEAD_DIM, block), f32),
            pltpu.SemaphoreType.DMA((6, n)),
            pltpu.SemaphoreType.DMA((6, n)),
            pltpu.SemaphoreType.DMA((6,)),
            pltpu.SemaphoreType.DMA((4,)),
            pltpu.SemaphoreType.DMA((4, n)),
            pltpu.SemaphoreType.DMA((blocks,)),
            pltpu.SemaphoreType.DMA((blocks,)),
            pltpu.SemaphoreType.DMA((blocks,)),
            pltpu.SemaphoreType.DMA((blocks,)),
            pltpu.SemaphoreType.DMA((blocks,)),
            pltpu.SemaphoreType.DMA((blocks,)),
        ],
        compiler_params=pltpu.CompilerParams(
            vmem_limit_bytes=56 * MIB, collective_id=0, has_side_effects=True
        ),
    )(kind, layer_in, wq, wk, wv, gain, shift, bias_expand, w_proj, w_expand, w_reduce)
    x, a, normed, qkv, proj, expand, reduce, bias, logsum = outs
    bias = bias[:1]
    if not gather:
        bias = lax.all_gather(bias_expand, "dp", axis=1, tiled=True)
        expand = lax.all_gather(w_expand, "dp", axis=1, tiled=True)
        reduce = lax.all_gather(w_reduce, "dp", axis=1, tiled=True)
    return x, a, normed, qkv, proj, expand, reduce, bias.astype(f32), logsum


class HeadScatter:
    def __init__(self, width, src, from_core, far, near, from_chip, sems):
        self.width, self.src, self.from_core, self.far = width, src, from_core, far
        self.near, self.from_chip, self.sems = near, from_chip, sems
        self.me = lax.axis_index("head")
        self.core, self.chip = partner(self.me, 1), partner(self.me, 2)

    def to_core(self, r, k):
        who = self.core if k == 0 else partner(self.core, 2)
        return send_to(
            self.src(r).at[:, at_cols(who, self.width)],
            self.from_core.at[at_rows(r), k * self.width : (k + 1) * self.width],
            self.sems.at[2 * k, r],
            self.sems.at[2 * k + 1, r],
            head=self.core,
        )

    def to_chip(self, r):
        return send_to(
            self.far.at[r % 2],
            self.from_chip.at[at_rows(r), :],
            self.sems.at[4, r],
            self.sems.at[5, r],
            head=self.chip,
        )

    def start(self, r):
        self.to_core(r, 1).start()
        self.to_core(r, 0).start()

    def middle(self, r):
        src = self.src(r)
        self.to_core(r, 1).wait()
        self.far[r % 2] = (
            src[:, at_cols(self.chip, self.width)].astype(f32)
            + self.from_core[at_rows(r), self.width :].astype(f32)
        ).astype(bf16)
        self.to_chip(r).start()
        self.to_core(r, 0).wait()
        self.near[r % 2] = (
            src[:, at_cols(self.me, self.width)].astype(f32)
            + self.from_core[at_rows(r), : self.width].astype(f32)
        )

    def finish(self, r):
        self.to_chip(r).wait()
        return self.near[r % 2] + self.from_chip[at_rows(r), :].astype(f32)


GELU_C = 0.7978845608028654


def second_kernel(
    x_in, a_in, grad_out, layer_in, w_proj, w_expand, w_reduce, gain, shift, bias,
    grad_heads, grad_hid_out, ffn_out, hid_own, wide_out, narrow_out, proj_out, sums, grad_bias, grad_bias_reduce,
    g_buf, x_buf, a_buf, hid_buf, own_buf, ffn_buf, gh_buf, from_core, far_buf, near_buf, from_chip, wide, narrow, proj,
    g_sems, s_sems, copy_sems, final_sems,
):
    rows, width = layer_in.shape
    features = 4 * width
    block = SHORT
    n = rows // block
    me = lax.axis_index("head")
    greet([])

    g_gather = HeadGather(None, g_buf, width, g_sems)
    scatter = HeadScatter(width, lambda r: gh_buf.at[r % 2], from_core, far_buf, near_buf, from_chip, s_sems)

    def own_chunk(r):
        chunk = grad_out[at_rows(r), :]
        g_buf[at_rows(r), at_cols(me, width)] = chunk.astype(bf16)
        g_gather.start(r)
        return chunk

    def load_x(r):
        return pltpu.make_async_copy(x_in.at[at_rows(r), :], x_buf.at[r % 2], copy_sems.at[0, r])

    def load_a(r):
        return pltpu.make_async_copy(a_in.at[at_rows(r), :], a_buf.at[r % 2], copy_sems.at[1, r])

    def store_hid(r):
        return pltpu.make_async_copy(hid_buf.at[r % 2], grad_hid_out.at[at_rows(r), :], copy_sems.at[2, r])

    def store_ffn(r):
        return pltpu.make_async_copy(ffn_buf.at[r % 2], ffn_out.at[at_rows(r), :], copy_sems.at[3, r])

    def store_own(r):
        return pltpu.make_async_copy(own_buf.at[r % 2], hid_own.at[at_rows(r), :], copy_sems.at[4, r])

    def final(k, slot, buf, out):
        half = features // 2
        return pltpu.make_async_copy(
            buf.at[slot], out.at[slot * half : (slot + 1) * half, :], final_sems.at[k, slot]
        )

    own_chunk(0)
    own_chunk(1)
    load_x(0).start()
    load_a(0).start()
    wide[...] = jnp.zeros_like(wide)
    narrow[...] = jnp.zeros_like(narrow)
    proj[...] = jnp.zeros_like(proj)
    sums[...] = jnp.zeros_like(sums)
    grad_bias[...] = jnp.zeros_like(grad_bias)
    grad_bias_reduce[...] = jnp.sum(grad_out[...], axis=0, keepdims=True)

    def body(r, _):
        g_gather.forward(r)

        @pl.when(r + 2 < n)
        def _():
            own_chunk(r + 2)

        load_x(r).wait()
        load_a(r).wait()

        @pl.when(r + 1 < n)
        def _():
            load_x(r + 1).start()
            load_a(r + 1).start()

        @pl.when(r >= 2)
        def _():
            store_hid(r - 2).wait()
            store_ffn(r - 2).wait()
            store_own(r - 2).wait()

        slot = r % 2
        a = a_buf[slot]
        attn = dot(a, w_proj[...])
        hidden = attn + x_buf[slot].astype(f32)
        own_buf[slot] = dot(a, w_proj[:, at_cols(me, width)]) + layer_in[at_rows(r), :]
        store_own(r).start()
        centre = hidden - jnp.sum(hidden, axis=1, keepdims=True) * (1.0 / features)
        spread = jnp.sum(centre * centre, axis=1, keepdims=True) * (1.0 / features)
        scale = lax.rsqrt(spread + eps)
        centred = centre * scale
        low = (centred * gain[...] + shift[...]).astype(bf16)
        z = dot(low, w_expand[...]) + bias[...]
        z2 = z * z
        t = jnp.tanh(z * (GELU_C + (GELU_C * 0.044715) * z2))
        half = 0.5 + 0.5 * t
        activated = (z * half).astype(bf16)
        slope = half + (0.5 * z) * (1.0 - t * t) * (GELU_C + (3.0 * GELU_C * 0.044715) * z2)
        g_gather.arrive(r)
        g = g_buf[at_rows(r), :]
        gp = slope * dot(g, w_reduce[...])
        gp_low = gp.astype(bf16)
        gn = dot(gp_low, w_expand[...], NT)
        scaled = gn * gain[...]
        mean_scaled = jnp.sum(scaled, axis=1, keepdims=True) * (1.0 / features)
        mean_both = jnp.sum(scaled * centred, axis=1, keepdims=True) * (1.0 / features)
        back = (scaled - mean_scaled - centred * mean_both) * scale
        back_low = (back + 0.25 * g.astype(f32)).astype(bf16)
        hid_buf[slot] = back_low
        store_hid(r).start()
        gh_buf[slot] = dot(back_low, w_proj[...], NT).astype(bf16)
        scatter.start(r)
        sums[0:1, :] += jnp.sum(gn * centred, axis=0, keepdims=True)
        sums[1:2, :] += jnp.sum(gn, axis=0, keepdims=True)
        grad_bias[...] += jnp.sum(gp_low.astype(f32), axis=0, keepdims=True)
        ffn_buf[slot] = dot(activated, w_reduce[...], NT).astype(bf16)
        store_ffn(r).start()
        wide[...] += dot(low, gp_low, TN)
        narrow[...] += dot(g, activated, TN)
        scatter.middle(r)
        proj[...] += dot(a, back_low, TN)

        @pl.when(r >= 1)
        def _():
            grad_heads[at_rows(r - 1), :] = scatter.finish(r - 1).astype(bf16)

        return 0

    lax.fori_loop(0, n, body, 0)
    for k, (full, buf, out) in enumerate(
        ((wide, ffn_buf, wide_out), (narrow, x_buf, narrow_out), (proj, hid_buf, proj_out))
    ):
        for p in range(2):
            if buf is ffn_buf:
                store_ffn(n - 2 + p).wait()
            if buf is hid_buf:
                store_hid(n - 2 + p).wait()
            half = features // 2
            slot = (n - 2 + p) % 2
            buf[slot] = full[slot * half : (slot + 1) * half, :].astype(bf16)
            final(k, slot, buf, out).start()
    grad_heads[at_rows(n - 1), :] = scatter.finish(n - 1).astype(bf16)
    for k, (buf, out) in enumerate(((ffn_buf, wide_out), (x_buf, narrow_out), (hid_buf, proj_out))):
        for slot in range(2):
            final(k, slot, buf, out).wait()

    def settle(r, _):
        g_gather.sent(r)

        @pl.when(r >= n - 2)
        def _():
            store_own(r).wait()

        return 0

    lax.fori_loop(0, n, settle, 0)


def second(x, a, grad_out, layer_in, w_proj, w_expand, w_reduce, gain, shift, bias):
    rows, width = layer_in.shape
    features = 4 * width
    units = w_expand.shape[1]
    block = SHORT
    n = rows // block
    any_spec = pl.BlockSpec(memory_space=pl.ANY)
    vmem = pl.BlockSpec(memory_space=pltpu.VMEM)
    return pl.pallas_call(
        second_kernel,
        in_specs=[any_spec] * 2 + [vmem] * 8,
        out_specs=[vmem] + [any_spec] * 6 + [vmem] * 3,
        out_shape=[
            jax.ShapeDtypeStruct((rows, width), bf16),
            jax.ShapeDtypeStruct((rows, features), bf16),
            jax.ShapeDtypeStruct((rows, features), bf16),
            jax.ShapeDtypeStruct((rows, width), f32),
            jax.ShapeDtypeStruct((features, units), bf16),
            jax.ShapeDtypeStruct((features, units), bf16),
            jax.ShapeDtypeStruct((features, features), bf16),
            jax.ShapeDtypeStruct((2, features), f32),
            jax.ShapeDtypeStruct((1, units), f32),
            jax.ShapeDtypeStruct((1, width), f32),
        ],
        scratch_shapes=[
            pltpu.VMEM((rows, features), bf16),
            pltpu.VMEM((2, block, features), bf16),
            pltpu.VMEM((2, block, features), bf16),
            pltpu.VMEM((2, block, features), bf16),
            pltpu.VMEM((2, block, width), f32),
            pltpu.VMEM((2, block, features), bf16),
            pltpu.VMEM((2, block, features), bf16),
            pltpu.VMEM((rows, 2 * width), bf16),
            pltpu.VMEM((2, block, width), bf16),
            pltpu.VMEM((2, block, width), f32),
            pltpu.VMEM((rows, width), bf16),
            pltpu.VMEM((features, units), f32),
            pltpu.VMEM((features, units), f32),
            pltpu.VMEM((features, features), f32),
            pltpu.SemaphoreType.DMA((6, n)),
            pltpu.SemaphoreType.DMA((6, n)),
            pltpu.SemaphoreType.DMA((5, n)),
            pltpu.SemaphoreType.DMA((3, 2)),
        ],
        compiler_params=pltpu.CompilerParams(
            vmem_limit_bytes=62 * MIB, collective_id=1, has_side_effects=True
        ),
    )(x, a, grad_out, layer_in, w_proj, w_expand, w_reduce, gain, shift, bias)


def attend_back_kernel(heads, kind, slopes, qkv, grad, attended, logsum, grad_qkv, total_q, delta):
    block = SHORT
    j = pl.program_id(0)
    n = pl.num_programs(0)
    high = jnp.where(kind[0] == 1, n, j + 1)
    at = pl.multiple_of(j * block, block)
    key_place = lax.broadcasted_iota(jnp.int32, (block, block), 0)
    query_place = lax.broadcasted_iota(jnp.int32, (block, block), 1)
    width = heads * HEAD_DIM

    @pl.when(j == 0)
    def _():
        total_q[...] = jnp.zeros_like(total_q)

        def fill(i, _):
            here = pl.ds(pl.multiple_of(i * block, block), block)
            for h in range(heads):
                cols = slice(h * HEAD_DIM, (h + 1) * HEAD_DIM)
                both = grad[here, cols].astype(f32) * attended[here, cols].astype(f32)
                delta[i, h : h + 1, :] = jnp.sum(both.T, axis=0, keepdims=True)
            return 0

        lax.fori_loop(0, n, fill, 0)

    def pair(h, i, masked):
        start = pl.multiple_of(i * block, block)
        cols = slice(h * HEAD_DIM, (h + 1) * HEAD_DIM)
        q = qkv[pl.ds(start, block), h * HEAD_DIM : (h + 1) * HEAD_DIM]
        k = qkv[pl.ds(at, block), width + h * HEAD_DIM : width + (h + 1) * HEAD_DIM]
        v = qkv[pl.ds(at, block), 2 * width + h * HEAD_DIM : 2 * width + (h + 1) * HEAD_DIM]
        g = grad[pl.ds(start, block), cols]
        place = (key_place + (j - i) * block).astype(f32) * (slopes[h] * LOG2E)
        s = dot(k, q, NT) * (SCALE * LOG2E) + place
        if masked:
            s = jnp.where(key_place <= query_place, s, masked_value)
        p = jnp.exp2(s - logsum[i, h : h + 1, :])
        ds = (p * (dot(v, g, NT) - delta[i, h : h + 1, :])).astype(bf16)
        dv = dot(p.astype(bf16), g)
        dk = dot(ds, q)
        total_q[pl.ds(start, block), cols] += dot(ds, k, TN)
        return dk, dv

    first = [pair(h, j, True) for h in range(heads)]
    carry = tuple(x for both in first for x in both)

    def step(i, carry):
        new = []
        for h in range(heads):
            dk, dv = pair(h, i, False)
            new += [carry[2 * h] + dk, carry[2 * h + 1] + dv]
        return tuple(new)

    carry = lax.fori_loop(j + 1, high, step, carry)
    for h in range(heads):
        cols = slice(h * HEAD_DIM, (h + 1) * HEAD_DIM)
        grad_qkv[:, cols] = (total_q[pl.ds(at, block), cols] * SCALE).astype(bf16)
        grad_qkv[:, width + h * HEAD_DIM : width + (h + 1) * HEAD_DIM] = (
            carry[2 * h] * SCALE
        ).astype(bf16)
        grad_qkv[:, 2 * width + h * HEAD_DIM : 2 * width + (h + 1) * HEAD_DIM] = carry[
            2 * h + 1
        ].astype(bf16)


def attend_back(qkv, grad, attended, logsum, slopes, kind):
    rows = qkv.shape[0]
    width = qkv.shape[1] // 3
    heads = width // HEAD_DIM
    block = SHORT
    n = rows // block
    return pl.pallas_call(
        functools.partial(attend_back_kernel, heads),
        grid=(n,),
        in_specs=[
            pl.BlockSpec(memory_space=pltpu.SMEM),
            pl.BlockSpec(memory_space=pltpu.SMEM),
            full_spec(qkv.shape),
            full_spec(grad.shape),
            full_spec(attended.shape),
            full_spec(logsum.shape),
        ],
        out_specs=pl.BlockSpec((block, 3 * width), lambda j: (j, 0)),
        out_shape=jax.ShapeDtypeStruct((rows, 3 * width), bf16),
        scratch_shapes=[pltpu.VMEM((rows, width), f32), pltpu.VMEM((n, heads, block), f32)],
        compiler_params=pltpu.CompilerParams(vmem_limit_bytes=56 * MIB),
        cost_estimate=pl.CostEstimate(
            flops=20 * rows * rows * width, bytes_accessed=rows * width * 20, transcendentals=0
        ),
    )(kind, slopes, qkv, grad, attended, logsum)


def finish_kernel(x_in, grad_qkv, weight, gain, grad_hid, last, sums):
    step = pl.program_id(0)
    features = x_in.shape[1]
    gf = dot(grad_qkv[...], weight[...], NT)
    x = x_in[...].astype(f32)
    centre = x - jnp.sum(x, axis=1, keepdims=True) * (1.0 / features)
    spread = jnp.sum(centre * centre, axis=1, keepdims=True) * (1.0 / features)
    scale = lax.rsqrt(spread + eps)
    centred = centre * scale
    scaled = gf * gain[...]
    mean_scaled = jnp.sum(scaled, axis=1, keepdims=True) * (1.0 / features)
    mean_both = jnp.sum(scaled * centred, axis=1, keepdims=True) * (1.0 / features)
    back = (scaled - mean_scaled - centred * mean_both) * scale
    last[...] = (back + grad_hid[...].astype(f32)).astype(bf16)

    @pl.when(step == 0)
    def _():
        sums[...] = jnp.zeros_like(sums)

    sums[0:1, :] += jnp.sum(gf * centred, axis=0, keepdims=True)
    sums[1:2, :] += jnp.sum(gf, axis=0, keepdims=True)


def finish(x, grad_qkv, weight, gain, grad_hid):
    rows, features = x.shape
    block = SHORT

    def rows_of(columns):
        return pl.BlockSpec((block, columns), lambda i: (i, 0))

    return pl.pallas_call(
        finish_kernel,
        grid=(rows // block,),
        in_specs=[rows_of(features), rows_of(grad_qkv.shape[1]), full_spec(weight.shape), full_spec(gain.shape), rows_of(features)],
        out_specs=[rows_of(features), full_spec((2, features))],
        out_shape=[jax.ShapeDtypeStruct((rows, features), bf16), jax.ShapeDtypeStruct((2, features), f32)],
        compiler_params=pltpu.CompilerParams(vmem_limit_bytes=48 * MIB),
        cost_estimate=pl.CostEstimate(
            flops=2 * rows * features * grad_qkv.shape[1], bytes_accessed=rows * features * 8, transcendentals=0
        ),
    )(x, grad_qkv, weight, gain, grad_hid)


def flip(value, axis, size, mask):
    return lax.ppermute(value, axis, [(k, k ^ mask) for k in range(size)])


def reorder(value, rank, axis=0, size=4):
    width = value.shape[axis] // size
    return jnp.concatenate(
        [lax.dynamic_slice_in_dim(value, (rank ^ k) * width, width, axis) for k in range(size)], axis
    )


def scatter_dp(blocks, size):
    held = {k: blocks[k].astype(f32) for k in range(size)}
    for mask in masks_of(size):
        mine = [k for k in sorted(held) if not k & mask]
        got = flip(jnp.stack([held[k ^ mask] for k in mine]).astype(bf16), "dp", size, mask)
        held = {k: held[k] + got[p].astype(f32) for p, k in enumerate(mine)}
    return held[0]


def gather_dp(value, size):
    blocks = {0: value}
    for mask in reversed(masks_of(size)):
        order = sorted(blocks)
        got = flip(jnp.stack([blocks[k] for k in order]), "dp", size, mask)
        for k, at in enumerate(order):
            blocks[at ^ mask] = got[k]
    return [blocks[k] for k in range(size)]


def scatter_head(value, rank):
    width = value.shape[1] // 4

    def cols(k):
        return lax.dynamic_slice_in_dim(value, (rank ^ k) * width, width, 1)

    got = flip(jnp.concatenate([cols(1), cols(3)], 1), "head", 4, 1).astype(f32)
    far = cols(2).astype(f32) + got[:, width:]
    near = cols(0).astype(f32) + got[:, :width]
    return near + flip(far.astype(bf16), "head", 4, 2).astype(f32)


def sum_dp(value, dp_size):
    for mask in masks_of(dp_size):
        value = value + flip(value, "dp", dp_size, mask)
    return value


def sum_small(value, dp_size):
    for mask in (1, 2):
        value = value + flip(value, "head", 4, mask)
    return sum_dp(value, dp_size)


def all_sum_dp(value, dp_size):
    me = lax.axis_index("dp")
    parts = reorder(value, me, 0, dp_size)
    r = value.shape[0] // dp_size
    own = scatter_dp([parts[k * r : (k + 1) * r] for k in range(dp_size)], dp_size)
    return reorder(jnp.concatenate(gather_dp(own.astype(bf16), dp_size), 0), me, 0, dp_size).astype(f32)


def shards(
    dp_size,
    layer_in,
    bucket,
    w_query,
    w_key,
    w_value,
    w_proj,
    attn_gain,
    attn_shift,
    ffn_gain,
    ffn_shift,
    w_expand,
    bias_expand,
    w_reduce,
    bias_reduce,
    grad_out,
):
    rank = lax.axis_index("head")
    group = lax.axis_index("dp")
    rows, width = layer_in.shape
    features = 4 * width
    heads_here = w_query.shape[1] // HEAD_DIM
    head_index = rank * heads_here + jnp.arange(heads_here)
    slopes = jnp.exp2(-8.0 * (head_index.astype(f32) + 1.0) / HEADS)
    gain_1, shift_1 = attn_gain[None], attn_shift[None]
    x, a, normed_attn, qkv, proj, expand, reduce, bias, logsum = first(
        bucket, layer_in, w_query, w_key, w_value, gain_1, shift_1, bias_expand, w_proj, w_expand, w_reduce, dp_size
    )
    (
        grad_heads, grad_hid, ffn_partial, hid_own, grad_wide, grad_narrow, proj_part, sums_2, grad_bias, grad_bias_reduce,
    ) = second(
        x, a, grad_out, layer_in, proj, expand, reduce, ffn_gain[None], ffn_shift[None], bias
    )
    layer_out = hid_own + bias_reduce + scatter_head(ffn_partial, rank)
    local = w_expand.shape[1]

    def columns_home(value):
        value = reorder(value, group, 1, dp_size)
        return scatter_dp([value[:, k * local : (k + 1) * local] for k in range(dp_size)], dp_size)

    grad_expand = columns_home(grad_wide)
    grad_reduce = columns_home(grad_narrow)
    grad_bias_expand = columns_home(grad_bias)
    grad_proj = all_sum_dp(scatter_head(proj_part.T, rank).T, dp_size)

    attended = lax.dynamic_slice_in_dim(a, rank * width, width, 1)
    grad_qkv = attend_back(qkv, grad_heads, attended, logsum, slopes, bucket)
    weight_grad = all_sum_dp(dot(normed_attn, grad_qkv, TN), dp_size)
    grad_query, grad_key, grad_value = (weight_grad[:, k * width : (k + 1) * width] for k in range(3))
    w_qkv = jnp.concatenate([w_query, w_key, w_value], 1)
    last, sums_1 = finish(x, grad_qkv, w_qkv, gain_1, grad_hid)
    grad_in = scatter_head(last, rank)
    small = sum_small(jnp.concatenate([sums_2, sums_1], 0), dp_size)
    grad_bias_reduce = sum_dp(grad_bias_reduce[0], dp_size)
    return (
        layer_out,
        grad_in,
        grad_query,
        grad_key,
        grad_value,
        grad_proj,
        small[2],
        small[3],
        small[0],
        small[1],
        grad_expand,
        grad_bias_expand,
        grad_reduce,
        grad_bias_reduce,
    )


def solution(mesh):
    placed = (
        P("dp", "head"),
        P("dp"),
        P(None, "head"),
        P(None, "head"),
        P(None, "head"),
        P("head", None),
        P(),
        P(),
        P(),
        P(),
        P(None, ("dp", "head")),
        P(None, ("dp", "head")),
        P(None, ("dp", "head")),
        P("head"),
        P("dp", "head"),
    )
    return jax.shard_map(
        functools.partial(shards, mesh.shape["dp"]),
        mesh=mesh,
        in_specs=placed,
        out_specs=(
            P("dp", "head"),
            P("dp", "head"),
            P(None, "head"),
            P(None, "head"),
            P(None, "head"),
            P("head", None),
            P(),
            P(),
            P(),
            P(),
            P(None, ("dp", "head")),
            P(None, ("dp", "head")),
            P(None, ("dp", "head")),
            P("head"),
        ),
        check_vma=False,
    )
```

time: 565 us -> 494 us (0.87)
  Pallas kernels: 104 us -> 224 us
  waiting for transfers between devices: 229 us -> 141 us
  matrix products: 53.2 us -> 7.51 us
  starting transfers between devices: 93.6 us -> 66.1 us
  other arithmetic: 47 us -> 30.4 us
  local copies, waits for them, and re-layouts: 31.7 us -> 17.9 us
    pallas_call x4 -> x3, Pallas kernels: 87.5 us -> 207 us  [the longest x1 98.7 us: second(): pl.pallas_call(second_kernel, in_specs=[any_spec] * 2 + [vmem] * 8, out_s...]
    ppermute x58 -> x35, waiting for transfers between devices: 229 us -> 141 us  [flip(): return lax.ppermute(value, axis, [(k, k ^ mask) for k in range(size)])]
    dot_general x5 -> x1, matrix products: 53.2 us -> 7.51 us  [dot(): return lax.dot_general(left, right, dims, preferred_element_type=f32)]
    ppermute x58 -> x35, starting transfers between devices: 93.6 us -> 66.1 us  [flip(): return lax.ppermute(value, axis, [(k, k ^ mask) for k in range(size)])]
    unnamed x150 -> x70, local copies, waits for them, and re-layouts: 22.2 us -> 4.75 us
    dynamic_slice x10 -> x4, local copies, waits for them, and re-layouts: 2.02 us -> 8.15 us  [the longest x3 5.49 us: cols(): return lax.dynamic_slice_in_dim(value, (rank ^ k) * width, width, 1)]
  transfers between devices with their start and end apart: 58 -> 35, of which waited for: 27 -> 18; matrix products, arithmetic and copies ran while one was open for 16% -> 10% of each run, Pallas kernels for 10% -> 7%
where the time goes in v2:
time: 494 us; the launch traced here: 489 us
  Pallas kernels  224 us (45%)
  waiting for transfers between devices  141 us (29%)
  starting transfers between devices  66.1 us (13%)
  other arithmetic  30.4 us (6%)
  local copies, waits for them, and re-layouts  17.9 us (4%)
  matrix products  7.51 us (2%)
    ppermute x35, waiting for transfers between devices, flip(): return lax.ppermute(value, axis, [(k, k ^ mask) for k in range(size)])  141 us
    pallas_call x1, Pallas kernels, second(): pl.pallas_call(second_kernel, in_specs=[any_spec] * 2 + [vmem] * 8, out_s...  98.7 us
    pallas_call x1, Pallas kernels, first(): pl.pallas_call(functools.partial(first_kernel, masks, gather), in_specs=[...  92.7 us
    ppermute x35, starting transfers between devices, flip(): return lax.ppermute(value, axis, [(k, k ^ mask) for k in range(size)])  66.1 us
    pallas_call x1, Pallas kernels, attend_back(): pl.pallas_call(functools.partial(attend_back_kernel, heads), grid=(n,), i...  16.9 us
    pallas_call x1, Pallas kernels, finish(): pl.pallas_call(finish_kernel, grid=(rows // block,), in_specs=[rows_of(fe...  15.5 us
  transfers between devices with their start and end apart: 35, of which 18 were waited for; matrix products, arithmetic and copies ran while one was open for 10% of the time, Pallas kernels for 7%

profile of v2, /device:TPU:0, one launch (start us, length us, event | category | flops | bytes accessed | tf_op | source)
XLA Modules:
  0.0 489.4 jit_solution(7020240374848489357)
XLA Ops:
  1.3 92.7 %shard_map.254 = (bf16[3072,1024]{1,0:T(8,128)(2,1)}, bf16[3072,1024]{1,0:T(8,128)(2,1)}, bf16[3072,1024]{1,0:T(8,128)(2,1)}, bf16[3072,768]{1,0:T(8,128)(2,1)},...) custom-call(s32[1]{0:T(128)S(6)} %copy.57.kind, ...), custom_call_target="tpu_custom_call" | custom-call | tf_op jit(solution)/shard_map/pallas_call | solution.py:379
  94.0 1.3 slice_convert_fusion.bias
  95.3 98.7 %shard_map.255 = (bf16[3072,256]{1,0:T(8,128)(2,1)}, bf16[3072,1024]{1,0:T(8,128)(2,1)}, bf16[3072,1024]{1,0:T(8,128)(2,1)}, f32[3072,256]{1,0:T(8,128)}, bf16[1...) custom-call(bf16[3072,1024]{1,0:T(8,128)(2,1)} %get-tuple-element.35, ...), custom_call_target="tpu_custom_call" | custom-call | tf_op jit(solution)/shard_map/pallas_call | solution.py:638
  194.7 1.4 dynamic-slice_bitcast_fusion.5
  197.2 1.5 collective-permute-start.29
  199.4 2.7 constant_dynamic-slice_fusion.10.attended
  202.6 16.9 %shard_map.256.grad_qkv = bf16[3072,768]{1,0:T(8,128)(2,1)} custom-call(s32[1]{0:T(128)S(6)} %copy.57.kind, f32[2]{0:T(128)} %multiply_exponential_fusion.slopes, bf16[3072,768]{1,0:T(8,128)(2,1)} %get-tuple-element.43.qkv, bf16[3072,256]{1,0:T(8,128)(2,1)} %get-tuple-element.44.grad, bf16[3072,256]{1,0:T(8,128)(2,1)} %constant_dynamic-slice_fusion.10.attended, ...), custom_call_target="tpu_custom_call" | custom-call | flops 48318382080 | bytes 15728640 | tf_op jit(solution)/shard_map/pallas_call | solution.py:750
  219.5 15.5 %shard_map.257 = (bf16[3072,1024]{1,0:T(8,128)(2,1)}, f32[2,1024]{1,0:T(2,128)S(1)}) custom-call(bf16[3072,1024]{1,0:T(8,128)(2,1)} %get-tuple-element.35.x_in, bf16[3072,768]{1,0:T(8,128)(2,1)} %shard_map.256.grad_qkv, bf16[1024,768]{1,0:T(8,128)(2,1)S(1)} %pad_maximum_fusion.2.weight, f32[1,1024]{1,0:T(1,128)S(1)} %bitcast.346, ...), custom_call_target="tpu_custom_call" | custom-call | flops 4831838208 | bytes 25165824 | tf_op jit(solution)/shard_map/pallas_call | solution.py:801
  235.1 7.5 %fusion.77 = f32[1024,768]{1,0:T(8,128)S(1)} fusion(bf16[3072,1024]{1,0:T(8,128)(2,1)} %get-tuple-element.48, bf16[3072,768]{1,0:T(8,128)(2,1)S(1)} %copy-done.1), kind=kOutput, calls=%fused_computation.228 | convolution fusion | flops 4831838208 | bytes 14155776 | tf_op jit(solution)/shard_map/dot_general | solution.py:28
  242.6 1.7 copy-done.10
  245.4 1.5 collective-permute-start.4
  247.9 1.3 dynamic-slice_bitcast_fusion.1
  249.2 2.1 constant_dynamic-slice_fusion.9
  251.3 2.1 constant_dynamic-slice_fusion.12
  254.5 1.9 pad_maximum_fusion.1
  258.6 1.2 collective-permute-start.19
  259.9 2.5 collective-permute-done.19
  263.2 27.1 %collective-permute-start.27 = (bf16[2,1,128]{2,1,0:T(2,128)(2,1)S(1)}, bf16[2,1,128]{2,1,0:T(2,128)(2,1)S(1)}, u32[]{:S(2)}, u32[]{:S(2)}) collective-permute-start(bf16[2,1,128]{2,1,0:T(2,128)(2,1)S(1)} %pad_maximum_fusion.18), channel_id=1, source_target_pairs={{0,8},{4,12},{8,0},{12,4},{16,24},{20,28},{24,16},{28,20},{1,9},{5... | collective-permute-start | bytes 1544 | tf_op jit(solution)/shard_map/ppermute | solution.py:815
  290.5 2.8 collective-permute-start.21
  295.0 1.4 collective-permute-start.34
  296.4 1.4 collective-permute-done.28
  300.8 1.8 collective-permute-done.22
  303.7 1.3 fusion.27
  305.7 1.2 fusion.20
  307.0 1.6 collective-permute-start.30
  308.9 14.2 %collective-permute-done.23 = bf16[4,1024,128]{2,1,0:T(8,128)(2,1)S(1)} collective-permute-done((bf16[4,1024,128]{2,1,0:T(8,128)(2,1)}, bf16[4,1024,128]{2,1,0:T(8,128)(2,1)S(1)}, u32[]{:S(2)}, u32[]{:S(2)}) %collective-permute-start.23) | collective-permute-done | bytes 1048608 | tf_op jit(solution)/shard_map/ppermute | solution.py:815
  323.1 1.6 collective-permute-start.11
  327.3 7.2 %collective-permute-done.11 = bf16[1024,256]{0,1:T(8,128)(2,1)S(1)} collective-permute-done((bf16[1024,256]{0,1:T(8,128)(2,1)S(1)}, bf16[1024,256]{0,1:T(8,128)(2,1)S(1)}, u32[]{:S(2)}, u32[]{:S(2)}) %collective-permute-start.11) | collective-permute-done | bytes 524320 | tf_op jit(solution)/shard_map/ppermute | solution.py:815
  334.4 2.8 collective-permute-start.6
  337.5 6.0 %collective-permute-done.6 = bf16[1,128,768]{2,1,0:T(8,128)(2,1)S(1)} collective-permute-done((bf16[1,128,768]{2,1,0:T(8,128)(2,1)S(1)}, bf16[1,128,768]{2,1,0:T(8,128)(2,1)S(1)}, u32[]{:S(2)}, u32[]{:S(2)}) %collective-permute-start.6) | collective-permute-done | bytes 196640 | tf_op jit(solution)/shard_map/ppermute | solution.py:815
  347.7 2.2 collective-permute-done.12
  350.8 4.3 collective-permute-start.13
  355.3 4.5 collective-permute-done.13
  360.9 1.9 collective-permute-start.14
  362.8 15.6 %collective-permute-done.14 = bf16[1,32,1024]{2,1,0:T(8,128)(2,1)S(1)} collective-permute-done((bf16[1,32,1024]{2,1,0:T(8,128)(2,1)S(1)}, bf16[1,32,1024]{2,1,0:T(8,128)(2,1)S(1)}, u32[]{:S(2)}, u32[]{:S(2)}) %collective-permute-start.14) | collective-permute-done | bytes 65568 | tf_op jit(solution)/shard_map/ppermute | solution.py:815
  378.5 3.0 collective-permute-start.15
  381.6 1.9 convert_add_fusion
  383.4 5.3 %collective-permute-done.15 = bf16[1,32,1024]{2,1,0:T(8,128)(2,1)S(1)} collective-permute-done((bf16[1,32,1024]{2,1,0:T(8,128)(2,1)S(1)}, bf16[1,32,1024]{2,1,0:T(8,128)(2,1)S(1)}, u32[]{:S(2)}, u32[]{:S(2)}) %collective-permute-start.15) | collective-permute-done | bytes 65568 | tf_op jit(solution)/shard_map/ppermute | solution.py:815
  390.3 3.5 collective-permute-done.16
  396.2 7.0 %collective-permute-done.17 = bf16[4,32,1024]{2,1,0:T(8,128)(2,1)S(1)} collective-permute-done((bf16[4,32,1024]{2,1,0:T(8,128)(2,1)S(1)}, bf16[4,32,1024]{2,1,0:T(8,128)(2,1)S(1)}, u32[]{:S(2)}, u32[]{:S(2)}) %collective-permute-start.17) | collective-permute-done | bytes 262176 | tf_op jit(solution)/shard_map/ppermute | solution.py:815
  404.5 11.7 %collective-permute-done.9 = bf16[4,128,768]{2,1,0:T(8,128)(2,1)S(1)} collective-permute-done((bf16[4,128,768]{2,1,0:T(8,128)(2,1)S(1)}, bf16[4,128,768]{2,1,0:T(8,128)(2,1)S(1)}, u32[]{:S(2)}, u32[]{:S(2)}) %collective-permute-start.9) | collective-permute-done | bytes 786464 | tf_op jit(solution)/shard_map/ppermute | solution.py:815
  420.0 1.8 collective-permute-start.3
  423.5 1.4 collective-permute-start.1
  424.9 1.7 fusion.73
  426.7 30.8 %collective-permute-done.3 = bf16[3072,256]{1,0:T(8,128)(2,1)} collective-permute-done((bf16[3072,256]{1,0:T(8,128)(2,1)S(1)}, bf16[3072,256]{1,0:T(8,128)(2,1)}, u32[]{:S(2)}, u32[]{:S(2)}) %collective-permute-start.3) | collective-permute-done | bytes 1572896 | tf_op jit(solution)/shard_map/ppermute | solution.py:815
  457.5 4.0 fusion.1
  461.5 24.9 %collective-permute-done.1 = bf16[3072,256]{1,0:T(8,128)(2,1)S(1)} collective-permute-done((bf16[3072,256]{1,0:T(8,128)(2,1)S(1)}, bf16[3072,256]{1,0:T(8,128)(2,1)S(1)}, u32[]{:S(2)}, u32[]{:S(2)}) %collective-permute-start.1) | collective-permute-done | bytes 1572896 | tf_op jit(solution)/shard_map/ppermute | solution.py:815
  486.4 2.6 fusion.4
  (170 shorter events, 35.9 us)
Async XLA Ops:
  194.1 96.3 %collective-permute-start.32 = (f32[256]{0:T(256)}, f32[256]{0:T(256)S(1)}, u32[]{:S(2)}, u32[]{:S(2)}) collective-permute-start(f32[256]{0:T(256)} %bitcast.364), channel_id=1, source_target_pairs={{0,4},{4,0},{8,12},{12,8},{16,20},{20,16},{24,28},{28,24},{1,5},{5... | collective-permute-start | bytes 3080 | tf_op jit(solution)/shard_map/ppermute | solution.py:815
  194.7 4.0 copy-start.15
  194.7 4.7 copy-start.7
  194.7 4.7 copy-start.8
  194.7 4.7 copy-start.9
  197.2 107.9 %collective-permute-start.29 = (bf16[4,1024,128]{2,1,0:T(8,128)(2,1)}, bf16[4,1024,128]{2,1,0:T(8,128)(2,1)}, u32[]{:S(2)}, u32[]{:S(2)}) collective-permute-start(bf16[4,1024,128]{2,1,0:T(8,128)(2,1)} %pad_maximum_fusion.5), channel_id=1, source_target_pairs={{0,4},{4,0},{8,12},{12,8},{16,20},{20,16},{24,28},{28,24},{1,5},{5... | collective-permute-start | bytes 3145736 | tf_op jit(solution)/shard_map/ppermute | solution.py:815
  198.7 61.1 %collective-permute-start.26 = (bf16[4,1,128]{2,1,0:T(2,128)(2,1)S(1)}, bf16[4,1,128]{2,1,0:T(2,128)(2,1)S(1)}, u32[]{:S(2)}, u32[]{:S(2)}) collective-permute-start(bf16[4,1,128]{2,1,0:T(2,128)(2,1)S(1)} %pad_maximum_fusion.17), channel_id=1, source_target_pairs={{0,4},{4,0},{8,12},{12,8},{16,20},{20,16},{24,28},{28,24},{1,5},{5... | collective-permute-start | bytes 3080 | tf_op jit(solution)/shard_map/ppermute | solution.py:815
  202.6 16.9 %copy-start = (f32[1024]{0:T(1024)S(1)}, f32[1024]{0:T(1024)}, u32[]{:S(2)}) copy-start(f32[1024]{0:T(1024)} %param.21) | copy-start | bytes 12292
  219.5 15.5 %copy-start.14 = (f32[2,1024]{1,0:T(2,128)S(1)}, f32[2,1024]{1,0:T(2,128)}, u32[]{:S(2)}) copy-start(f32[2,1024]{1,0:T(2,128)} %get-tuple-element.50) | copy-start | bytes 24580
  219.5 15.6 %copy-start.1 = (bf16[3072,768]{1,0:T(8,128)(2,1)S(1)}, bf16[3072,768]{1,0:T(8,128)(2,1)}, u32[]{:S(2)}) copy-start(bf16[3072,768]{1,0:T(8,128)(2,1)} %shard_map.256.grad_qkv) | copy-start | bytes 14155780
  235.0 23.6 %collective-permute-start.18 = (f32[4,1024]{1,0:T(4,128)S(1)}, f32[4,1024]{1,0:T(4,128)S(1)}, u32[]{:S(2)}, u32[]{:S(2)}) collective-permute-start(f32[4,1024]{1,0:T(4,128)S(1)} %pad_maximum_fusion.16), channel_id=1, source_target_pairs={{0,1},{1,0},{2,3},{3,2},{4,5},{5,4},{6,7},{7,6},{8,9},{9,8},{10,11... | collective-permute-start | bytes 49160 | tf_op jit(solution)/shard_map/ppermute | solution.py:815
  245.4 57.9 %collective-permute-start.4 = (bf16[4,128,768]{2,1,0:T(8,128)(2,1)}, bf16[4,128,768]{2,1,0:T(8,128)(2,1)}, u32[]{:S(2)}, u32[]{:S(2)}) collective-permute-start(bf16[4,128,768]{2,1,0:T(8,128)(2,1)} %pad_maximum_fusion.6), channel_id=1, source_target_pairs={{0,4},{4,0},{8,12},{12,8},{16,20},{20,16},{24,28},{28,24},{1,5},{5... | collective-permute-start | bytes 2359304 | tf_op jit(solution)/shard_map/ppermute | solution.py:815
  256.6 33.7 %copy-start.17 = (f32[1,256]{1,0:T(1,128)S(1)}, f32[1,256]{1,0:T(1,128)}, u32[]{:S(2)}) copy-start(f32[1,256]{1,0:T(1,128)} %get-tuple-element.55) | copy-start | bytes 3076
  258.6 3.8 collective-permute-start.19
  262.4 28.1 %collective-permute-start.20 = (f32[4,1024]{1,0:T(4,128)S(1)}, f32[4,1024]{1,0:T(4,128)S(1)}, u32[]{:S(2)}, u32[]{:S(2)}) collective-permute-start(f32[4,1024]{1,0:T(4,128)S(1)} %add.335), channel_id=1, source_target_pairs={{0,4},{4,0},{8,12},{12,8},{16,20},{20,16},{24,28},{28,24},{1,5},{5... | collective-permute-start | bytes 49160 | tf_op jit(solution)/shard_map/ppermute | solution.py:815
  263.2 30.0 %collective-permute-start.27 = (bf16[2,1,128]{2,1,0:T(2,128)(2,1)S(1)}, bf16[2,1,128]{2,1,0:T(2,128)(2,1)S(1)}, u32[]{:S(2)}, u32[]{:S(2)}) collective-permute-start(bf16[2,1,128]{2,1,0:T(2,128)(2,1)S(1)} %pad_maximum_fusion.18), channel_id=1, source_target_pairs={{0,8},{4,12},{8,0},{12,4},{16,24},{20,28},{24,16},{28,20},{1,9},{5... | collective-permute-start | bytes 1544 | tf_op jit(solution)/shard_map/ppermute | solution.py:815
  290.4 15.3 %copy-start.5 = (bf16[1024,1024]{1,0:T(8,128)(2,1)S(1)}, bf16[1024,1024]{1,0:T(8,128)(2,1)}, u32[]{:S(2)}) copy-start(bf16[1024,1024]{1,0:T(8,128)(2,1)} %get-tuple-element.54) | copy-start | bytes 6291460
  290.4 3.6 collective-permute-start.33
  290.5 4.5 collective-permute-start.21
  293.3 4.5 collective-permute-start.28
  294.0 12.9 %collective-permute-start.10 = (bf16[1024,512]{0,1:T(8,128)(2,1)}, bf16[1024,512]{0,1:T(8,128)(2,1)S(1)}, u32[]{:S(2)}, u32[]{:S(2)}) collective-permute-start(bf16[1024,512]{0,1:T(8,128)(2,1)} %pad_maximum_fusion.3), channel_id=1, source_target_pairs={{0,1},{1,0},{2,3},{3,2},{4,5},{5,4},{6,7},{7,6},{8,9},{9,8},{10,11... | collective-permute-start | bytes 3145736 | tf_op jit(solution)/shard_map/ppermute | solution.py:815
  295.0 4.5 collective-permute-start.34
  297.8 4.8 collective-permute-start.22
  299.5 23.7 %collective-permute-start.23 = (bf16[4,1024,128]{2,1,0:T(8,128)(2,1)}, bf16[4,1024,128]{2,1,0:T(8,128)(2,1)S(1)}, u32[]{:S(2)}, u32[]{:S(2)}) collective-permute-start(bf16[4,1024,128]{2,1,0:T(8,128)(2,1)} %pad_maximum_fusion.4), channel_id=1, source_target_pairs={{0,4},{4,0},{8,12},{12,8},{16,20},{20,16},{24,28},{28,24},{1,5},{5... | collective-permute-start | bytes 3145736 | tf_op jit(solution)/shard_map/ppermute | solution.py:815
  302.6 114.0 %collective-permute-start.2 = (bf16[3072,512]{1,0:T(8,128)(2,1)}, bf16[3072,512]{1,0:T(8,128)(2,1)S(1)}, u32[]{:S(2)}, u32[]{:S(2)}) collective-permute-start(bf16[3072,512]{1,0:T(8,128)(2,1)} %pad_maximum_fusion.1), channel_id=1, source_target_pairs={{0,1},{1,0},{2,3},{3,2},{4,5},{5,4},{6,7},{7,6},{8,9},{9,8},{10,11... | collective-permute-start | bytes 9437192 | tf_op jit(solution)/shard_map/ppermute | solution.py:815
  303.2 118.6 %collective-permute-start = (bf16[3072,512]{1,0:T(8,128)(2,1)S(1)}, bf16[3072,512]{1,0:T(8,128)(2,1)S(1)}, u32[]{:S(2)}, u32[]{:S(2)}) collective-permute-start(bf16[3072,512]{1,0:T(8,128)(2,1)S(1)} %pad_maximum_fusion), channel_id=1, source_target_pairs={{0,1},{1,0},{2,3},{3,2},{4,5},{5,4},{6,7},{7,6},{8,9},{9,8},{10,11... | collective-permute-start | bytes 9437192 | tf_op jit(solution)/shard_map/ppermute | solution.py:815
  305.1 19.9 %collective-permute-start.5 = (bf16[2,128,768]{2,1,0:T(8,128)(2,1)S(1)}, bf16[2,128,768]{2,1,0:T(8,128)(2,1)S(1)}, u32[]{:S(2)}, u32[]{:S(2)}) collective-permute-start(bf16[2,128,768]{2,1,0:T(8,128)(2,1)S(1)} %pad_maximum_fusion.10), channel_id=1, source_target_pairs={{0,8},{4,12},{8,0},{12,4},{16,24},{20,28},{24,16},{28,20},{1,9},{5... | collective-permute-start | bytes 1179656 | tf_op jit(solution)/shard_map/ppermute | solution.py:815
  306.9 17.8 %copy-start.4 = (bf16[1024,1024]{1,0:T(8,128)(2,1)S(1)}, bf16[1024,1024]{1,0:T(8,128)(2,1)}, u32[]{:S(2)}) copy-start(bf16[1024,1024]{1,0:T(8,128)(2,1)} %get-tuple-element.52) | copy-start | bytes 6291460
  307.0 38.6 %collective-permute-start.30 = (bf16[2,1024,128]{2,1,0:T(8,128)(2,1)S(1)}, bf16[2,1024,128]{2,1,0:T(8,128)(2,1)S(1)}, u32[]{:S(2)}, u32[]{:S(2)}) collective-permute-start(bf16[2,1024,128]{2,1,0:T(8,128)(2,1)S(1)} %pad_maximum_fusion.9), channel_id=1, source_target_pairs={{0,8},{4,12},{8,0},{12,4},{16,24},{20,28},{24,16},{28,20},{1,9},{5... | collective-permute-start | bytes 1572872 | tf_op jit(solution)/shard_map/ppermute | solution.py:815
  323.1 11.3 %collective-permute-start.11 = (bf16[1024,256]{0,1:T(8,128)(2,1)S(1)}, bf16[1024,256]{0,1:T(8,128)(2,1)S(1)}, u32[]{:S(2)}, u32[]{:S(2)}) collective-permute-start(bf16[1024,256]{0,1:T(8,128)(2,1)S(1)} %fusion.5), channel_id=1, source_target_pairs={{0,2},{1,3},{2,0},{3,1},{4,6},{5,7},{6,4},{7,5},{8,10},{9,11},{10,... | collective-permute-start | bytes 1572872 | tf_op jit(solution)/shard_map/ppermute | solution.py:815
  324.9 25.9 %collective-permute-start.24 = (bf16[2,1024,128]{2,1,0:T(8,128)(2,1)S(1)}, bf16[2,1024,128]{2,1,0:T(8,128)(2,1)S(1)}, u32[]{:S(2)}, u32[]{:S(2)}) collective-permute-start(bf16[2,1024,128]{2,1,0:T(8,128)(2,1)S(1)} %pad_maximum_fusion.8), channel_id=1, source_target_pairs={{0,8},{4,12},{8,0},{12,4},{16,24},{20,28},{24,16},{28,20},{1,9},{5... | collective-permute-start | bytes 1572872 | tf_op jit(solution)/shard_map/ppermute | solution.py:815
  334.4 9.1 %collective-permute-start.6 = (bf16[1,128,768]{2,1,0:T(8,128)(2,1)S(1)}, bf16[1,128,768]{2,1,0:T(8,128)(2,1)S(1)}, u32[]{:S(2)}, u32[]{:S(2)}) collective-permute-start(bf16[1,128,768]{2,1,0:T(8,128)(2,1)S(1)} %fusion.29), channel_id=1, source_target_pairs={{0,16},{4,20},{8,24},{12,28},{16,0},{20,4},{24,8},{28,12},{1,17},{... | collective-permute-start | bytes 589832 | tf_op jit(solution)/shard_map/ppermute | solution.py:815
  343.5 6.4 %collective-permute-start.12 = (bf16[4,32,1024]{2,1,0:T(8,128)(2,1)S(1)}, bf16[4,32,1024]{2,1,0:T(8,128)(2,1)S(1)}, u32[]{:S(2)}, u32[]{:S(2)}) collective-permute-start(bf16[4,32,1024]{2,1,0:T(8,128)(2,1)S(1)} %pad_maximum_fusion.12), channel_id=1, source_target_pairs={{0,4},{4,0},{8,12},{12,8},{16,20},{20,16},{24,28},{28,24},{1,5},{5... | collective-permute-start | bytes 786440 | tf_op jit(solution)/shard_map/ppermute | solution.py:815
  345.6 15.3 %collective-permute-start.7 = (bf16[1,128,768]{2,1,0:T(8,128)(2,1)S(1)}, bf16[1,128,768]{2,1,0:T(8,128)(2,1)S(1)}, u32[]{:S(2)}, u32[]{:S(2)}) collective-permute-start(bf16[1,128,768]{2,1,0:T(8,128)(2,1)S(1)} %bitcast.351), channel_id=1, source_target_pairs={{0,16},{4,20},{8,24},{12,28},{16,0},{20,4},{24,8},{28,12},{1,17},{... | collective-permute-start | bytes 589832 | tf_op jit(solution)/shard_map/ppermute | solution.py:815
  349.9 28.6 %collective-permute-start.31 = (bf16[1,1024,128]{2,1,0:T(8,128)(2,1)S(1)}, bf16[1,1024,128]{2,1,0:T(8,128)(2,1)S(1)}, u32[]{:S(2)}, u32[]{:S(2)}) collective-permute-start(bf16[1,1024,128]{2,1,0:T(8,128)(2,1)S(1)} %fusion.22), channel_id=1, source_target_pairs={{0,16},{4,20},{8,24},{12,28},{16,0},{20,4},{24,8},{28,12},{1,17},{... | collective-permute-start | bytes 786440 | tf_op jit(solution)/shard_map/ppermute | solution.py:815
  350.8 8.9 %collective-permute-start.13 = (bf16[2,32,1024]{2,1,0:T(8,128)(2,1)S(1)}, bf16[2,32,1024]{2,1,0:T(8,128)(2,1)S(1)}, u32[]{:S(2)}, u32[]{:S(2)}) collective-permute-start(bf16[2,32,1024]{2,1,0:T(8,128)(2,1)S(1)} %pad_maximum_fusion.14), channel_id=1, source_target_pairs={{0,8},{4,12},{8,0},{12,4},{16,24},{20,28},{24,16},{28,20},{1,9},{5... | collective-permute-start | bytes 393224 | tf_op jit(solution)/shard_map/ppermute | solution.py:815
  359.8 29.7 %collective-permute-start.25 = (bf16[1,1024,128]{2,1,0:T(8,128)(2,1)S(1)}, bf16[1,1024,128]{2,1,0:T(8,128)(2,1)S(1)}, u32[]{:S(2)}, u32[]{:S(2)}) collective-permute-start(bf16[1,1024,128]{2,1,0:T(8,128)(2,1)S(1)} %fusion.19), channel_id=1, source_target_pairs={{0,16},{4,20},{8,24},{12,28},{16,0},{20,4},{24,8},{28,12},{1,17},{... | collective-permute-start | bytes 786440 | tf_op jit(solution)/shard_map/ppermute | solution.py:815
  360.9 17.6 %collective-permute-start.14 = (bf16[1,32,1024]{2,1,0:T(8,128)(2,1)S(1)}, bf16[1,32,1024]{2,1,0:T(8,128)(2,1)S(1)}, u32[]{:S(2)}, u32[]{:S(2)}) collective-permute-start(bf16[1,32,1024]{2,1,0:T(8,128)(2,1)S(1)} %fusion.44), channel_id=1, source_target_pairs={{0,16},{4,20},{8,24},{12,28},{16,0},{20,4},{24,8},{28,12},{1,17},{... | collective-permute-start | bytes 196616 | tf_op jit(solution)/shard_map/ppermute | solution.py:815
  378.4 16.5 %collective-permute-start.8 = (bf16[2,128,768]{2,1,0:T(8,128)(2,1)S(1)}, bf16[2,128,768]{2,1,0:T(8,128)(2,1)S(1)}, u32[]{:S(2)}, u32[]{:S(2)}) collective-permute-start(bf16[2,128,768]{2,1,0:T(8,128)(2,1)S(1)} %pad_maximum_fusion.11), channel_id=1, source_target_pairs={{0,8},{4,12},{8,0},{12,4},{16,24},{20,28},{24,16},{28,20},{1,9},{5... | collective-permute-start | bytes 1179656 | tf_op jit(solution)/shard_map/ppermute | solution.py:815
  378.5 10.3 %collective-permute-start.15 = (bf16[1,32,1024]{2,1,0:T(8,128)(2,1)S(1)}, bf16[1,32,1024]{2,1,0:T(8,128)(2,1)S(1)}, u32[]{:S(2)}, u32[]{:S(2)}) collective-permute-start(bf16[1,32,1024]{2,1,0:T(8,128)(2,1)S(1)} %bitcast.354), channel_id=1, source_target_pairs={{0,16},{4,20},{8,24},{12,28},{16,0},{20,4},{24,8},{28,12},{1,17},{... | collective-permute-start | bytes 196616 | tf_op jit(solution)/shard_map/ppermute | solution.py:815
  388.8 5.0 %collective-permute-start.16 = (bf16[2,32,1024]{2,1,0:T(8,128)(2,1)S(1)}, bf16[2,32,1024]{2,1,0:T(8,128)(2,1)S(1)}, u32[]{:S(2)}, u32[]{:S(2)}) collective-permute-start(bf16[2,32,1024]{2,1,0:T(8,128)(2,1)S(1)} %pad_maximum_fusion.15), channel_id=1, source_target_pairs={{0,8},{4,12},{8,0},{12,4},{16,24},{20,28},{24,16},{28,20},{1,9},{5... | collective-permute-start | bytes 393224 | tf_op jit(solution)/shard_map/ppermute | solution.py:815
  393.9 9.3 %collective-permute-start.17 = (bf16[4,32,1024]{2,1,0:T(8,128)(2,1)S(1)}, bf16[4,32,1024]{2,1,0:T(8,128)(2,1)S(1)}, u32[]{:S(2)}, u32[]{:S(2)}) collective-permute-start(bf16[4,32,1024]{2,1,0:T(8,128)(2,1)S(1)} %pad_maximum_fusion.13), channel_id=1, source_target_pairs={{0,4},{4,0},{8,12},{12,8},{16,20},{20,16},{24,28},{28,24},{1,5},{5... | collective-permute-start | bytes 786440 | tf_op jit(solution)/shard_map/ppermute | solution.py:815
  395.1 21.2 %collective-permute-start.9 = (bf16[4,128,768]{2,1,0:T(8,128)(2,1)S(1)}, bf16[4,128,768]{2,1,0:T(8,128)(2,1)S(1)}, u32[]{:S(2)}, u32[]{:S(2)}) collective-permute-start(bf16[4,128,768]{2,1,0:T(8,128)(2,1)S(1)} %pad_maximum_fusion.7), channel_id=1, source_target_pairs={{0,4},{4,0},{8,12},{12,8},{16,20},{20,16},{24,28},{28,24},{1,5},{5... | collective-permute-start | bytes 2359304 | tf_op jit(solution)/shard_map/ppermute | solution.py:815
  419.3 3.5 slice-start
  420.0 37.5 %collective-permute-start.3 = (bf16[3072,256]{1,0:T(8,128)(2,1)S(1)}, bf16[3072,256]{1,0:T(8,128)(2,1)}, u32[]{:S(2)}, u32[]{:S(2)}) collective-permute-start(bf16[3072,256]{1,0:T(8,128)(2,1)S(1)} %fusion), channel_id=1, source_target_pairs={{0,2},{1,3},{2,0},{3,1},{4,6},{5,7},{6,4},{7,5},{8,10},{9,11},{10,... | collective-permute-start | bytes 4718600 | tf_op jit(solution)/shard_map/ppermute | solution.py:815
  423.5 62.9 %collective-permute-start.1 = (bf16[3072,256]{1,0:T(8,128)(2,1)S(1)}, bf16[3072,256]{1,0:T(8,128)(2,1)S(1)}, u32[]{:S(2)}, u32[]{:S(2)}) collective-permute-start(bf16[3072,256]{1,0:T(8,128)(2,1)S(1)} %fusion.2), channel_id=1, source_target_pairs={{0,2},{1,3},{2,0},{3,1},{4,6},{5,7},{6,4},{7,5},{8,10},{9,11},{10,... | collective-permute-start | bytes 4718600 | tf_op jit(solution)/shard_map/ppermute | solution.py:815
  426.7 59.7 %copy-start.16 = (f32[256]{0:T(256)S(1)}, f32[256]{0:T(256)}, u32[]{:S(2)}) copy-start(f32[256]{0:T(256)} %param.28) | copy-start | bytes 3076
  457.5 28.9 %copy-start.2 = (f32[3072,256]{1,0:T(8,128)S(1)}, f32[3072,256]{1,0:T(8,128)}, u32[]{:S(2)}) copy-start(f32[3072,256]{1,0:T(8,128)} %get-tuple-element.41) | copy-start | bytes 9437188
  (9 other events, 16.9 us)

commit v3 on v2

--- a/solution.py
+++ b/solution.py
@@ -589,7 +589,7 @@
         wide[...] += dot(low, gp_low, TN)
         narrow[...] += dot(g, activated, TN)
         scatter.middle(r)
-        proj[...] += dot(a, back_low, TN)
+        proj[...] += dot(back_low, a, TN)
 
         @pl.when(r >= 1)
         def _():
@@ -677,200 +677,596 @@
     )(x, a, grad_out, layer_in, w_proj, w_expand, w_reduce, gain, shift, bias)
 
 
-def attend_back_kernel(heads, kind, slopes, qkv, grad, attended, logsum, grad_qkv, total_q, delta):
-    block = SHORT
-    j = pl.program_id(0)
-    n = pl.num_programs(0)
-    high = jnp.where(kind[0] == 1, n, j + 1)
-    at = pl.multiple_of(j * block, block)
-    key_place = lax.broadcasted_iota(jnp.int32, (block, block), 0)
-    query_place = lax.broadcasted_iota(jnp.int32, (block, block), 1)
-    width = heads * HEAD_DIM
-
-    @pl.when(j == 0)
-    def _():
-        total_q[...] = jnp.zeros_like(total_q)
-
-        def fill(i, _):
-            here = pl.ds(pl.multiple_of(i * block, block), block)
-            for h in range(heads):
-                cols = slice(h * HEAD_DIM, (h + 1) * HEAD_DIM)
-                both = grad[here, cols].astype(f32) * attended[here, cols].astype(f32)
-                delta[i, h : h + 1, :] = jnp.sum(both.T, axis=0, keepdims=True)
-            return 0
-
-        lax.fori_loop(0, n, fill, 0)
-
-    def pair(h, i, masked):
-        start = pl.multiple_of(i * block, block)
-        cols = slice(h * HEAD_DIM, (h + 1) * HEAD_DIM)
-        q = qkv[pl.ds(start, block), h * HEAD_DIM : (h + 1) * HEAD_DIM]
-        k = qkv[pl.ds(at, block), width + h * HEAD_DIM : width + (h + 1) * HEAD_DIM]
-        v = qkv[pl.ds(at, block), 2 * width + h * HEAD_DIM : 2 * width + (h + 1) * HEAD_DIM]
-        g = grad[pl.ds(start, block), cols]
-        place = (key_place + (j - i) * block).astype(f32) * (slopes[h] * LOG2E)
-        s = dot(k, q, NT) * (SCALE * LOG2E) + place
-        if masked:
-            s = jnp.where(key_place <= query_place, s, masked_value)
-        p = jnp.exp2(s - logsum[i, h : h + 1, :])
-        ds = (p * (dot(v, g, NT) - delta[i, h : h + 1, :])).astype(bf16)
-        dv = dot(p.astype(bf16), g)
-        dk = dot(ds, q)
-        total_q[pl.ds(start, block), cols] += dot(ds, k, TN)
-        return dk, dv
-
-    first = [pair(h, j, True) for h in range(heads)]
-    carry = tuple(x for both in first for x in both)
-
-    def step(i, carry):
-        new = []
-        for h in range(heads):
-            dk, dv = pair(h, i, False)
-            new += [carry[2 * h] + dk, carry[2 * h + 1] + dv]
-        return tuple(new)
-
-    carry = lax.fori_loop(j + 1, high, step, carry)
-    for h in range(heads):
-        cols = slice(h * HEAD_DIM, (h + 1) * HEAD_DIM)
-        grad_qkv[:, cols] = (total_q[pl.ds(at, block), cols] * SCALE).astype(bf16)
-        grad_qkv[:, width + h * HEAD_DIM : width + (h + 1) * HEAD_DIM] = (
-            carry[2 * h] * SCALE
+class DpScatter:
+    def __init__(self, part, recv_buf, masks, send, recv):
+        self.part, self.recv_buf, self.masks = part, recv_buf, masks
+        self.group = lax.axis_index("dp")
+        self.send, self.recv = send, recv
+        size = 1 << len(masks)
+        left, at = list(range(size)), 0
+        self.plan = []
+        for mask in masks:
+            mine = [k for k in left if not k & mask]
+            self.plan.append((mask, [(k, at + p) for p, k in enumerate(mine)]))
+            at += len(mine)
+            left = mine
+
+    def where(self, k):
+        who = self.group
+        for mask in self.masks:
+            if k & mask:
+                who = partner(who, mask)
+        return self.part(who)
+
+    def copy(self, mask, k, slot):
+        return send_to(
+            self.where(k ^ mask), self.recv_buf.at[slot], self.send.at[slot], self.recv.at[slot],
+            dp=partner(self.group, mask),
+        )
+
+    def start(self, step):
+        mask, items = self.plan[step]
+        for k, slot in items:
+            self.copy(mask, k, slot).start()
+
+    def arrive(self, step):
+        mask, items = self.plan[step]
+        for k, slot in items:
+            self.copy(mask, k, slot).wait_recv()
+            ref = self.where(k)
+            ref[...] = (ref[...].astype(f32) + self.recv_buf[slot].astype(f32)).astype(bf16)
+
+    def sent(self):
+        for mask, items in self.plan:
+            for k, slot in items:
+                self.copy(mask, k, slot).wait_send()
+
+
+class DpSpread:
+    def __init__(self, own, slot_of, masks, send, recv):
+        self.own, self.slot_of = own, slot_of
+        self.masks = list(reversed(masks))
+        self.group = lax.axis_index("dp")
+        self.send, self.recv = send, recv
+        held, self.plan, at = [0], [], 0
+        for mask in self.masks:
+            self.plan.append((mask, [(k, at + p) for p, k in enumerate(held)]))
+            at += len(held)
+            held = held + [k ^ mask for k in held]
+
+    def block(self, k):
+        who = self.group
+        for mask in self.masks:
+            if k & mask:
+                who = partner(who, mask)
+        return self.slot_of(who)
+
+    def copies(self, step, there):
+        mask, items = self.plan[step]
+        out = []
+        for k, sem in items:
+            if there:
+                src, at = (self.own if k == 0 else self.block(k)), self.block(k)
+            else:
+                src = at = self.block(k ^ mask)
+            out.append(
+                send_to(src, at, self.send.at[sem], self.recv.at[sem], dp=partner(self.group, mask))
+            )
+        return out
+
+    def start(self, step):
+        for copy in self.copies(step, True):
+            copy.start()
+
+    def arrive(self, step):
+        for copy in self.copies(step, False):
+            copy.wait_recv()
+
+    def sent(self):
+        for step in range(len(self.plan)):
+            for copy in self.copies(step, True):
+                copy.wait_send()
+
+
+class DpSum:
+    def __init__(self, buf, recv_buf, out, masks, sems, keep_sem):
+        size = 1 << len(masks)
+        rows = buf.shape[0] // size
+        self.steps = len(masks)
+        self.scatter = DpScatter(lambda k: buf.at[at_rows(k, rows), :], recv_buf, masks, sems.at[0], sems.at[1])
+        me = lax.axis_index("dp")
+        own = buf.at[at_rows(me, rows), :]
+        self.keep = pltpu.make_async_copy(own, out.at[at_rows(me, rows), :], keep_sem)
+        self.spread = DpSpread(own, lambda k: out.at[at_rows(k, rows), :], masks, sems.at[2], sems.at[3])
+
+    def start(self):
+        self.scatter.start(0)
+
+    def advance(self, step):
+        if step < self.steps:
+            self.scatter.arrive(step)
+            if step + 1 < self.steps:
+                self.scatter.start(step + 1)
+            else:
+                self.keep.start()
+                self.spread.start(0)
+        else:
+            self.spread.arrive(step - self.steps)
+            if step + 1 < 2 * self.steps:
+                self.spread.start(step - self.steps + 1)
+
+    def settle(self):
+        self.scatter.sent()
+        self.spread.sent()
+        self.keep.wait()
+
+
+class HeadSum:
+    def __init__(self, width, src, mine, from_core, far, from_chip, sems):
+        self.width, self.src, self.mine = width, src, mine
+        self.from_core, self.far, self.from_chip, self.sems = from_core, far, from_chip, sems
+        self.me = lax.axis_index("head")
+        self.core, self.chip = partner(self.me, 1), partner(self.me, 2)
+
+    def to_core(self, r, k):
+        who = self.core if k == 0 else partner(self.core, 2)
+        return send_to(
+            self.src(r).at[:, at_cols(who, self.width)],
+            self.from_core.at[at_rows(r), k * self.width : (k + 1) * self.width],
+            self.sems.at[2 * k, r],
+            self.sems.at[2 * k + 1, r],
+            head=self.core,
+        )
+
+    def to_chip(self, r):
+        return send_to(
+            self.far(r), self.from_chip.at[at_rows(r), :], self.sems.at[4, r], self.sems.at[5, r], head=self.chip
+        )
+
+    def start(self, r):
+        self.to_core(r, 1).start()
+        self.to_core(r, 0).start()
+
+    def middle(self, r):
+        self.to_core(r, 1).wait()
+        self.far(r)[...] = (
+            self.mine(r, self.chip, 1) + self.from_core[at_rows(r), self.width :].astype(f32)
         ).astype(bf16)
-        grad_qkv[:, 2 * width + h * HEAD_DIM : 2 * width + (h + 1) * HEAD_DIM] = carry[
-            2 * h + 1
-        ].astype(bf16)
-
-
-def attend_back(qkv, grad, attended, logsum, slopes, kind):
+        self.to_chip(r).start()
+        self.to_core(r, 0).wait()
+        return self.mine(r, self.me, 0) + self.from_core[at_rows(r), : self.width].astype(f32)
+
+    def finish(self, r):
+        self.to_chip(r).wait()
+        return self.from_chip[at_rows(r), :].astype(f32)
+
+
+def third_kernel(
+    masks, scatter_inside,
+    kind, qkv, grad_heads, logsum, wq, wk, wv, gain, sums_2, grad_bias, grad_bias_reduce, wide, narrow,
+    a_in, x_in, normed_in, grad_hid, ffn, proj,
+    ffn_sum, total_sum, sum_a, sum_b, wide_sum, narrow_sum, small,
+    dqkv, dk_acc, dv_acc, dq_acc, delta, wgrad, slots, pay_a, pay_b, recv_a, recv_b, recv_w, recv_n,
+    s_core, s_far, s_chip, s_near, s_mine, s_out, f_src, f_core, f_far, f_chip, small_recv,
+    wg_sems, s_sems, mine_sems, out_sems, f_sems, a_sems, b_sems, w_sems, n_sems, slot_sems, keep_sems, small_sems, total_sems,
+):
     rows = qkv.shape[0]
-    width = qkv.shape[1] // 3
-    heads = width // HEAD_DIM
+    width = grad_heads.shape[1]
+    features = x_in.shape[1]
     block = SHORT
     n = rows // block
+    heads = width // HEAD_DIM
+    me = lax.axis_index("head")
+    group = lax.axis_index("dp")
+    steps = len(masks)
+    greet(masks)
+
+    if scatter_inside:
+        local = wide_sum.shape[1]
+        wide_rs = DpScatter(lambda k: wide.at[:, at_cols(k, local)], recv_w, masks, w_sems.at[0], w_sems.at[1])
+        narrow_rs = DpScatter(lambda k: narrow.at[:, at_cols(k, local)], recv_n, masks, n_sems.at[0], n_sems.at[1])
+        wide_rs.start(0)
+        narrow_rs.start(0)
+
+    n_proj = features // block
+    n_side = n_proj + n
+
+    def side_src(c):
+        return proj.at[at_rows(c), :] if c < n_proj else ffn.at[at_rows(c - n_proj), :]
+
+    def side_load(c, k):
+        who = me if k == 0 else partner(me, 2)
+        return pltpu.make_async_copy(
+            side_src(c).at[:, at_cols(who, width)], s_mine.at[c % 2, k], mine_sems.at[k, c]
+        )
+
+    def side_mine(c, who, k):
+        side_load(c, k).wait()
+        return s_mine[c % 2, k].astype(f32)
+
+    side = HeadSum(width, side_src, side_mine, s_core, lambda c: s_far.at[c % 3], s_chip, s_sems)
+
+    def side_copy(c):
+        return pltpu.make_async_copy(s_out.at[c % 2], ffn_sum.at[at_rows(c - n_proj), :], out_sems.at[c])
+
+    def side_start(c):
+        side_load(c, 1).start()
+        side_load(c, 0).start()
+        side.start(c)
+
+    def side_finish(c):
+        value = (s_near[c % 3] + side.finish(c)).astype(bf16)
+        if c < n_proj:
+            pay_a[c * block : (c + 1) * block, 3 * HEAD_DIM :] = value
+        else:
+            if c - 2 >= n_proj:
+                side_copy(c - 2).wait()
+            s_out[c % 2] = value
+            side_copy(c).start()
+
+    def side_step(c):
+        if c < n_side:
+            s_near[c % 3] = side.middle(c)
+            if c + 2 < n_side:
+                side_start(c + 2)
+        if 0 <= c - 2 < n_side:
+            side_finish(c - 2)
+
+    side_start(0)
+    side_start(1)
+
+    apart = (1 - kind[0]).astype(f32) * masked_value
+    slopes = [s * LOG2E for s in head_slopes(me, heads)]
+    two = 2 * block
+    pairs = rows // two
+    attended = pltpu.make_async_copy(a_in.at[:, at_cols(me, width)], dqkv.at[:, 0:width], wg_sems.at[2])
+    attended.start()
+    attended.wait()
+
+    def fill(i, _):
+        for h in range(heads):
+            cols = slice(h * HEAD_DIM, (h + 1) * HEAD_DIM)
+            both = grad_heads[at_rows(i), cols].astype(f32) * dqkv[at_rows(i), cols].astype(f32)
+            delta[i, h : h + 1, :] = jnp.sum(both.T, axis=0, keepdims=True)
+        return 0
+
+    lax.fori_loop(0, n, fill, 0)
+
+    def load_normed(h, m):
+        at = (h * pairs + pairs - 1 - m) % 2
+        return [
+            pltpu.make_async_copy(
+                normed_in.at[at_rows(2 * m + p), :], slots.at[2 * at + p], slot_sems.at[2 * at + p]
+            )
+            for p in range(2)
+        ]
+
+    for copy in load_normed(0, pairs - 1):
+        copy.start()
+
+    key_place = lax.broadcasted_iota(jnp.int32, (block, two), 0)
+    query_place = lax.broadcasted_iota(jnp.int32, (block, two), 1)
+
+    def head_cols(h, k):
+        return pl.ds(pl.multiple_of(k * width + h * HEAD_DIM, HEAD_DIM), HEAD_DIM)
+
+    def sweep(h, service):
+        own_cols = pl.ds(pl.multiple_of(h * HEAD_DIM, HEAD_DIM), HEAD_DIM)
+        slope = slopes[h]
+        dk_acc[...] = jnp.zeros_like(dk_acc)
+        dv_acc[...] = jnp.zeros_like(dv_acc)
+
+        def tile(m, j, single):
+            q_size = block if single else two
+            start = 2 * m + 1 if single else 2 * m
+            at = pl.ds(pl.multiple_of(start * block, block), q_size)
+            q = qkv[at, head_cols(h, 0)]
+            g = grad_heads[at, own_cols]
+            k = qkv[at_rows(j), head_cols(h, 1)]
+            v = qkv[at_rows(j), head_cols(h, 2)]
+            keys, queries = key_place[:, :q_size], query_place[:, :q_size]
+            if single:
+                place = keys.astype(f32) * slope
+                allowed = keys <= queries
+                lse, dlt = logsum[start, h : h + 1, :], delta[start, h : h + 1, :]
+            else:
+                second = (queries >= block).astype(jnp.int32)
+                offset = (j - start) * block
+                place = (keys + offset - second * block).astype(f32) * slope
+                allowed = keys + offset <= queries
+                place += jnp.where(second + start == j, 0.0, apart)
+                lse = jnp.concatenate([logsum[start, h : h + 1, :], logsum[start + 1, h : h + 1, :]], 1)
+                dlt = jnp.concatenate([delta[start, h : h + 1, :], delta[start + 1, h : h + 1, :]], 1)
+            s = dot(k, q, NT) * (SCALE * LOG2E) + place
+            p = jnp.where(allowed, jnp.exp2(s - lse), 0.0)
+            ds = (p * (dot(v, g, NT) - dlt)).astype(bf16)
+            dv_acc[at_rows(j), :] += dot(p.astype(bf16), g)
+            dk_acc[at_rows(j), :] += dot(ds, q)
+            if single:
+                dq_acc[:, block:] += dot(k, ds, TN)
+            else:
+                dq_acc[...] += dot(k, ds, TN)
+
+        def outer(step, _):
+            m = pairs - 1 - step
+            dq_acc[...] = jnp.zeros_like(dq_acc)
+
+            def inner(j, _):
+                service(step, j)
+                tile(m, j, False)
+                return 0
+
+            lax.fori_loop(0, 2 * m + 1, inner, 0)
+            tile(m, 2 * m + 1, True)
+            for copy in load_normed(h, m):
+                copy.wait()
+
+            @pl.when(step + 1 < pairs)
+            def _():
+                for copy in load_normed(h, m - 1):
+                    copy.start()
+
+            if h + 1 < heads:
+                @pl.when(step + 1 == pairs)
+                def _():
+                    for copy in load_normed(h + 1, pairs - 1):
+                        copy.start()
+
+            at = pl.ds(pl.multiple_of(m * two, two), two)
+            dq = (dq_acc[...] * SCALE).T.astype(bf16)
+            dk = (dk_acc[at, :] * SCALE).astype(bf16)
+            dv = dv_acc[at, :].astype(bf16)
+            dqkv[at, head_cols(h, 0)] = dq
+            dqkv[at, head_cols(h, 1)] = dk
+            dqkv[at, head_cols(h, 2)] = dv
+            slot = (h * pairs + step) % 2
+            low = jnp.concatenate([slots[2 * slot], slots[2 * slot + 1]], 0)
+            part = dot(low, jnp.concatenate([dq, dk, dv], 1), TN)
+
+            @pl.when(step == 0)
+            def _():
+                wgrad[...] = part
+
+            @pl.when(step > 0)
+            def _():
+                wgrad[...] += part
+
+            return 0
+
+        lax.fori_loop(0, pairs, outer, 0)
+
+    todo = {}
+
+    def tiles_of():
+        return [(step, j) for step in range(pairs) for j in range(2 * (pairs - 1 - step) + 1)]
+
+    places = [(h, step, j) for h in range(heads) for step, j in tiles_of()]
+    spread_out = len(places) / (n_side + 2.0)
+    for c in range(n_side + 2):
+        at = min(int((c + 0.7) * spread_out), len(places) - 1)
+        todo.setdefault(places[at], []).append(functools.partial(side_step, c))
+    if scatter_inside:
+        for s in range(steps - 1):
+            for scatter, share in ((wide_rs, 0.45 + 0.25 * s), (narrow_rs, 0.72 + 0.2 * s)):
+                def go(scatter=scatter, s=s):
+                    scatter.arrive(s)
+                    scatter.start(s + 1)
+
+                at = min(int(share * len(places)), len(places) - 1)
+                todo.setdefault(places[at], []).append(go)
+
+    def service_of(h):
+        def service(step, j):
+            for (hh, at_step, at_j), actions in todo.items():
+                if hh == h:
+                    @pl.when((step == at_step) & (j == at_j))
+                    def _(actions=actions):
+                        for action in actions:
+                            action()
+
+        return service
+
+    first_sum = DpSum(pay_a, recv_a, sum_a, masks, a_sems, keep_sems.at[0])
+    second_sum = DpSum(pay_b, recv_b, sum_b, masks, b_sems, keep_sems.at[1])
+    sweep(0, service_of(0))
+    pay_a[:, 0 : 3 * HEAD_DIM] = wgrad[...].astype(bf16)
+    first_sum.start()
+    sweep(1, service_of(1))
+    pay_b[...] = wgrad[...].astype(bf16)
+    second_sum.start()
+
+    def load_x(q):
+        return pltpu.make_async_copy(x_in.at[at_rows(n - 1 - q), :], slots.at[q % 2], total_sems.at[0, q])
+
+    def load_hid(q):
+        return pltpu.make_async_copy(grad_hid.at[at_rows(n - 1 - q), :], slots.at[2 + q % 2], total_sems.at[1, q])
+
+    def last_mine(q, who, k):
+        return f_src[q % 2, :, at_cols(who, width)].astype(f32)
+
+    last = HeadSum(width, lambda q: f_src.at[q % 2], last_mine, f_core, lambda q: f_far.at[at_rows(q), :], f_chip, f_sems)
+
+    def last_copy(q):
+        return pltpu.make_async_copy(
+            dqkv.at[at_rows(n - 1 - q), 0:width], total_sum.at[at_rows(n - 1 - q), :], total_sems.at[2, q]
+        )
+
+    load_x(0).start()
+    load_hid(0).start()
+    small[...] = jnp.zeros_like(small)
+    small[0:2, :] = sums_2[...]
+    small[4:5, 0:grad_bias.shape[1]] = grad_bias[...]
+    small[5:6, 0:width] = grad_bias_reduce[...]
+
+    def last_chunk(q, _):
+        load_x(q).wait()
+        load_hid(q).wait()
+
+        @pl.when(q + 1 < n)
+        def _():
+            load_x(q + 1).start()
+            load_hid(q + 1).start()
+
+        at = at_rows(n - 1 - q)
+        gf = dot(dqkv[at, 0:width], wq[...], NT)
+        gf += dot(dqkv[at, width : 2 * width], wk[...], NT)
+        gf += dot(dqkv[at, 2 * width :], wv[...], NT)
+        x = slots[q % 2].astype(f32)
+        centre = x - jnp.sum(x, axis=1, keepdims=True) * (1.0 / features)
+        spread = jnp.sum(centre * centre, axis=1, keepdims=True) * (1.0 / features)
+        scale = lax.rsqrt(spread + eps)
+        centred = centre * scale
+        scaled = gf * gain[...]
+        mean_scaled = jnp.sum(scaled, axis=1, keepdims=True) * (1.0 / features)
+        mean_both = jnp.sum(scaled * centred, axis=1, keepdims=True) * (1.0 / features)
+        back = (scaled - mean_scaled - centred * mean_both) * scale
+        f_src[q % 2] = (back + slots[2 + q % 2].astype(f32)).astype(bf16)
+        last.start(q)
+        small[2:3, :] += jnp.sum(gf * centred, axis=0, keepdims=True)
+        small[3:4, :] += jnp.sum(gf, axis=0, keepdims=True)
+        near = last.middle(q)
+        dk_acc[at_rows(q), :] = near[:, 0:HEAD_DIM]
+        dv_acc[at_rows(q), :] = near[:, HEAD_DIM:]
+        return 0
+
+    half = n // 2
+    lax.fori_loop(0, half, last_chunk, 0)
+    if scatter_inside:
+        wide_rs.arrive(steps - 1)
+        wide_sum[...] = wide[:, at_cols(group, local)].astype(f32)
+    first_sum.advance(0)
+    lax.fori_loop(half, n, last_chunk, 0)
+    if scatter_inside:
+        narrow_rs.arrive(steps - 1)
+        narrow_sum[...] = narrow[:, at_cols(group, local)].astype(f32)
+
+    def small_copy(s):
+        where = {"head": partner(me, masks_of(4)[s])} if s < 2 else {"dp": partner(group, masks[s - 2])}
+        return send_to(small, small_recv.at[s], small_sems.at[0, s], small_sems.at[1, s], **where)
+
+    def small_step(s):
+        small_copy(s).wait()
+        if s < 2:
+            small[0:4, :] += small_recv[s, 0:4, :]
+        else:
+            small[...] += small_recv[s]
+        if s + 1 < 2 + steps:
+            small_copy(s + 1).start()
+
+    def last_finish(q):
+        far = last.finish(q)
+        at = at_rows(n - 1 - q)
+        dqkv[at, 0:HEAD_DIM] = (dk_acc[at_rows(q), :] + far[:, 0:HEAD_DIM]).astype(bf16)
+        dqkv[at, HEAD_DIM:width] = (dv_acc[at_rows(q), :] + far[:, HEAD_DIM:]).astype(bf16)
+        last_copy(q).start()
+
+    small_copy(0).start()
+    for s in range(2 * steps):
+        second_sum.advance(s)
+        if s + 1 < 2 * steps:
+            first_sum.advance(s + 1)
+        if s < n:
+            last_finish(s)
+        if s < 2 + steps:
+            small_step(s)
+    for s in range(2 * steps, max(n, 2 + steps)):
+        if s < n:
+            last_finish(s)
+        if s < 2 + steps:
+            small_step(s)
+    first_sum.settle()
+    second_sum.settle()
+    if scatter_inside:
+        wide_rs.sent()
+        narrow_rs.sent()
+    for c in range(n_side - 2, n_side):
+        side_copy(c).wait()
+    for q in range(n):
+        last_copy(q).wait()
+
+
+def third(
+    kind, qkv, grad_heads, logsum, wq, wk, wv, gain, sums_2, grad_bias, grad_bias_reduce, wide, narrow,
+    a, x, normed, grad_hid, ffn, proj, local, dp_size,
+):
+    rows, width = grad_heads.shape
+    features = x.shape[1]
+    block = SHORT
+    n = rows // block
+    heads = width // HEAD_DIM
+    masks = masks_of(dp_size)
+    inside = local % 128 == 0
+    home = local if inside else 128
+    any_spec = pl.BlockSpec(memory_space=pl.ANY)
+    vmem = pl.BlockSpec(memory_space=pltpu.VMEM)
+    blocks = max(dp_size - 1, 1)
+    n_side = features // block + n
+    cols_a, cols_b = 3 * HEAD_DIM + width, 3 * HEAD_DIM
+    part = features // dp_size
+    recv_blocks = blocks if inside else 1
+
+    def dma(*shape):
+        return pltpu.SemaphoreType.DMA(shape)
+
     return pl.pallas_call(
-        functools.partial(attend_back_kernel, heads),
-        grid=(n,),
-        in_specs=[
-            pl.BlockSpec(memory_space=pltpu.SMEM),
-            pl.BlockSpec(memory_space=pltpu.SMEM),
-            full_spec(qkv.shape),
-            full_spec(grad.shape),
-            full_spec(attended.shape),
-            full_spec(logsum.shape),
+        functools.partial(third_kernel, masks, inside),
+        in_specs=[pl.BlockSpec(memory_space=pltpu.SMEM)] + [vmem] * 12 + [any_spec] * 6,
+        out_specs=[any_spec] * 4 + [vmem] * 3,
+        out_shape=[
+            jax.ShapeDtypeStruct((rows, width), bf16),
+            jax.ShapeDtypeStruct((rows, width), bf16),
+            jax.ShapeDtypeStruct((features, cols_a), bf16),
+            jax.ShapeDtypeStruct((features, cols_b), bf16),
+            jax.ShapeDtypeStruct((features, home), f32),
+            jax.ShapeDtypeStruct((features, home), f32),
+            jax.ShapeDtypeStruct((8, features), f32),
         ],
-        out_specs=pl.BlockSpec((block, 3 * width), lambda j: (j, 0)),
-        out_shape=jax.ShapeDtypeStruct((rows, 3 * width), bf16),
-        scratch_shapes=[pltpu.VMEM((rows, width), f32), pltpu.VMEM((n, heads, block), f32)],
-        compiler_params=pltpu.CompilerParams(vmem_limit_bytes=56 * MIB),
-        cost_estimate=pl.CostEstimate(
-            flops=20 * rows * rows * width, bytes_accessed=rows * width * 20, transcendentals=0
+        scratch_shapes=[
+            pltpu.VMEM((rows, 3 * width), bf16),
+            pltpu.VMEM((rows, HEAD_DIM), f32),
+            pltpu.VMEM((rows, HEAD_DIM), f32),
+            pltpu.VMEM((HEAD_DIM, 2 * block), f32),
+            pltpu.VMEM((n, heads, block), f32),
+            pltpu.VMEM((features, cols_b), f32),
+            pltpu.VMEM((4, block, features), bf16),
+            pltpu.VMEM((features, cols_a), bf16),
+            pltpu.VMEM((features, cols_b), bf16),
+            pltpu.VMEM((blocks, part, cols_a), bf16),
+            pltpu.VMEM((blocks, part, cols_b), bf16),
+            pltpu.VMEM((recv_blocks, features, home), bf16),
+            pltpu.VMEM((recv_blocks, features, home), bf16),
+            pltpu.VMEM((n_side * block, 2 * width), bf16),
+            pltpu.VMEM((3, block, width), bf16),
+            pltpu.VMEM((n_side * block, width), bf16),
+            pltpu.VMEM((3, block, width), f32),
+            pltpu.VMEM((2, 2, block, width), bf16),
+            pltpu.VMEM((2, block, width), bf16),
+            pltpu.VMEM((2, block, features), bf16),
+            pltpu.VMEM((rows, 2 * width), bf16),
+            pltpu.VMEM((rows, width), bf16),
+            pltpu.VMEM((rows, width), bf16),
+            pltpu.VMEM((2 + len(masks), 8, features), f32),
+            dma(3),
+            dma(6, n_side),
+            dma(2, n_side),
+            dma(n_side),
+            dma(6, n),
+            dma(4, blocks),
+            dma(4, blocks),
+            dma(2, blocks),
+            dma(2, blocks),
+            dma(4),
+            dma(2),
+            dma(2, 2 + len(masks)),
+            dma(3, n),
+        ],
+        compiler_params=pltpu.CompilerParams(
+            vmem_limit_bytes=63 * MIB, collective_id=2, has_side_effects=True
         ),
-    )(kind, slopes, qkv, grad, attended, logsum)
-
-
-def finish_kernel(x_in, grad_qkv, weight, gain, grad_hid, last, sums):
-    step = pl.program_id(0)
-    features = x_in.shape[1]
-    gf = dot(grad_qkv[...], weight[...], NT)
-    x = x_in[...].astype(f32)
-    centre = x - jnp.sum(x, axis=1, keepdims=True) * (1.0 / features)
-    spread = jnp.sum(centre * centre, axis=1, keepdims=True) * (1.0 / features)
-    scale = lax.rsqrt(spread + eps)
-    centred = centre * scale
-    scaled = gf * gain[...]
-    mean_scaled = jnp.sum(scaled, axis=1, keepdims=True) * (1.0 / features)
-    mean_both = jnp.sum(scaled * centred, axis=1, keepdims=True) * (1.0 / features)
-    back = (scaled - mean_scaled - centred * mean_both) * scale
-    last[...] = (back + grad_hid[...].astype(f32)).astype(bf16)
-
-    @pl.when(step == 0)
-    def _():
-        sums[...] = jnp.zeros_like(sums)
-
-    sums[0:1, :] += jnp.sum(gf * centred, axis=0, keepdims=True)
-    sums[1:2, :] += jnp.sum(gf, axis=0, keepdims=True)
-
-
-def finish(x, grad_qkv, weight, gain, grad_hid):
-    rows, features = x.shape
-    block = SHORT
-
-    def rows_of(columns):
-        return pl.BlockSpec((block, columns), lambda i: (i, 0))
-
-    return pl.pallas_call(
-        finish_kernel,
-        grid=(rows // block,),
-        in_specs=[rows_of(features), rows_of(grad_qkv.shape[1]), full_spec(weight.shape), full_spec(gain.shape), rows_of(features)],
-        out_specs=[rows_of(features), full_spec((2, features))],
-        out_shape=[jax.ShapeDtypeStruct((rows, features), bf16), jax.ShapeDtypeStruct((2, features), f32)],
-        compiler_params=pltpu.CompilerParams(vmem_limit_bytes=48 * MIB),
-        cost_estimate=pl.CostEstimate(
-            flops=2 * rows * features * grad_qkv.shape[1], bytes_accessed=rows * features * 8, transcendentals=0
-        ),
-    )(x, grad_qkv, weight, gain, grad_hid)
-
-
-def flip(value, axis, size, mask):
-    return lax.ppermute(value, axis, [(k, k ^ mask) for k in range(size)])
-
-
-def reorder(value, rank, axis=0, size=4):
-    width = value.shape[axis] // size
-    return jnp.concatenate(
-        [lax.dynamic_slice_in_dim(value, (rank ^ k) * width, width, axis) for k in range(size)], axis
+    )(
+        kind, qkv, grad_heads, logsum, wq, wk, wv, gain, sums_2, grad_bias, grad_bias_reduce, wide, narrow,
+        a, x, normed, grad_hid, ffn, proj,
     )
-
-
-def scatter_dp(blocks, size):
-    held = {k: blocks[k].astype(f32) for k in range(size)}
-    for mask in masks_of(size):
-        mine = [k for k in sorted(held) if not k & mask]
-        got = flip(jnp.stack([held[k ^ mask] for k in mine]).astype(bf16), "dp", size, mask)
-        held = {k: held[k] + got[p].astype(f32) for p, k in enumerate(mine)}
-    return held[0]
-
-
-def gather_dp(value, size):
-    blocks = {0: value}
-    for mask in reversed(masks_of(size)):
-        order = sorted(blocks)
-        got = flip(jnp.stack([blocks[k] for k in order]), "dp", size, mask)
-        for k, at in enumerate(order):
-            blocks[at ^ mask] = got[k]
-    return [blocks[k] for k in range(size)]
-
-
-def scatter_head(value, rank):
-    width = value.shape[1] // 4
-
-    def cols(k):
-        return lax.dynamic_slice_in_dim(value, (rank ^ k) * width, width, 1)
-
-    got = flip(jnp.concatenate([cols(1), cols(3)], 1), "head", 4, 1).astype(f32)
-    far = cols(2).astype(f32) + got[:, width:]
-    near = cols(0).astype(f32) + got[:, :width]
-    return near + flip(far.astype(bf16), "head", 4, 2).astype(f32)
-
-
-def sum_dp(value, dp_size):
-    for mask in masks_of(dp_size):
-        value = value + flip(value, "dp", dp_size, mask)
-    return value
-
-
-def sum_small(value, dp_size):
-    for mask in (1, 2):
-        value = value + flip(value, "head", 4, mask)
-    return sum_dp(value, dp_size)
-
-
-def all_sum_dp(value, dp_size):
-    me = lax.axis_index("dp")
-    parts = reorder(value, me, 0, dp_size)
-    r = value.shape[0] // dp_size
-    own = scatter_dp([parts[k * r : (k + 1) * r] for k in range(dp_size)], dp_size)
-    return reorder(jnp.concatenate(gather_dp(own.astype(bf16), dp_size), 0), me, 0, dp_size).astype(f32)
 
 
 def shards(
@@ -891,46 +1287,35 @@
     bias_reduce,
     grad_out,
 ):
-    rank = lax.axis_index("head")
     group = lax.axis_index("dp")
-    rows, width = layer_in.shape
-    features = 4 * width
-    heads_here = w_query.shape[1] // HEAD_DIM
-    head_index = rank * heads_here + jnp.arange(heads_here)
-    slopes = jnp.exp2(-8.0 * (head_index.astype(f32) + 1.0) / HEADS)
-    gain_1, shift_1 = attn_gain[None], attn_shift[None]
-    x, a, normed_attn, qkv, proj, expand, reduce, bias, logsum = first(
-        bucket, layer_in, w_query, w_key, w_value, gain_1, shift_1, bias_expand, w_proj, w_expand, w_reduce, dp_size
+    width = layer_in.shape[1]
+    local = w_expand.shape[1]
+    gain_1 = attn_gain[None]
+    x, a, normed, qkv, proj, expand, reduce, bias, logsum = first(
+        bucket, layer_in, w_query, w_key, w_value, gain_1, attn_shift[None], bias_expand, w_proj, w_expand, w_reduce, dp_size
     )
     (
-        grad_heads, grad_hid, ffn_partial, hid_own, grad_wide, grad_narrow, proj_part, sums_2, grad_bias, grad_bias_reduce,
+        grad_heads, grad_hid, ffn, hid_own, grad_wide, grad_narrow, proj_part, sums_2, grad_bias, grad_bias_reduce,
     ) = second(
         x, a, grad_out, layer_in, proj, expand, reduce, ffn_gain[None], ffn_shift[None], bias
     )
-    layer_out = hid_own + bias_reduce + scatter_head(ffn_partial, rank)
-    local = w_expand.shape[1]
-
-    def columns_home(value):
-        value = reorder(value, group, 1, dp_size)
-        return scatter_dp([value[:, k * local : (k + 1) * local] for k in range(dp_size)], dp_size)
-
-    grad_expand = columns_home(grad_wide)
-    grad_reduce = columns_home(grad_narrow)
-    grad_bias_expand = columns_home(grad_bias)
-    grad_proj = all_sum_dp(scatter_head(proj_part.T, rank).T, dp_size)
-
-    attended = lax.dynamic_slice_in_dim(a, rank * width, width, 1)
-    grad_qkv = attend_back(qkv, grad_heads, attended, logsum, slopes, bucket)
-    weight_grad = all_sum_dp(dot(normed_attn, grad_qkv, TN), dp_size)
-    grad_query, grad_key, grad_value = (weight_grad[:, k * width : (k + 1) * width] for k in range(3))
-    w_qkv = jnp.concatenate([w_query, w_key, w_value], 1)
-    last, sums_1 = finish(x, grad_qkv, w_qkv, gain_1, grad_hid)
-    grad_in = scatter_head(last, rank)
-    small = sum_small(jnp.concatenate([sums_2, sums_1], 0), dp_size)
-    grad_bias_reduce = sum_dp(grad_bias_reduce[0], dp_size)
+    ffn_sum, grad_in, sum_a, sum_b, grad_expand, grad_reduce, small = third(
+        bucket, qkv, grad_heads, logsum, w_query, w_key, w_value, gain_1, sums_2, grad_bias, grad_bias_reduce,
+        grad_wide, grad_narrow, a, x, normed, grad_hid, ffn, proj_part, local, dp_size,
+    )
+    if local % 128:
+        grad_expand = lax.psum_scatter(grad_wide.astype(f32), "dp", scatter_dimension=1, tiled=True)
+        grad_reduce = lax.psum_scatter(grad_narrow.astype(f32), "dp", scatter_dimension=1, tiled=True)
+    layer_out = hid_own + bias_reduce + ffn_sum.astype(f32)
+    head = HEAD_DIM
+    grad_query, grad_key, grad_value = (
+        jnp.concatenate([sum_a[:, k * head : (k + 1) * head], sum_b[:, k * head : (k + 1) * head]], 1).astype(f32)
+        for k in range(3)
+    )
+    grad_proj = sum_a[:, 3 * head :].astype(f32).T
     return (
         layer_out,
-        grad_in,
+        grad_in.astype(f32),
         grad_query,
         grad_key,
         grad_value,
@@ -940,9 +1325,9 @@
         small[0],
         small[1],
         grad_expand,
-        grad_bias_expand,
+        lax.dynamic_slice(small, (4, group * local), (1, local)),
         grad_reduce,
-        grad_bias_reduce,
+        small[5, :width],
     )
 
 

time: 494 us -> 376 us (0.76)
  waiting for transfers between devices: 141 us -> 0 us
  Pallas kernels: 224 us -> 352 us
  starting transfers between devices: 66.1 us -> 0 us
  other arithmetic: 30.4 us -> 9.48 us
  local copies, waits for them, and re-layouts: 17.9 us -> 6.16 us
  matrix products: 7.51 us -> 0 us
    ppermute x35 -> x0, waiting for transfers between devices: 141 us -> none  [flip(): return lax.ppermute(value, axis, [(k, k ^ mask) for k in range(size)])]
    pallas_call x2 -> x1, Pallas kernels: 32.4 us -> 161 us  [third(): pl.pallas_call(functools.partial(third_kernel, masks, inside), in_specs=[...]
    ppermute x35 -> x0, starting transfers between devices: 66.1 us -> none  [flip(): return lax.ppermute(value, axis, [(k, k ^ mask) for k in range(size)])]
    add x14 -> x1, other arithmetic: 10.8 us -> 1.97 us  [shards(): layer_out = hid_own + bias_reduce + ffn_sum.astype(f32)]
    dynamic_slice x4 -> x1, local copies, waits for them, and re-layouts: 8.15 us -> 0.58 us  [shards(): lax.dynamic_slice(small, (4, group * local), (1, local))]
    dot_general x1 -> x0, matrix products: 7.51 us -> none  [dot(): return lax.dot_general(left, right, dims, preferred_element_type=f32)]
    another operation x19 -> x0, other arithmetic: 6.3 us -> none  [the longest x15 6.1 us: scatter_dp(): jnp.stack([held[k ^ mask] for k in mine]).astype(bf16)]
  transfers between devices with their start and end apart: 35 -> 0, of which waited for: 18 -> 0; matrix products, arithmetic and copies ran while one was open for 10% -> 0% of each run, Pallas kernels for 7% -> 0%
where the time goes in v3:
time: 376 us; the launch traced here: 370 us
  Pallas kernels  352 us (94%)
  other arithmetic  9.48 us (3%)
  local copies, waits for them, and re-layouts  6.16 us (2%)
    pallas_call x1, Pallas kernels, third(): pl.pallas_call(functools.partial(third_kernel, masks, inside), in_specs=[...  161 us
    pallas_call x1, Pallas kernels, second(): pl.pallas_call(second_kernel, in_specs=[any_spec] * 2 + [vmem] * 8, out_s...  98.4 us
    pallas_call x1, Pallas kernels, first(): pl.pallas_call(functools.partial(first_kernel, masks, gather), in_specs=[...  92.7 us

profile of v3, /device:TPU:0, one launch (start us, length us, event | category | flops | bytes accessed | tf_op | source)
XLA Modules:
  0.0 369.8 jit_solution(2887664383480741822)
XLA Ops:
  1.3 92.7 %shard_map.254 = (bf16[3072,1024]{1,0:T(8,128)(2,1)}, bf16[3072,1024]{1,0:T(8,128)(2,1)}, bf16[3072,1024]{1,0:T(8,128)(2,1)}, bf16[3072,768]{1,0:T(8,128)(2,1)},...) custom-call(s32[1]{0:T(128)S(6)} %copy.32.kind, ...), custom_call_target="tpu_custom_call" | custom-call | tf_op jit(solution)/shard_map/pallas_call | solution.py:379
  94.0 1.3 slice_convert_fusion.bias
  95.3 98.4 %shard_map.255 = (bf16[3072,256]{1,0:T(8,128)(2,1)}, bf16[3072,1024]{1,0:T(8,128)(2,1)}, bf16[3072,1024]{1,0:T(8,128)(2,1)}, f32[3072,256]{1,0:T(8,128)}, bf16[1...) custom-call(bf16[3072,1024]{1,0:T(8,128)(2,1)} %get-tuple-element.40, ...), custom_call_target="tpu_custom_call" | custom-call | tf_op jit(solution)/shard_map/pallas_call | solution.py:638
  193.8 161.2 %shard_map.256 = (bf16[3072,256]{1,0:T(8,128)(2,1)}, bf16[3072,256]{1,0:T(8,128)(2,1)}, bf16[1024,640]{1,0:T(8,128)(2,1)}, bf16[1024,384]{1,0:T(8,128)(2,1)}, f3...) custom-call(s32[1]{0:T(128)S(6)} %copy.32.kind, bf16[3072,768]{1,0:T(8,128)(2,1)} %get-tuple-element.47.qkv, ...), custom_call_target="tpu_custom_call" | custom-call | tf_op jit(solution)/shard_map/pallas_call | solution.py:1211
  355.0 1.5 fusion
  356.5 0.0 copy-start
  356.5 0.0 copy-start.2
  356.5 0.0 copy-start.6
  356.5 1.0 maximum_convert_fusion.2
  357.6 1.0 maximum_convert_fusion.1
  358.6 1.0 maximum_convert_fusion
  359.7 0.0 copy-done
  359.7 0.0 copy-done.2
  359.7 0.0 copy-done.6
  359.7 0.0 copy-start.1
  359.7 2.0 convert_add_fusion
  361.6 0.0 copy-done.1
  361.6 0.0 copy-start.5
  361.6 0.0 copy-start.4
  361.6 1.9 convert_element_type.21
  363.6 0.0 copy-start.3
  363.6 1.2 convert_bitcast_fusion
  364.7 1.3 copy.29
  366.0 0.0 copy-done.5
  366.1 0.6 fusion.2
  366.7 0.6 constant_dynamic-slice_fusion
  367.2 0.6 slice.51
  367.8 0.0 copy-done.4
  367.8 0.8 copy.33
  368.6 0.0 copy-done.3
  368.6 0.8 copy.34
Async XLA Ops:
  356.5 3.2 copy-start
  356.5 3.1 copy-start.2
  356.5 3.1 copy-start.6
  359.7 2.0 copy-start.1
  361.6 4.4 %copy-start.5 = (f32[8,1024]{1,0:T(8,128)S(1)}, f32[8,1024]{1,0:T(8,128)}, u32[]{:S(2)}) copy-start(f32[8,1024]{1,0:T(8,128)} %get-tuple-element.63) | copy-start | bytes 98308
  361.6 6.2 %copy-start.4 = (f32[1024,128]{1,0:T(8,128)S(1)}, f32[1024,128]{1,0:T(8,128)}, u32[]{:S(2)}) copy-start(f32[1024,128]{1,0:T(8,128)} %get-tuple-element.117) | copy-start | bytes 1572868
  363.6 5.0 %copy-start.3 = (f32[1024,128]{1,0:T(8,128)S(1)}, f32[1024,128]{1,0:T(8,128)}, u32[]{:S(2)}) copy-start(f32[1024,128]{1,0:T(8,128)} %get-tuple-element.119) | copy-start | bytes 1572868

commit v4 on v3

--- a/solution.py
+++ b/solution.py
@@ -108,10 +108,9 @@
         self.copy(r, self.slot(r, self.chip), self.chip, 2, head=self.core).wait_send()
 
 
-class DpGather:
-    def __init__(self, own, full, width, masks, send, recv):
-        self.own, self.full, self.width = own, full, width
-        self.masks = list(reversed(masks))
+class DpSpread:
+    def __init__(self, own, slot_of, masks, send, recv):
+        self.own, self.slot_of, self.masks = own, slot_of, masks
         self.group = lax.axis_index("dp")
         self.send, self.recv = send, recv
         held, self.plan, at = [0], [], 0
@@ -122,10 +121,10 @@
 
     def block(self, k):
         who = self.group
-        for mask in masks_of(1 << len(self.masks)):
+        for mask in self.masks:
             if k & mask:
                 who = partner(who, mask)
-        return self.full.at[:, at_cols(who, self.width)]
+        return self.slot_of(who)
 
     def copies(self, step, there):
         mask, items = self.plan[step]
@@ -169,7 +168,7 @@
     kind, layer_in, wq, wk, wv, gain, shift, bias_expand, w_proj, w_expand, w_reduce,
     x_out, a_out, normed_out, qkv_out, proj_out, expand_out, reduce_out, bias_out, logsum,
     x_buf, normed_buf, qkv_buf, a_buf, bias_buf, total, x_sems, a_sems, p_sems, local_sems, copy_sems,
-    e_send, e_recv, r_send, r_recv, b_send, b_recv,
+    e_send, e_recv, r_send, r_recv, b_send, b_recv, q_send, q_recv,
 ):
     rows, width = layer_in.shape
     features = 4 * width
@@ -186,11 +185,29 @@
     def p_copy(src, owner, k, **where):
         return send_to(src, proj_out.at[at_cols(owner, width), :], p_sems.at[2 * k], p_sems.at[2 * k + 1], **where)
 
+    piece = width // (1 << len(masks))
+
+    def p_rows(owner, k):
+        return proj_out.at[pl.ds(pl.multiple_of(owner * width + k * piece, piece), piece), :]
+
+    def p_piece(owner, to):
+        return send_to(
+            w_proj.at[pl.ds(pl.multiple_of(group * piece, piece), piece), :], p_rows(owner, group),
+            p_sems.at[0], p_sems.at[1], head=to,
+        )
+
+    far_rows = DpSpread(p_rows(chip, group), lambda k: p_rows(chip, k), masks[::-1], q_send, q_recv)
+
     if gather:
-        expand = DpGather(w_expand, expand_out, w_expand.shape[1], masks, e_send, e_recv)
-        reduce = DpGather(w_reduce, reduce_out, w_reduce.shape[1], masks, r_send, r_recv)
         bias_buf[...] = jnp.broadcast_to(bias_expand[...], bias_buf.shape)
-        bias = DpGather(bias_buf, bias_out, w_expand.shape[1], masks, b_send, b_recv)
+
+        def columns_of(ref):
+            return lambda k: ref.at[:, at_cols(k, w_expand.shape[1])]
+
+        far_first, near_first = masks[::-1], masks[:1] + masks[1:][::-1]
+        expand = DpSpread(w_expand, columns_of(expand_out), far_first, e_send, e_recv)
+        bias = DpSpread(bias_buf, columns_of(bias_out), far_first, b_send, b_recv)
+        reduce = DpSpread(w_reduce, columns_of(reduce_out), near_first, r_send, r_recv)
         expand.start(0)
         bias.start(0)
         reduce.start(0)
@@ -199,8 +216,12 @@
         x_buf[at_rows(r), at_cols(me, width)] = layer_in[at_rows(r), :].astype(bf16)
         x_gather.start(r)
 
+    if gather:
+        p_piece(me, chip).start()
+        p_copy(w_proj, me, 1, head=core).start()
     own_chunk(0)
     own_chunk(1)
+    own_chunk(2)
     keeps = [pltpu.make_async_copy(w_proj, proj_out.at[at_cols(me, width), :], local_sems.at[0])]
     if gather:
         own_cols = at_cols(group, w_expand.shape[1])
@@ -291,25 +312,36 @@
         def _():
             x_gather.forward(r)
 
-            @pl.when(r + 2 < n)
+            @pl.when(r + 3 < n)
             def _():
-                own_chunk(r + 2)
-
-            @pl.when(r + 2 == n)
+                own_chunk(r + 3)
+
+            if not gather:
+                @pl.when(r + 2 == n)
+                def _():
+                    p_copy(w_proj, me, 0, head=chip).start()
+                    p_copy(w_proj, me, 1, head=core).start()
+
+        if gather:
+            @pl.when(r == 2)
             def _():
-                p_copy(w_proj, me, 0, head=chip).start()
-                p_copy(w_proj, me, 1, head=core).start()
-
-        if gather:
+                p_piece(chip, chip).wait_recv()
+                far_rows.start(0)
+
             for s in range(1, steps):
-                @pl.when(r == min(2 * s, n - 1))
+                @pl.when(r == min(s + 3, n))
+                def _(s=s):
+                    far_rows.arrive(s - 1)
+                    far_rows.start(s)
+
+                @pl.when(r == min(2 * s + 1, n - 1))
                 def _(s=s):
                     expand.arrive(s - 1)
                     bias.arrive(s - 1)
                     expand.start(s)
                     bias.start(s)
 
-                @pl.when(r == min(2 * s + 1, n))
+                @pl.when(r == min(4 * s - 3, n))
                 def _(s=s):
                     reduce.arrive(s - 1)
                     reduce.start(s)
@@ -322,7 +354,10 @@
 
     lax.fori_loop(0, n + 1, body, 0)
 
-    p_copy(w_proj, chip, 0, head=chip).wait_recv()
+    if gather:
+        far_rows.arrive(steps - 1)
+    else:
+        p_copy(w_proj, chip, 0, head=chip).wait_recv()
     p_forward = p_copy(proj_out.at[at_cols(chip, width), :], chip, 2, head=core)
     p_forward.start()
 
@@ -349,7 +384,11 @@
     lax.fori_loop(0, n, settle, 0)
     p_copy(w_proj, core, 1, head=core).wait_recv()
     p_copy(w_proj, partner(core, 2), 2, head=core).wait_recv()
-    p_copy(w_proj, me, 0, head=chip).wait_send()
+    if gather:
+        p_piece(me, chip).wait_send()
+        far_rows.sent()
+    else:
+        p_copy(w_proj, me, 0, head=chip).wait_send()
     p_copy(w_proj, me, 1, head=core).wait_send()
     p_forward.wait_send()
     for keep in keeps:
@@ -371,7 +410,7 @@
     heads = width // HEAD_DIM
     masks = masks_of(dp_size)
     local = w_expand.shape[1]
-    gather = local % 128 == 0
+    gather = local % 128 == 0 and (width // dp_size) % 16 == 0
     units = local * dp_size if gather else 128
     any_spec = pl.BlockSpec(memory_space=pl.ANY)
     vmem = pl.BlockSpec(memory_space=pltpu.VMEM)
@@ -403,13 +442,8 @@
             pltpu.SemaphoreType.DMA((6,)),
             pltpu.SemaphoreType.DMA((4,)),
             pltpu.SemaphoreType.DMA((4, n)),
-            pltpu.SemaphoreType.DMA((blocks,)),
-            pltpu.SemaphoreType.DMA((blocks,)),
-            pltpu.SemaphoreType.DMA((blocks,)),
-            pltpu.SemaphoreType.DMA((blocks,)),
-            pltpu.SemaphoreType.DMA((blocks,)),
-            pltpu.SemaphoreType.DMA((blocks,)),
-        ],
+        ]
+        + [pltpu.SemaphoreType.DMA((blocks,))] * 8,
         compiler_params=pltpu.CompilerParams(
             vmem_limit_bytes=56 * MIB, collective_id=0, has_side_effects=True
         ),
@@ -476,10 +510,10 @@
 
 
 def second_kernel(
-    x_in, a_in, grad_out, layer_in, w_proj, w_expand, w_reduce, gain, shift, bias,
+    x_in, a_in, layer_in, w_proj_in, w_expand_in, w_reduce_in, grad_out, gain, shift, bias,
     grad_heads, grad_hid_out, ffn_out, hid_own, wide_out, narrow_out, proj_out, sums, grad_bias, grad_bias_reduce,
     g_buf, x_buf, a_buf, hid_buf, own_buf, ffn_buf, gh_buf, from_core, far_buf, near_buf, from_chip, wide, narrow, proj,
-    g_sems, s_sems, copy_sems, final_sems,
+    w_proj, w_expand, w_reduce, in_buf, g_sems, s_sems, copy_sems, final_sems, load_sems,
 ):
     rows, width = layer_in.shape
     features = 4 * width
@@ -497,6 +531,16 @@
         g_gather.start(r)
         return chunk
 
+    loads = [
+        pltpu.make_async_copy(src, dst, load_sems.at[k])
+        for k, (src, dst) in enumerate(
+            ((w_proj_in, w_proj), (w_expand_in, w_expand), (w_reduce_in, w_reduce))
+        )
+    ]
+
+    def load_in(r):
+        return pltpu.make_async_copy(layer_in.at[at_rows(r), :], in_buf.at[r % 2], copy_sems.at[5, r])
+
     def load_x(r):
         return pltpu.make_async_copy(x_in.at[at_rows(r), :], x_buf.at[r % 2], copy_sems.at[0, r])
 
@@ -520,8 +564,12 @@
 
     own_chunk(0)
     own_chunk(1)
+    load_a(0).start()
+    loads[0].start()
     load_x(0).start()
-    load_a(0).start()
+    load_in(0).start()
+    loads[1].start()
+    loads[2].start()
     wide[...] = jnp.zeros_like(wide)
     narrow[...] = jnp.zeros_like(narrow)
     proj[...] = jnp.zeros_like(proj)
@@ -538,11 +586,17 @@
 
         load_x(r).wait()
         load_a(r).wait()
+        load_in(r).wait()
+
+        @pl.when(r == 0)
+        def _():
+            loads[0].wait()
 
         @pl.when(r + 1 < n)
         def _():
             load_x(r + 1).start()
             load_a(r + 1).start()
+            load_in(r + 1).start()
 
         @pl.when(r >= 2)
         def _():
@@ -554,13 +608,19 @@
         a = a_buf[slot]
         attn = dot(a, w_proj[...])
         hidden = attn + x_buf[slot].astype(f32)
-        own_buf[slot] = dot(a, w_proj[:, at_cols(me, width)]) + layer_in[at_rows(r), :]
+        own_buf[slot] = dot(a, w_proj[:, at_cols(me, width)]) + in_buf[slot]
         store_own(r).start()
         centre = hidden - jnp.sum(hidden, axis=1, keepdims=True) * (1.0 / features)
         spread = jnp.sum(centre * centre, axis=1, keepdims=True) * (1.0 / features)
         scale = lax.rsqrt(spread + eps)
         centred = centre * scale
         low = (centred * gain[...] + shift[...]).astype(bf16)
+
+        @pl.when(r == 0)
+        def _():
+            loads[1].wait()
+            loads[2].wait()
+
         z = dot(low, w_expand[...]) + bias[...]
         z2 = z * z
         t = jnp.tanh(z * (GELU_C + (GELU_C * 0.044715) * z2))
@@ -587,8 +647,8 @@
         ffn_buf[slot] = dot(activated, w_reduce[...], NT).astype(bf16)
         store_ffn(r).start()
         wide[...] += dot(low, gp_low, TN)
+        scatter.middle(r)
         narrow[...] += dot(g, activated, TN)
-        scatter.middle(r)
         proj[...] += dot(back_low, a, TN)
 
         @pl.when(r >= 1)
@@ -637,7 +697,7 @@
     vmem = pl.BlockSpec(memory_space=pltpu.VMEM)
     return pl.pallas_call(
         second_kernel,
-        in_specs=[any_spec] * 2 + [vmem] * 8,
+        in_specs=[any_spec] * 6 + [vmem] * 4,
         out_specs=[vmem] + [any_spec] * 6 + [vmem] * 3,
         out_shape=[
             jax.ShapeDtypeStruct((rows, width), bf16),
@@ -666,20 +726,26 @@
             pltpu.VMEM((features, units), f32),
             pltpu.VMEM((features, units), f32),
             pltpu.VMEM((features, features), f32),
+            pltpu.VMEM((features, features), bf16),
+            pltpu.VMEM((features, units), bf16),
+            pltpu.VMEM((features, units), bf16),
+            pltpu.VMEM((2, block, width), f32),
             pltpu.SemaphoreType.DMA((6, n)),
             pltpu.SemaphoreType.DMA((6, n)),
-            pltpu.SemaphoreType.DMA((5, n)),
+            pltpu.SemaphoreType.DMA((6, n)),
             pltpu.SemaphoreType.DMA((3, 2)),
+            pltpu.SemaphoreType.DMA((3,)),
         ],
         compiler_params=pltpu.CompilerParams(
             vmem_limit_bytes=62 * MIB, collective_id=1, has_side_effects=True
         ),
-    )(x, a, grad_out, layer_in, w_proj, w_expand, w_reduce, gain, shift, bias)
+    )(x, a, layer_in, w_proj, w_expand, w_reduce, grad_out, gain, shift, bias)
 
 
 class DpScatter:
-    def __init__(self, part, recv_buf, masks, send, recv):
+    def __init__(self, part, recv_buf, masks, send, recv, first_part=None):
         self.part, self.recv_buf, self.masks = part, recv_buf, masks
+        self.first_part = first_part or part
         self.group = lax.axis_index("dp")
         self.send, self.recv = send, recv
         size = 1 << len(masks)
@@ -691,16 +757,17 @@
             at += len(mine)
             left = mine
 
-    def where(self, k):
+    def where(self, k, part):
         who = self.group
         for mask in self.masks:
             if k & mask:
                 who = partner(who, mask)
-        return self.part(who)
+        return part(who)
 
     def copy(self, mask, k, slot):
+        part = self.first_part if mask == self.masks[0] else self.part
         return send_to(
-            self.where(k ^ mask), self.recv_buf.at[slot], self.send.at[slot], self.recv.at[slot],
+            self.where(k ^ mask, part), self.recv_buf.at[slot], self.send.at[slot], self.recv.at[slot],
             dp=partner(self.group, mask),
         )
 
@@ -713,59 +780,13 @@
         mask, items = self.plan[step]
         for k, slot in items:
             self.copy(mask, k, slot).wait_recv()
-            ref = self.where(k)
+            ref = self.where(k, self.part)
             ref[...] = (ref[...].astype(f32) + self.recv_buf[slot].astype(f32)).astype(bf16)
 
     def sent(self):
         for mask, items in self.plan:
             for k, slot in items:
                 self.copy(mask, k, slot).wait_send()
-
-
-class DpSpread:
-    def __init__(self, own, slot_of, masks, send, recv):
-        self.own, self.slot_of = own, slot_of
-        self.masks = list(reversed(masks))
-        self.group = lax.axis_index("dp")
-        self.send, self.recv = send, recv
-        held, self.plan, at = [0], [], 0
-        for mask in self.masks:
-            self.plan.append((mask, [(k, at + p) for p, k in enumerate(held)]))
-            at += len(held)
-            held = held + [k ^ mask for k in held]
-
-    def block(self, k):
-        who = self.group
-        for mask in self.masks:
-            if k & mask:
-                who = partner(who, mask)
-        return self.slot_of(who)
-
-    def copies(self, step, there):
-        mask, items = self.plan[step]
-        out = []
-        for k, sem in items:
-            if there:
-                src, at = (self.own if k == 0 else self.block(k)), self.block(k)
-            else:
-                src = at = self.block(k ^ mask)
-            out.append(
-                send_to(src, at, self.send.at[sem], self.recv.at[sem], dp=partner(self.group, mask))
-            )
-        return out
-
-    def start(self, step):
-        for copy in self.copies(step, True):
-            copy.start()
-
-    def arrive(self, step):
-        for copy in self.copies(step, False):
-            copy.wait_recv()
-
-    def sent(self):
-        for step in range(len(self.plan)):
-            for copy in self.copies(step, True):
-                copy.wait_send()
 
 
 class DpSum:
@@ -777,7 +798,9 @@
         me = lax.axis_index("dp")
         own = buf.at[at_rows(me, rows), :]
         self.keep = pltpu.make_async_copy(own, out.at[at_rows(me, rows), :], keep_sem)
-        self.spread = DpSpread(own, lambda k: out.at[at_rows(k, rows), :], masks, sems.at[2], sems.at[3])
+        self.spread = DpSpread(
+            own, lambda k: out.at[at_rows(k, rows), :], masks[::-1], sems.at[2], sems.at[3]
+        )
 
     def start(self):
         self.scatter.start(0)
@@ -843,12 +866,13 @@
 
 def third_kernel(
     masks, scatter_inside,
-    kind, qkv, grad_heads, logsum, wq, wk, wv, gain, sums_2, grad_bias, grad_bias_reduce, wide, narrow,
-    a_in, x_in, normed_in, grad_hid, ffn, proj,
-    ffn_sum, total_sum, sum_a, sum_b, wide_sum, narrow_sum, small,
-    dqkv, dk_acc, dv_acc, dq_acc, delta, wgrad, slots, pay_a, pay_b, recv_a, recv_b, recv_w, recv_n,
+    kind, qkv, grad_heads, logsum, wq, wk, wv, gain, sums_2, grad_bias, grad_bias_reduce,
+    wide_in, narrow_in, a_in, x_in, normed_in, grad_hid, ffn, proj,
+    ffn_sum, total_sum, sum_p, sum_a, sum_b, wide_sum, narrow_sum, small,
+    dqkv, dk_acc, dv_acc, dq_acc, delta, wgrad, slots, wide, narrow, pay_p, pay_a, pay_b,
+    recv_p, recv_a, recv_b, recv_w, recv_n,
     s_core, s_far, s_chip, s_near, s_mine, s_out, f_src, f_core, f_far, f_chip, small_recv,
-    wg_sems, s_sems, mine_sems, out_sems, f_sems, a_sems, b_sems, w_sems, n_sems, slot_sems, keep_sems, small_sems, total_sems,
+    wg_sems, s_sems, mine_sems, out_sems, f_sems, p_sems, a_sems, b_sems, w_sems, n_sems, slot_sems, keep_sems, small_sems, total_sems,
 ):
     rows = qkv.shape[0]
     width = grad_heads.shape[1]
@@ -861,12 +885,40 @@
     steps = len(masks)
     greet(masks)
 
+    agenda = []
+
+    def due(time, action, *args):
+        agenda.append((time, len(agenda), functools.partial(action, *args)))
+
+    turned = masks[1:2] + masks[:1] + masks[2:]
+
     if scatter_inside:
         local = wide_sum.shape[1]
-        wide_rs = DpScatter(lambda k: wide.at[:, at_cols(k, local)], recv_w, masks, w_sems.at[0], w_sems.at[1])
-        narrow_rs = DpScatter(lambda k: narrow.at[:, at_cols(k, local)], recv_n, masks, n_sems.at[0], n_sems.at[1])
+
+        def columns_of(ref):
+            return lambda k: ref.at[:, at_cols(k, local)]
+
+        wide_rs = DpScatter(columns_of(wide), recv_w, masks, w_sems.at[0], w_sems.at[1], columns_of(wide_in))
+        narrow_rs = DpScatter(columns_of(narrow), recv_n, turned, n_sems.at[0], n_sems.at[1], columns_of(narrow_in))
         wide_rs.start(0)
         narrow_rs.start(0)
+        loads = [
+            pltpu.make_async_copy(wide_in, wide, keep_sems.at[3]),
+            pltpu.make_async_copy(narrow_in, narrow, keep_sems.at[4]),
+        ]
+
+        def scatter_step(scatter, load, out, s):
+            if s == 0:
+                load.wait()
+            scatter.arrive(s)
+            if s + 1 < steps:
+                scatter.start(s + 1)
+            else:
+                out[...] = scatter.part(group)[...].astype(f32)
+
+        for s in range(steps):
+            due((63, 70.5, 85)[min(s, 2)] + max(s - 2, 0), scatter_step, wide_rs, loads[0], wide_sum, s)
+            due((28.5, 51.5, 66)[min(s, 2)] + max(s - 2, 0), scatter_step, narrow_rs, loads[1], narrow_sum, s)
 
     n_proj = features // block
     n_side = n_proj + n
@@ -897,7 +949,7 @@
     def side_finish(c):
         value = (s_near[c % 3] + side.finish(c)).astype(bf16)
         if c < n_proj:
-            pay_a[c * block : (c + 1) * block, 3 * HEAD_DIM :] = value
+            pay_p[c * block : (c + 1) * block, :] = value
         else:
             if c - 2 >= n_proj:
                 side_copy(c - 2).wait()
@@ -914,6 +966,23 @@
 
     side_start(0)
     side_start(1)
+    for c in range(n_side + 2):
+        due((4.1, 7.0, 15.6, 23.0, 35.4, 40.5, 47.5, 52.2, 75, 80.5)[min(c, 9)] + max(c - 9, 0), side_step, c)
+    if scatter_inside:
+        for load in loads:
+            load.start()
+
+    proj_sum = DpSum(pay_p, recv_p, sum_p, masks, p_sems, keep_sems.at[0])
+    first_sum = DpSum(pay_a, recv_a, sum_a, turned, a_sems, keep_sems.at[1])
+    second_sum = DpSum(pay_b, recv_b, sum_b, masks, b_sems, keep_sems.at[2])
+    due(25, proj_sum.start)
+    for which, times in (
+        (proj_sum, (36, 40.5, 45, 57, 63, 81)),
+        (first_sum, (41, 48, 60, 66, 77, 100)),
+        (second_sum, (59.5, 63, 66, 68, 78, 300)),
+    ):
+        for s in range(2 * steps):
+            due(times[min(s * 3 // steps, 5)] + 0.01 * s, which.advance, s)
 
     apart = (1 - kind[0]).astype(f32) * masked_value
     slopes = [s * LOG2E for s in head_slopes(me, heads)]
@@ -997,6 +1066,7 @@
                 return 0
 
             lax.fori_loop(0, 2 * m + 1, inner, 0)
+            service(step, 2 * m + 1)
             tile(m, 2 * m + 1, True)
             for copy in load_normed(h, m):
                 copy.wait()
@@ -1035,41 +1105,37 @@
 
         lax.fori_loop(0, pairs, outer, 0)
 
-    todo = {}
-
-    def tiles_of():
-        return [(step, j) for step in range(pairs) for j in range(2 * (pairs - 1 - step) + 1)]
-
-    places = [(h, step, j) for h in range(heads) for step, j in tiles_of()]
-    spread_out = len(places) / (n_side + 2.0)
-    for c in range(n_side + 2):
-        at = min(int((c + 0.7) * spread_out), len(places) - 1)
-        todo.setdefault(places[at], []).append(functools.partial(side_step, c))
-    if scatter_inside:
-        for s in range(steps - 1):
-            for scatter, share in ((wide_rs, 0.45 + 0.25 * s), (narrow_rs, 0.72 + 0.2 * s)):
-                def go(scatter=scatter, s=s):
-                    scatter.arrive(s)
-                    scatter.start(s + 1)
-
-                at = min(int(share * len(places)), len(places) - 1)
-                todo.setdefault(places[at], []).append(go)
+    places, clock = [], 3.0
+    for h in range(heads):
+        for step in range(pairs):
+            tiles = 2 * (pairs - 1 - step) + 2
+            for j in range(tiles):
+                places.append((clock, h, step, j))
+                clock += 1.9 if j + 1 < tiles else 1.1
+            clock += 1.6
+    finish_clock, finish_time = clock, 2.7
+
+    def events(start, end):
+        return [action for time, _, action in sorted(agenda, key=lambda e: e[:2]) if start <= time < end]
+
+    def run(actions):
+        for action in actions:
+            action()
 
     def service_of(h):
         def service(step, j):
-            for (hh, at_step, at_j), actions in todo.items():
-                if hh == h:
+            for k, (time, at_h, at_step, at_j) in enumerate(places):
+                earlier = places[k - 1][0] if k else -1.0
+                actions = events(earlier + 1e-6, time + 1e-6)
+                if at_h == h and actions:
                     @pl.when((step == at_step) & (j == at_j))
                     def _(actions=actions):
-                        for action in actions:
-                            action()
+                        run(actions)
 
         return service
 
-    first_sum = DpSum(pay_a, recv_a, sum_a, masks, a_sems, keep_sems.at[0])
-    second_sum = DpSum(pay_b, recv_b, sum_b, masks, b_sems, keep_sems.at[1])
     sweep(0, service_of(0))
-    pay_a[:, 0 : 3 * HEAD_DIM] = wgrad[...].astype(bf16)
+    pay_a[...] = wgrad[...].astype(bf16)
     first_sum.start()
     sweep(1, service_of(1))
     pay_b[...] = wgrad[...].astype(bf16)
@@ -1097,6 +1163,11 @@
     small[0:2, :] = sums_2[...]
     small[4:5, 0:grad_bias.shape[1]] = grad_bias[...]
     small[5:6, 0:width] = grad_bias_reduce[...]
+
+    def last_middle(q):
+        near = last.middle(q)
+        dk_acc[at_rows(q), :] = near[:, 0:HEAD_DIM]
+        dv_acc[at_rows(q), :] = near[:, HEAD_DIM:]
 
     def last_chunk(q, _):
         load_x(q).wait()
@@ -1124,21 +1195,28 @@
         last.start(q)
         small[2:3, :] += jnp.sum(gf * centred, axis=0, keepdims=True)
         small[3:4, :] += jnp.sum(gf, axis=0, keepdims=True)
-        near = last.middle(q)
-        dk_acc[at_rows(q), :] = near[:, 0:HEAD_DIM]
-        dv_acc[at_rows(q), :] = near[:, HEAD_DIM:]
+        @pl.when(q >= 1)
+        def _():
+            last_middle(q - 1)
+
         return 0
 
-    half = n // 2
-    lax.fori_loop(0, half, last_chunk, 0)
-    if scatter_inside:
-        wide_rs.arrive(steps - 1)
-        wide_sum[...] = wide[:, at_cols(group, local)].astype(f32)
-    first_sum.advance(0)
-    lax.fori_loop(half, n, last_chunk, 0)
-    if scatter_inside:
-        narrow_rs.arrive(steps - 1)
-        narrow_sum[...] = narrow[:, at_cols(group, local)].astype(f32)
+    done = places[-1][0] + 1e-6
+
+    def last_step(q, _):
+        for k in range(n):
+            start = done if k == 0 else finish_clock + (k - 1) * finish_time
+            actions = events(start, finish_clock + k * finish_time)
+            if actions:
+                @pl.when(q == k)
+                def _(actions=actions):
+                    run(actions)
+
+        return last_chunk(q, _)
+
+    lax.fori_loop(0, n, last_step, 0)
+    last_middle(n - 1)
+    done = finish_clock + (n - 1) * finish_time
 
     def small_copy(s):
         where = {"head": partner(me, masks_of(4)[s])} if s < 2 else {"dp": partner(group, masks[s - 2])}
@@ -1161,19 +1239,12 @@
         last_copy(q).start()
 
     small_copy(0).start()
-    for s in range(2 * steps):
-        second_sum.advance(s)
-        if s + 1 < 2 * steps:
-            first_sum.advance(s + 1)
-        if s < n:
-            last_finish(s)
-        if s < 2 + steps:
-            small_step(s)
-    for s in range(2 * steps, max(n, 2 + steps)):
-        if s < n:
-            last_finish(s)
-        if s < 2 + steps:
-            small_step(s)
+    for s in range(2 + steps):
+        due(done + 2.5 * (s + 1), small_step, s)
+    for q in range(n):
+        due(max(done, finish_clock + 6.1 * (q + 1) + 4.0), last_finish, q)
+    run(events(done, 1e9))
+    proj_sum.settle()
     first_sum.settle()
     second_sum.settle()
     if scatter_inside:
@@ -1201,7 +1272,7 @@
     vmem = pl.BlockSpec(memory_space=pltpu.VMEM)
     blocks = max(dp_size - 1, 1)
     n_side = features // block + n
-    cols_a, cols_b = 3 * HEAD_DIM + width, 3 * HEAD_DIM
+    cols = 3 * HEAD_DIM
     part = features // dp_size
     recv_blocks = blocks if inside else 1
 
@@ -1210,13 +1281,14 @@
 
     return pl.pallas_call(
         functools.partial(third_kernel, masks, inside),
-        in_specs=[pl.BlockSpec(memory_space=pltpu.SMEM)] + [vmem] * 12 + [any_spec] * 6,
-        out_specs=[any_spec] * 4 + [vmem] * 3,
+        in_specs=[pl.BlockSpec(memory_space=pltpu.SMEM)] + [vmem] * 10 + [any_spec] * 8,
+        out_specs=[any_spec] * 5 + [vmem] * 3,
         out_shape=[
             jax.ShapeDtypeStruct((rows, width), bf16),
             jax.ShapeDtypeStruct((rows, width), bf16),
-            jax.ShapeDtypeStruct((features, cols_a), bf16),
-            jax.ShapeDtypeStruct((features, cols_b), bf16),
+            jax.ShapeDtypeStruct((features, width), bf16),
+            jax.ShapeDtypeStruct((features, cols), bf16),
+            jax.ShapeDtypeStruct((features, cols), bf16),
             jax.ShapeDtypeStruct((features, home), f32),
             jax.ShapeDtypeStruct((features, home), f32),
             jax.ShapeDtypeStruct((8, features), f32),
@@ -1227,12 +1299,16 @@
             pltpu.VMEM((rows, HEAD_DIM), f32),
             pltpu.VMEM((HEAD_DIM, 2 * block), f32),
             pltpu.VMEM((n, heads, block), f32),
-            pltpu.VMEM((features, cols_b), f32),
+            pltpu.VMEM((features, cols), f32),
             pltpu.VMEM((4, block, features), bf16),
-            pltpu.VMEM((features, cols_a), bf16),
-            pltpu.VMEM((features, cols_b), bf16),
-            pltpu.VMEM((blocks, part, cols_a), bf16),
-            pltpu.VMEM((blocks, part, cols_b), bf16),
+            pltpu.VMEM(wide.shape if inside else (16, 128), bf16),
+            pltpu.VMEM(narrow.shape if inside else (16, 128), bf16),
+            pltpu.VMEM((features, width), bf16),
+            pltpu.VMEM((features, cols), bf16),
+            pltpu.VMEM((features, cols), bf16),
+            pltpu.VMEM((blocks, part, width), bf16),
+            pltpu.VMEM((blocks, part, cols), bf16),
+            pltpu.VMEM((blocks, part, cols), bf16),
             pltpu.VMEM((recv_blocks, features, home), bf16),
             pltpu.VMEM((recv_blocks, features, home), bf16),
             pltpu.VMEM((n_side * block, 2 * width), bf16),
@@ -1253,10 +1329,11 @@
             dma(6, n),
             dma(4, blocks),
             dma(4, blocks),
+            dma(4, blocks),
             dma(2, blocks),
             dma(2, blocks),
             dma(4),
-            dma(2),
+            dma(5),
             dma(2, 2 + len(masks)),
             dma(3, n),
         ],
@@ -1299,7 +1376,7 @@
     ) = second(
         x, a, grad_out, layer_in, proj, expand, reduce, ffn_gain[None], ffn_shift[None], bias
     )
-    ffn_sum, grad_in, sum_a, sum_b, grad_expand, grad_reduce, small = third(
+    ffn_sum, grad_in, sum_p, sum_a, sum_b, grad_expand, grad_reduce, small = third(
         bucket, qkv, grad_heads, logsum, w_query, w_key, w_value, gain_1, sums_2, grad_bias, grad_bias_reduce,
         grad_wide, grad_narrow, a, x, normed, grad_hid, ffn, proj_part, local, dp_size,
     )
@@ -1312,7 +1389,7 @@
         jnp.concatenate([sum_a[:, k * head : (k + 1) * head], sum_b[:, k * head : (k + 1) * head]], 1).astype(f32)
         for k in range(3)
     )
-    grad_proj = sum_a[:, 3 * head :].astype(f32).T
+    grad_proj = sum_p.astype(f32).T
     return (
         layer_out,
         grad_in.astype(f32),

time: 376 us -> 335 us (0.89)
  Pallas kernels: 352 us -> 313 us
    pallas_call x1, Pallas kernels: 161 us -> 123 us  [third(): pl.pallas_call(functools.partial(third_kernel, masks, inside), in_specs=[...]
where the time goes in v4:
time: 335 us; the launch traced here: 330 us
  Pallas kernels  313 us (93%)
  other arithmetic  8.39 us (3%)
  local copies, waits for them, and re-layouts  6.13 us (2%)
    pallas_call x1, Pallas kernels, third(): pl.pallas_call(functools.partial(third_kernel, masks, inside), in_specs=[...  123 us
    pallas_call x1, Pallas kernels, second(): pl.pallas_call(second_kernel, in_specs=[any_spec] * 6 + [vmem] * 4, out_s...  99.1 us
    pallas_call x1, Pallas kernels, first(): pl.pallas_call(functools.partial(first_kernel, masks, gather), in_specs=[...  91.5 us

profile of v4, /device:TPU:0, one launch (start us, length us, event | category | flops | bytes accessed | tf_op | source)
XLA Modules:
  0.0 329.6 jit_solution(14228200457682822346)
XLA Ops:
  1.3 91.5 %shard_map.254 = (bf16[3072,1024]{1,0:T(8,128)(2,1)}, bf16[3072,1024]{1,0:T(8,128)(2,1)}, bf16[3072,1024]{1,0:T(8,128)(2,1)}, bf16[3072,768]{1,0:T(8,128)(2,1)},...) custom-call(s32[1]{0:T(128)S(6)} %copy.32.kind, ...), custom_call_target="tpu_custom_call" | custom-call | tf_op jit(solution)/shard_map/pallas_call | solution.py:418
  92.8 1.3 slice_convert_fusion.bias
  94.1 99.1 %shard_map.255 = (bf16[3072,256]{1,0:T(8,128)(2,1)}, bf16[3072,1024]{1,0:T(8,128)(2,1)}, bf16[3072,1024]{1,0:T(8,128)(2,1)}, f32[3072,256]{1,0:T(8,128)}, bf16[1...) custom-call(bf16[3072,1024]{1,0:T(8,128)(2,1)} %get-tuple-element.41, ...), custom_call_target="tpu_custom_call" | custom-call | tf_op jit(solution)/shard_map/pallas_call | solution.py:698
  193.3 122.8 %shard_map.256 = (bf16[3072,256]{1,0:T(8,128)(2,1)}, bf16[3072,256]{1,0:T(8,128)(2,1)}, bf16[1024,256]{1,0:T(8,128)(2,1)}, bf16[1024,384]{1,0:T(8,128)(2,1)}, bf...) custom-call(s32[1]{0:T(128)S(6)} %copy.32.kind, ...), custom_call_target="tpu_custom_call" | custom-call | tf_op jit(solution)/shard_map/pallas_call | solution.py:1282
  316.1 1.5 fusion
  317.5 0.0 copy-start
  317.5 0.0 copy-start.2
  317.5 0.0 copy-start.7
  317.5 1.0 maximum_convert_fusion.2
  318.6 1.0 maximum_convert_fusion.1
  319.6 1.0 maximum_convert_fusion
  320.7 0.0 copy-done
  320.7 0.0 copy-done.2
  320.7 0.0 copy-done.7
  320.7 0.0 copy-start.1
  320.7 2.0 convert_add_fusion
  322.7 0.0 copy-start.3
  322.7 0.0 copy-done.1
  322.7 0.0 copy-start.6
  322.7 0.0 copy-start.5
  322.7 1.9 convert_element_type.21
  324.6 0.0 copy-start.4
  324.6 0.0 copy-done.3
  324.6 0.1 convert_bitcast_fusion
  324.7 1.3 copy.29
  326.0 0.0 copy-done.6
  326.0 0.6 fusion.2
  326.6 0.6 constant_dynamic-slice_fusion
  327.2 0.6 slice.47
  327.7 0.0 copy-done.5
  327.7 0.8 copy.33
  328.5 0.0 copy-done.4
  328.5 0.8 copy.34
Async XLA Ops:
  317.5 3.2 copy-start
  317.5 3.1 copy-start.2
  317.5 3.1 copy-start.7
  320.7 2.0 copy-start.1
  322.7 1.9 copy-start.3
  322.7 3.3 %copy-start.6 = (f32[8,1024]{1,0:T(8,128)S(1)}, f32[8,1024]{1,0:T(8,128)}, u32[]{:S(2)}) copy-start(f32[8,1024]{1,0:T(8,128)} %get-tuple-element.65) | copy-start | bytes 98308
  322.7 5.1 %copy-start.5 = (f32[1024,128]{1,0:T(8,128)S(1)}, f32[1024,128]{1,0:T(8,128)}, u32[]{:S(2)}) copy-start(f32[1024,128]{1,0:T(8,128)} %get-tuple-element.119) | copy-start | bytes 1572868
  324.6 4.0 %copy-start.4 = (f32[1024,128]{1,0:T(8,128)S(1)}, f32[1024,128]{1,0:T(8,128)}, u32[]{:S(2)}) copy-start(f32[1024,128]{1,0:T(8,128)} %get-tuple-element.121) | copy-start | bytes 1572868

commit v5 on v4

--- a/solution.py
+++ b/solution.py
@@ -449,12 +449,11 @@
         ),
     )(kind, layer_in, wq, wk, wv, gain, shift, bias_expand, w_proj, w_expand, w_reduce)
     x, a, normed, qkv, proj, expand, reduce, bias, logsum = outs
-    bias = bias[:1]
     if not gather:
-        bias = lax.all_gather(bias_expand, "dp", axis=1, tiled=True)
+        bias = jnp.broadcast_to(lax.all_gather(bias_expand, "dp", axis=1, tiled=True), (16, local * dp_size))
         expand = lax.all_gather(w_expand, "dp", axis=1, tiled=True)
         reduce = lax.all_gather(w_reduce, "dp", axis=1, tiled=True)
-    return x, a, normed, qkv, proj, expand, reduce, bias.astype(f32), logsum
+    return x, a, normed, qkv, proj, expand, reduce, bias, logsum
 
 
 class HeadScatter:
@@ -608,7 +607,10 @@
         a = a_buf[slot]
         attn = dot(a, w_proj[...])
         hidden = attn + x_buf[slot].astype(f32)
-        own_buf[slot] = dot(a, w_proj[:, at_cols(me, width)]) + in_buf[slot]
+        own = attn[:, 0:width]
+        for k in range(1, 4):
+            own = jnp.where(me == k, attn[:, k * width : (k + 1) * width], own)
+        own_buf[slot] = own + in_buf[slot]
         store_own(r).start()
         centre = hidden - jnp.sum(hidden, axis=1, keepdims=True) * (1.0 / features)
         spread = jnp.sum(centre * centre, axis=1, keepdims=True) * (1.0 / features)
@@ -621,7 +623,7 @@
             loads[1].wait()
             loads[2].wait()
 
-        z = dot(low, w_expand[...]) + bias[...]
+        z = dot(low, w_expand[...]) + bias[0:1, :].astype(f32)
         z2 = z * z
         t = jnp.tanh(z * (GELU_C + (GELU_C * 0.044715) * z2))
         half = 0.5 + 0.5 * t
@@ -742,6 +744,22 @@
     )(x, a, layer_in, w_proj, w_expand, w_reduce, grad_out, gain, shift, bias)
 
 
+EARLY = 0
+TIMES = {
+    "start": 25.4,
+    "middle": (8.4, 12.6, 20.2, 21.1, 21.7, 26.6, 31.4, 38.8),
+    "finish": (15.8, 22.4, 56.4, 76.2, 79.1, 82.6, 86.4, 87.9),
+    "wide": (59.1, 71.4, 94.0),
+    "narrow": (33.3, 51.5, 80.5),
+    "proj": (36.2, 40.5, 49.8, 56.8, 66.6, 82.7),
+    "first": (44.3, 56.8, 61.0, 67.5, 74.8, 81.6),
+    "first_turned": (39.4, 47.3, 60.2, 69.7, 69.7, 86.4),
+    "second": (56.5, 60.1, 68.3, 72.2, 74.9, 312.3),
+    "second_turned": (61.0, 63.4, 68.6, 72.3, 78.2, 407.9),
+    "small": (73.9, 74.9, 76.7, 77.5, 78.5),
+}
+
+
 class DpScatter:
     def __init__(self, part, recv_buf, masks, send, recv, first_part=None):
         self.part, self.recv_buf, self.masks = part, recv_buf, masks
@@ -825,25 +843,25 @@
 
 
 class HeadSum:
-    def __init__(self, width, src, mine, from_core, far, from_chip, sems):
+    def __init__(self, width, src, mine, from_core, from_chip, sems):
         self.width, self.src, self.mine = width, src, mine
-        self.from_core, self.far, self.from_chip, self.sems = from_core, far, from_chip, sems
+        self.from_core, self.from_chip, self.sems = from_core, from_chip, sems
         self.me = lax.axis_index("head")
         self.core, self.chip = partner(self.me, 1), partner(self.me, 2)
+
+    def place(self, r, k):
+        return self.from_core.at[at_rows(r), k * self.width : (k + 1) * self.width]
 
     def to_core(self, r, k):
         who = self.core if k == 0 else partner(self.core, 2)
         return send_to(
-            self.src(r).at[:, at_cols(who, self.width)],
-            self.from_core.at[at_rows(r), k * self.width : (k + 1) * self.width],
-            self.sems.at[2 * k, r],
-            self.sems.at[2 * k + 1, r],
-            head=self.core,
+            self.src(r).at[:, at_cols(who, self.width)], self.place(r, k),
+            self.sems.at[2 * k, r], self.sems.at[2 * k + 1, r], head=self.core,
         )
 
     def to_chip(self, r):
         return send_to(
-            self.far(r), self.from_chip.at[at_rows(r), :], self.sems.at[4, r], self.sems.at[5, r], head=self.chip
+            self.place(r, 1), self.from_chip.at[at_rows(r), :], self.sems.at[4, r], self.sems.at[5, r], head=self.chip
         )
 
     def start(self, r):
@@ -851,17 +869,16 @@
         self.to_core(r, 0).start()
 
     def middle(self, r):
-        self.to_core(r, 1).wait()
-        self.far(r)[...] = (
-            self.mine(r, self.chip, 1) + self.from_core[at_rows(r), self.width :].astype(f32)
-        ).astype(bf16)
-        self.to_chip(r).start()
-        self.to_core(r, 0).wait()
-        return self.mine(r, self.me, 0) + self.from_core[at_rows(r), : self.width].astype(f32)
+        for k, who in ((1, self.chip), (0, self.me)):
+            self.to_core(r, k).wait()
+            place = self.place(r, k)
+            place[...] = (self.mine(r, who, k) + place[...].astype(f32)).astype(bf16)
+            if k == 1:
+                self.to_chip(r).start()
 
     def finish(self, r):
         self.to_chip(r).wait()
-        return self.from_chip[at_rows(r), :].astype(f32)
+        return self.place(r, 0)[...].astype(f32) + self.from_chip[at_rows(r), :].astype(f32)
 
 
 def third_kernel(
@@ -871,7 +888,7 @@
     ffn_sum, total_sum, sum_p, sum_a, sum_b, wide_sum, narrow_sum, small,
     dqkv, dk_acc, dv_acc, dq_acc, delta, wgrad, slots, wide, narrow, pay_p, pay_a, pay_b,
     recv_p, recv_a, recv_b, recv_w, recv_n,
-    s_core, s_far, s_chip, s_near, s_mine, s_out, f_src, f_core, f_far, f_chip, small_recv,
+    s_core, s_chip, s_mine, s_out, f_src, f_core, f_chip, f_slots, small_recv,
     wg_sems, s_sems, mine_sems, out_sems, f_sems, p_sems, a_sems, b_sems, w_sems, n_sems, slot_sems, keep_sems, small_sems, total_sems,
 ):
     rows = qkv.shape[0]
@@ -903,8 +920,8 @@
         wide_rs.start(0)
         narrow_rs.start(0)
         loads = [
-            pltpu.make_async_copy(wide_in, wide, keep_sems.at[3]),
-            pltpu.make_async_copy(narrow_in, narrow, keep_sems.at[4]),
+            pltpu.make_async_copy(wide_in, wide, keep_sems.at[5]),
+            pltpu.make_async_copy(narrow_in, narrow, keep_sems.at[6]),
         ]
 
         def scatter_step(scatter, load, out, s):
@@ -917,8 +934,8 @@
                 out[...] = scatter.part(group)[...].astype(f32)
 
         for s in range(steps):
-            due((63, 70.5, 85)[min(s, 2)] + max(s - 2, 0), scatter_step, wide_rs, loads[0], wide_sum, s)
-            due((28.5, 51.5, 66)[min(s, 2)] + max(s - 2, 0), scatter_step, narrow_rs, loads[1], narrow_sum, s)
+            due(TIMES["wide"][min(s, 2)] + max(s - 2, 0), scatter_step, wide_rs, loads[0], wide_sum, s)
+            due(TIMES["narrow"][min(s, 2)] + max(s - 2, 0), scatter_step, narrow_rs, loads[1], narrow_sum, s)
 
     n_proj = features // block
     n_side = n_proj + n
@@ -929,14 +946,14 @@
     def side_load(c, k):
         who = me if k == 0 else partner(me, 2)
         return pltpu.make_async_copy(
-            side_src(c).at[:, at_cols(who, width)], s_mine.at[c % 2, k], mine_sems.at[k, c]
+            side_src(c).at[:, at_cols(who, width)], s_mine.at[c % 4, k], mine_sems.at[k, c]
         )
 
     def side_mine(c, who, k):
         side_load(c, k).wait()
-        return s_mine[c % 2, k].astype(f32)
-
-    side = HeadSum(width, side_src, side_mine, s_core, lambda c: s_far.at[c % 3], s_chip, s_sems)
+        return s_mine[c % 4, k].astype(f32)
+
+    side = HeadSum(width, side_src, side_mine, s_core, s_chip, s_sems)
 
     def side_copy(c):
         return pltpu.make_async_copy(s_out.at[c % 2], ffn_sum.at[at_rows(c - n_proj), :], out_sems.at[c])
@@ -944,10 +961,14 @@
     def side_start(c):
         side_load(c, 1).start()
         side_load(c, 0).start()
-        side.start(c)
+
+    def side_middle(c):
+        side.middle(c)
+        if c + 4 < n_side:
+            side_start(c + 4)
 
     def side_finish(c):
-        value = (s_near[c % 3] + side.finish(c)).astype(bf16)
+        value = side.finish(c).astype(bf16)
         if c < n_proj:
             pay_p[c * block : (c + 1) * block, :] = value
         else:
@@ -956,30 +977,32 @@
             s_out[c % 2] = value
             side_copy(c).start()
 
-    def side_step(c):
-        if c < n_side:
-            s_near[c % 3] = side.middle(c)
-            if c + 2 < n_side:
-                side_start(c + 2)
-        if 0 <= c - 2 < n_side:
-            side_finish(c - 2)
-
-    side_start(0)
-    side_start(1)
-    for c in range(n_side + 2):
-        due((4.1, 7.0, 15.6, 23.0, 35.4, 40.5, 47.5, 52.2, 75, 80.5)[min(c, 9)] + max(c - 9, 0), side_step, c)
+    for c in range(min(4, n_side)):
+        side_start(c)
+    for c in range(n_side):
+        side.start(c)
+        due(TIMES["middle"][min(c, 7)] + 6 * max(c - 7, 0), side_middle, c)
+        due(TIMES["finish"][min(c, 7)] + 6 * max(c - 7, 0), side_finish, c)
     if scatter_inside:
         for load in loads:
             load.start()
 
     proj_sum = DpSum(pay_p, recv_p, sum_p, masks, p_sems, keep_sems.at[0])
-    first_sum = DpSum(pay_a, recv_a, sum_a, turned, a_sems, keep_sems.at[1])
-    second_sum = DpSum(pay_b, recv_b, sum_b, masks, b_sems, keep_sems.at[2])
-    due(25, proj_sum.start)
+    first_sums, second_sums = [], []
+    halves = 2 if features % (32 << steps) == 0 else 1
+    for p in range(halves):
+        at = slice(p * features // halves, (p + 1) * features // halves)
+        first_sums.append(
+            DpSum(pay_a.at[at], recv_a.at[p], sum_a.at[at], (turned, masks)[p], a_sems.at[p], keep_sems.at[1 + 2 * p])
+        )
+        second_sums.append(
+            DpSum(pay_b.at[at], recv_b.at[p], sum_b.at[at], (masks, turned)[p], b_sems.at[p], keep_sems.at[2 + 2 * p])
+        )
+    due(TIMES["start"], proj_sum.start)
     for which, times in (
-        (proj_sum, (36, 40.5, 45, 57, 63, 81)),
-        (first_sum, (41, 48, 60, 66, 77, 100)),
-        (second_sum, (59.5, 63, 66, 68, 78, 300)),
+        [(proj_sum, TIMES["proj"])]
+        + list(zip(first_sums, (TIMES["first"], TIMES["first_turned"])))
+        + list(zip(second_sums, (TIMES["second"], TIMES["second_turned"])))
     ):
         for s in range(2 * steps):
             due(times[min(s * 3 // steps, 5)] + 0.01 * s, which.advance, s)
@@ -1018,6 +1041,61 @@
 
     def head_cols(h, k):
         return pl.ds(pl.multiple_of(k * width + h * HEAD_DIM, HEAD_DIM), HEAD_DIM)
+
+    def load_x(q):
+        return pltpu.make_async_copy(x_in.at[at_rows(n - 1 - q), :], f_slots.at[q % 2], total_sems.at[0, q])
+
+    def load_hid(q):
+        return pltpu.make_async_copy(grad_hid.at[at_rows(n - 1 - q), :], f_slots.at[2 + q % 2], total_sems.at[1, q])
+
+    def last_mine(q, who, k):
+        return f_src[q % 2, :, at_cols(who, width)].astype(f32)
+
+    last = HeadSum(width, lambda q: f_src.at[q % 2], last_mine, f_core, f_chip, f_sems)
+
+    def last_copy(q):
+        return pltpu.make_async_copy(
+            dqkv.at[at_rows(n - 1 - q), 0:width], total_sum.at[at_rows(n - 1 - q), :], total_sems.at[2, q]
+        )
+
+    load_x(0).start()
+    load_hid(0).start()
+    small[...] = jnp.zeros_like(small)
+    small[0:2, :] = sums_2[...]
+    small[4:5, 0:grad_bias.shape[1]] = grad_bias[...]
+    small[5:6, 0:width] = grad_bias_reduce[...]
+
+    def last_chunk(q, _):
+        load_x(q).wait()
+        load_hid(q).wait()
+
+        @pl.when(q + 1 < n)
+        def _():
+            load_x(q + 1).start()
+            load_hid(q + 1).start()
+
+        at = at_rows(n - 1 - q)
+        gf = dot(dqkv[at, 0:width], wq[...], NT)
+        gf += dot(dqkv[at, width : 2 * width], wk[...], NT)
+        gf += dot(dqkv[at, 2 * width :], wv[...], NT)
+        x = f_slots[q % 2].astype(f32)
+        centre = x - jnp.sum(x, axis=1, keepdims=True) * (1.0 / features)
+        spread = jnp.sum(centre * centre, axis=1, keepdims=True) * (1.0 / features)
+        scale = lax.rsqrt(spread + eps)
+        centred = centre * scale
+        scaled = gf * gain[...]
+        mean_scaled = jnp.sum(scaled, axis=1, keepdims=True) * (1.0 / features)
+        mean_both = jnp.sum(scaled * centred, axis=1, keepdims=True) * (1.0 / features)
+        back = (scaled - mean_scaled - centred * mean_both) * scale
+        f_src[q % 2] = (back + f_slots[2 + q % 2].astype(f32)).astype(bf16)
+        last.start(q)
+        small[2:3, :] += jnp.sum(gf * centred, axis=0, keepdims=True)
+        small[3:4, :] += jnp.sum(gf, axis=0, keepdims=True)
+        @pl.when(q >= 1)
+        def _():
+            last.middle(q - 1)
+
+        return 0
 
     def sweep(h, service):
         own_cols = pl.ds(pl.multiple_of(h * HEAD_DIM, HEAD_DIM), HEAD_DIM)
@@ -1101,6 +1179,12 @@
             def _():
                 wgrad[...] += part
 
+            if h + 1 == heads:
+                for early in range(EARLY):
+                    @pl.when(step == early)
+                    def _(early=early):
+                        lax.fori_loop(2 * early, 2 * early + 2, last_chunk, 0)
+
             return 0
 
         lax.fori_loop(0, pairs, outer, 0)
@@ -1112,8 +1196,9 @@
             for j in range(tiles):
                 places.append((clock, h, step, j))
                 clock += 1.9 if j + 1 < tiles else 1.1
-            clock += 1.6
+            clock += 1.6 + (5.4 if h + 1 == heads and step < EARLY else 0.0)
     finish_clock, finish_time = clock, 2.7
+    begun = 2 * EARLY
 
     def events(start, end):
         return [action for time, _, action in sorted(agenda, key=lambda e: e[:2]) if start <= time < end]
@@ -1136,77 +1221,19 @@
 
     sweep(0, service_of(0))
     pay_a[...] = wgrad[...].astype(bf16)
-    first_sum.start()
+    for which in first_sums:
+        which.start()
     sweep(1, service_of(1))
     pay_b[...] = wgrad[...].astype(bf16)
-    second_sum.start()
-
-    def load_x(q):
-        return pltpu.make_async_copy(x_in.at[at_rows(n - 1 - q), :], slots.at[q % 2], total_sems.at[0, q])
-
-    def load_hid(q):
-        return pltpu.make_async_copy(grad_hid.at[at_rows(n - 1 - q), :], slots.at[2 + q % 2], total_sems.at[1, q])
-
-    def last_mine(q, who, k):
-        return f_src[q % 2, :, at_cols(who, width)].astype(f32)
-
-    last = HeadSum(width, lambda q: f_src.at[q % 2], last_mine, f_core, lambda q: f_far.at[at_rows(q), :], f_chip, f_sems)
-
-    def last_copy(q):
-        return pltpu.make_async_copy(
-            dqkv.at[at_rows(n - 1 - q), 0:width], total_sum.at[at_rows(n - 1 - q), :], total_sems.at[2, q]
-        )
-
-    load_x(0).start()
-    load_hid(0).start()
-    small[...] = jnp.zeros_like(small)
-    small[0:2, :] = sums_2[...]
-    small[4:5, 0:grad_bias.shape[1]] = grad_bias[...]
-    small[5:6, 0:width] = grad_bias_reduce[...]
-
-    def last_middle(q):
-        near = last.middle(q)
-        dk_acc[at_rows(q), :] = near[:, 0:HEAD_DIM]
-        dv_acc[at_rows(q), :] = near[:, HEAD_DIM:]
-
-    def last_chunk(q, _):
-        load_x(q).wait()
-        load_hid(q).wait()
-
-        @pl.when(q + 1 < n)
-        def _():
-            load_x(q + 1).start()
-            load_hid(q + 1).start()
-
-        at = at_rows(n - 1 - q)
-        gf = dot(dqkv[at, 0:width], wq[...], NT)
-        gf += dot(dqkv[at, width : 2 * width], wk[...], NT)
-        gf += dot(dqkv[at, 2 * width :], wv[...], NT)
-        x = slots[q % 2].astype(f32)
-        centre = x - jnp.sum(x, axis=1, keepdims=True) * (1.0 / features)
-        spread = jnp.sum(centre * centre, axis=1, keepdims=True) * (1.0 / features)
-        scale = lax.rsqrt(spread + eps)
-        centred = centre * scale
-        scaled = gf * gain[...]
-        mean_scaled = jnp.sum(scaled, axis=1, keepdims=True) * (1.0 / features)
-        mean_both = jnp.sum(scaled * centred, axis=1, keepdims=True) * (1.0 / features)
-        back = (scaled - mean_scaled - centred * mean_both) * scale
-        f_src[q % 2] = (back + slots[2 + q % 2].astype(f32)).astype(bf16)
-        last.start(q)
-        small[2:3, :] += jnp.sum(gf * centred, axis=0, keepdims=True)
-        small[3:4, :] += jnp.sum(gf, axis=0, keepdims=True)
-        @pl.when(q >= 1)
-        def _():
-            last_middle(q - 1)
-
-        return 0
+    for which in second_sums:
+        which.start()
 
     done = places[-1][0] + 1e-6
 
     def last_step(q, _):
-        for k in range(n):
-            start = done if k == 0 else finish_clock + (k - 1) * finish_time
-            actions = events(start, finish_clock + k * finish_time)
+        for k in range(begun, n):
+            start = done if k == begun else finish_clock + (k - begun - 1) * finish_time
+            actions = events(start, finish_clock + (k - begun) * finish_time)
             if actions:
                 @pl.when(q == k)
                 def _(actions=actions):
@@ -1214,9 +1241,9 @@
 
         return last_chunk(q, _)
 
-    lax.fori_loop(0, n, last_step, 0)
-    last_middle(n - 1)
-    done = finish_clock + (n - 1) * finish_time
+    lax.fori_loop(begun, n, last_step, 0)
+    last.middle(n - 1)
+    done = finish_clock + (n - begun - 1) * finish_time
 
     def small_copy(s):
         where = {"head": partner(me, masks_of(4)[s])} if s < 2 else {"dp": partner(group, masks[s - 2])}
@@ -1232,21 +1259,18 @@
             small_copy(s + 1).start()
 
     def last_finish(q):
-        far = last.finish(q)
-        at = at_rows(n - 1 - q)
-        dqkv[at, 0:HEAD_DIM] = (dk_acc[at_rows(q), :] + far[:, 0:HEAD_DIM]).astype(bf16)
-        dqkv[at, HEAD_DIM:width] = (dv_acc[at_rows(q), :] + far[:, HEAD_DIM:]).astype(bf16)
+        dqkv[at_rows(n - 1 - q), 0:width] = last.finish(q).astype(bf16)
         last_copy(q).start()
 
     small_copy(0).start()
     for s in range(2 + steps):
-        due(done + 2.5 * (s + 1), small_step, s)
+        due(max(done, TIMES["small"][min(s, 4)]) + max(s - 4, 0), small_step, s)
     for q in range(n):
-        due(max(done, finish_clock + 6.1 * (q + 1) + 4.0), last_finish, q)
+        due(max(done, finish_clock + 6.1 * (q - begun + 1) + 4.0), last_finish, q)
     run(events(done, 1e9))
     proj_sum.settle()
-    first_sum.settle()
-    second_sum.settle()
+    for which in first_sums + second_sums:
+        which.settle()
     if scatter_inside:
         wide_rs.sent()
         narrow_rs.sent()
@@ -1274,6 +1298,7 @@
     n_side = features // block + n
     cols = 3 * HEAD_DIM
     part = features // dp_size
+    halves = 2 if features % (32 * dp_size) == 0 else 1
     recv_blocks = blocks if inside else 1
 
     def dma(*shape):
@@ -1307,20 +1332,18 @@
             pltpu.VMEM((features, cols), bf16),
             pltpu.VMEM((features, cols), bf16),
             pltpu.VMEM((blocks, part, width), bf16),
-            pltpu.VMEM((blocks, part, cols), bf16),
-            pltpu.VMEM((blocks, part, cols), bf16),
+            pltpu.VMEM((halves, blocks, part // halves, cols), bf16),
+            pltpu.VMEM((halves, blocks, part // halves, cols), bf16),
             pltpu.VMEM((recv_blocks, features, home), bf16),
             pltpu.VMEM((recv_blocks, features, home), bf16),
             pltpu.VMEM((n_side * block, 2 * width), bf16),
-            pltpu.VMEM((3, block, width), bf16),
             pltpu.VMEM((n_side * block, width), bf16),
-            pltpu.VMEM((3, block, width), f32),
-            pltpu.VMEM((2, 2, block, width), bf16),
+            pltpu.VMEM((4, 2, block, width), bf16),
             pltpu.VMEM((2, block, width), bf16),
             pltpu.VMEM((2, block, features), bf16),
             pltpu.VMEM((rows, 2 * width), bf16),
             pltpu.VMEM((rows, width), bf16),
-            pltpu.VMEM((rows, width), bf16),
+            pltpu.VMEM((4, block, features), bf16),
             pltpu.VMEM((2 + len(masks), 8, features), f32),
             dma(3),
             dma(6, n_side),
@@ -1328,12 +1351,12 @@
             dma(n_side),
             dma(6, n),
             dma(4, blocks),
-            dma(4, blocks),
-            dma(4, blocks),
+            dma(halves, 4, blocks),
+            dma(halves, 4, blocks),
             dma(2, blocks),
             dma(2, blocks),
             dma(4),
-            dma(5),
+            dma(7),
             dma(2, 2 + len(masks)),
             dma(3, n),
         ],
@@ -1344,6 +1367,68 @@
         kind, qkv, grad_heads, logsum, wq, wk, wv, gain, sums_2, grad_bias, grad_bias_reduce, wide, narrow,
         a, x, normed, grad_hid, ffn, proj,
     )
+
+
+def output_kernel(
+    hid_own, ffn_sum, total, bias_reduce, sum_p, sum_a, sum_b, wide_sum, narrow_sum, small,
+    layer_out, grad_in, grad_q, grad_k, grad_v, grad_proj, grad_expand, grad_reduce,
+    attn_gain, attn_shift, ffn_gain, ffn_shift, grad_bias_reduce, *grad_bias,
+):
+    layer_out[...] = hid_own[...] + bias_reduce[...] + ffn_sum[...].astype(f32)
+    grad_in[...] = total[...].astype(f32)
+    for k, out in enumerate((grad_q, grad_k, grad_v)):
+        cols = slice(k * HEAD_DIM, (k + 1) * HEAD_DIM)
+        out[:, 0:HEAD_DIM] = sum_a[:, cols].astype(f32)
+        out[:, HEAD_DIM:] = sum_b[:, cols].astype(f32)
+    grad_proj[...] = sum_p[...].astype(f32).T
+    grad_expand[...] = wide_sum[...]
+    grad_reduce[...] = narrow_sum[...]
+    for k, out in ((2, attn_gain), (3, attn_shift), (0, ffn_gain), (1, ffn_shift)):
+        out[...] = small[k, :]
+    grad_bias_reduce[...] = small[5, 0 : grad_bias_reduce.shape[0]]
+    for out in grad_bias:
+        out[...] = small[4:5, at_cols(lax.axis_index("dp"), out.shape[1])]
+
+
+def outputs(hid_own, ffn_sum, total, bias_reduce, sum_p, sum_a, sum_b, wide_sum, narrow_sum, small, inside):
+    rows, width = hid_own.shape
+    features = sum_p.shape[0]
+    block = 2 * SHORT
+    part = features // 2
+    home = wide_sum.shape[1]
+
+    def by_rows(columns):
+        return pl.BlockSpec((block, columns), lambda i: (i, 0))
+
+    def by_part(columns):
+        return pl.BlockSpec((part, columns), lambda i: (jnp.minimum(i, 1), 0))
+
+    def of(*shape):
+        return jax.ShapeDtypeStruct(shape, f32)
+
+    return pl.pallas_call(
+        output_kernel,
+        grid=(rows // block,),
+        in_specs=[
+            by_rows(width), by_rows(width), by_rows(width), full_spec(bias_reduce.shape), by_part(width),
+            by_part(sum_a.shape[1]), by_part(sum_b.shape[1]), by_part(home), by_part(home), full_spec(small.shape),
+        ],
+        out_specs=[by_rows(width)] * 2
+        + [by_part(width)] * 3
+        + [pl.BlockSpec((width, part), lambda i: (0, jnp.minimum(i, 1)))]
+        + [by_part(home)] * 2
+        + [full_spec((features,))] * 4
+        + [full_spec((width,))]
+        + [full_spec((1, home))] * inside,
+        out_shape=[of(rows, width)] * 2
+        + [of(features, width)] * 3
+        + [of(width, features)]
+        + [of(features, home)] * 2
+        + [of(features)] * 4
+        + [of(width)]
+        + [of(1, home)] * inside,
+        compiler_params=pltpu.CompilerParams(vmem_limit_bytes=62 * MIB),
+    )(hid_own, ffn_sum, total, bias_reduce, sum_p, sum_a, sum_b, wide_sum, narrow_sum, small)
 
 
 def shards(
@@ -1376,35 +1461,36 @@
     ) = second(
         x, a, grad_out, layer_in, proj, expand, reduce, ffn_gain[None], ffn_shift[None], bias
     )
-    ffn_sum, grad_in, sum_p, sum_a, sum_b, grad_expand, grad_reduce, small = third(
+    ffn_sum, total, sum_p, sum_a, sum_b, wide_sum, narrow_sum, small = third(
         bucket, qkv, grad_heads, logsum, w_query, w_key, w_value, gain_1, sums_2, grad_bias, grad_bias_reduce,
         grad_wide, grad_narrow, a, x, normed, grad_hid, ffn, proj_part, local, dp_size,
     )
     if local % 128:
-        grad_expand = lax.psum_scatter(grad_wide.astype(f32), "dp", scatter_dimension=1, tiled=True)
-        grad_reduce = lax.psum_scatter(grad_narrow.astype(f32), "dp", scatter_dimension=1, tiled=True)
-    layer_out = hid_own + bias_reduce + ffn_sum.astype(f32)
-    head = HEAD_DIM
-    grad_query, grad_key, grad_value = (
-        jnp.concatenate([sum_a[:, k * head : (k + 1) * head], sum_b[:, k * head : (k + 1) * head]], 1).astype(f32)
-        for k in range(3)
+        wide_sum = lax.psum_scatter(grad_wide.astype(f32), "dp", scatter_dimension=1, tiled=True)
+        narrow_sum = lax.psum_scatter(grad_narrow.astype(f32), "dp", scatter_dimension=1, tiled=True)
+    (
+        layer_out, grad_in, grad_query, grad_key, grad_value, grad_proj, grad_expand, grad_reduce,
+        grad_attn_gain, grad_attn_shift, grad_ffn_gain, grad_ffn_shift, grad_bias_reduce, *grad_bias_expand,
+    ) = outputs(
+        hid_own, ffn_sum, total, bias_reduce[None], sum_p, sum_a, sum_b, wide_sum, narrow_sum, small, int(local % 128 == 0)
     )
-    grad_proj = sum_p.astype(f32).T
+    if local % 128:
+        grad_bias_expand = [lax.dynamic_slice(small, (4, group * local), (1, local))]
     return (
         layer_out,
-        grad_in.astype(f32),
+        grad_in,
         grad_query,
         grad_key,
         grad_value,
         grad_proj,
-        small[2],
-        small[3],
-        small[0],
-        small[1],
+        grad_attn_gain,
+        grad_attn_shift,
+        grad_ffn_gain,
+        grad_ffn_shift,
         grad_expand,
-        lax.dynamic_slice(small, (4, group * local), (1, local)),
+        grad_bias_expand[0],
         grad_reduce,
-        small[5, :width],
+        grad_bias_reduce,
     )
 
 

time: 335 us -> 321 us (0.958)
  other arithmetic: 8.39 us -> 0 us
  local copies, waits for them, and re-layouts: 6.13 us -> 0 us
    pallas_call x0 -> x1, Pallas kernels: none -> 8.42 us  [outputs(): pl.pallas_call(output_kernel, grid=(rows // block,), in_specs=[by_rows(wi...]
    convert_element_type x5 -> x0, other arithmetic: 6.34 us -> none  [the longest x3 3.12 us: shards(): jnp.concatenate([sum_a[:, k * head:(k + 1) * head], sum_b[:, k * head:(k...]
    pallas_call x1, Pallas kernels: 123 us -> 119 us  [third(): pl.pallas_call(functools.partial(third_kernel, masks, inside), in_specs=[...]
    pallas_call x1, Pallas kernels: 99.1 us -> 95.8 us  [second(): pl.pallas_call(second_kernel, in_specs=[any_spec] * 6 + [vmem] * 4, out_s...]
where the time goes in v5:
time: 321 us; the launch traced here: 317 us
  Pallas kernels  315 us (98%)
    pallas_call x1, Pallas kernels, third(): pl.pallas_call(functools.partial(third_kernel, masks, inside), in_specs=[...  119 us
    pallas_call x1, Pallas kernels, second(): pl.pallas_call(second_kernel, in_specs=[any_spec] * 6 + [vmem] * 4, out_s...  95.8 us
    pallas_call x1, Pallas kernels, first(): pl.pallas_call(functools.partial(first_kernel, masks, gather), in_specs=[...  91.5 us
    pallas_call x1, Pallas kernels, outputs(): pl.pallas_call(output_kernel, grid=(rows // block,), in_specs=[by_rows(wi...  8.42 us

profile of v5, /device:TPU:0, one launch (start us, length us, event | category | flops | bytes accessed | tf_op | source)
XLA Modules:
  0.0 316.7 jit_solution(5418708402165346604)
XLA Ops:
  1.3 91.5 %shard_map.254 = (bf16[3072,1024]{1,0:T(8,128)(2,1)}, bf16[3072,1024]{1,0:T(8,128)(2,1)}, bf16[3072,1024]{1,0:T(8,128)(2,1)}, bf16[3072,768]{1,0:T(8,128)(2,1)},...) custom-call(s32[1]{0:T(128)S(6)} %copy.29.kind, ...), custom_call_target="tpu_custom_call" | custom-call | tf_op jit(solution)/shard_map/pallas_call | solution.py:418
  92.8 95.8 %shard_map.255 = (bf16[3072,256]{1,0:T(8,128)(2,1)}, bf16[3072,1024]{1,0:T(8,128)(2,1)}, bf16[3072,1024]{1,0:T(8,128)(2,1)}, f32[3072,256]{1,0:T(8,128)}, bf16[1...) custom-call(bf16[3072,1024]{1,0:T(8,128)(2,1)} %get-tuple-element.55, ...), custom_call_target="tpu_custom_call" | custom-call | tf_op jit(solution)/shard_map/pallas_call | solution.py:700
  188.6 119.2 %shard_map.256 = (bf16[3072,256]{1,0:T(8,128)(2,1)}, bf16[3072,256]{1,0:T(8,128)(2,1)}, bf16[1024,256]{1,0:T(8,128)(2,1)}, bf16[1024,384]{1,0:T(8,128)(2,1)}, bf...) custom-call(s32[1]{0:T(128)S(6)} %copy.29.kind, ...), custom_call_target="tpu_custom_call" | custom-call | tf_op jit(solution)/shard_map/pallas_call | solution.py:1307
  307.8 8.4 %shard_map.257 = (f32[3072,256]{1,0:T(8,128)}, f32[3072,256]{1,0:T(8,128)}, f32[1024,256]{1,0:T(8,128)}, f32[1024,256]{1,0:T(8,128)}, f32[1024,256]{1,0:T(8,128)...) custom-call(f32[3072,256]{1,0:T(8,128)} %get-tuple-element.61.hid_ow, ...), custom_call_target="tpu_custom_call" | custom-call | tf_op jit(solution)/shard_map/pallas_call | solution.py:1409

commit v6 on v5

--- a/solution.py
+++ b/solution.py
@@ -883,13 +883,14 @@
 
 def third_kernel(
     masks, scatter_inside,
-    kind, qkv, grad_heads, logsum, wq, wk, wv, gain, sums_2, grad_bias, grad_bias_reduce,
+    kind, qkv_in, grad_heads, logsum, wq_in, wk_in, wv_in, gain, sums_2, grad_bias, grad_bias_reduce,
     wide_in, narrow_in, a_in, x_in, normed_in, grad_hid, ffn, proj,
     ffn_sum, total_sum, sum_p, sum_a, sum_b, wide_sum, narrow_sum, small,
     dqkv, dk_acc, dv_acc, dq_acc, delta, wgrad, slots, wide, narrow, pay_p, pay_a, pay_b,
     recv_p, recv_a, recv_b, recv_w, recv_n,
     s_core, s_chip, s_mine, s_out, f_src, f_core, f_chip, f_slots, small_recv,
     wg_sems, s_sems, mine_sems, out_sems, f_sems, p_sems, a_sems, b_sems, w_sems, n_sems, slot_sems, keep_sems, small_sems, total_sems,
+    qkv, wq, wk, wv, in_sems,
 ):
     rows = qkv.shape[0]
     width = grad_heads.shape[1]
@@ -1013,6 +1014,12 @@
     pairs = rows // two
     attended = pltpu.make_async_copy(a_in.at[:, at_cols(me, width)], dqkv.at[:, 0:width], wg_sems.at[2])
     attended.start()
+    ahead = [
+        pltpu.make_async_copy(src, dst, in_sems.at[k])
+        for k, (src, dst) in enumerate(((qkv_in, qkv), (wq_in, wq), (wk_in, wk), (wv_in, wv)))
+    ]
+    for load in ahead:
+        load.start()
     attended.wait()
 
     def fill(i, _):
@@ -1023,6 +1030,8 @@
         return 0
 
     lax.fori_loop(0, n, fill, 0)
+    for load in ahead:
+        load.wait()
 
     def load_normed(h, m):
         at = (h * pairs + pairs - 1 - m) % 2
@@ -1306,7 +1315,10 @@
 
     return pl.pallas_call(
         functools.partial(third_kernel, masks, inside),
-        in_specs=[pl.BlockSpec(memory_space=pltpu.SMEM)] + [vmem] * 10 + [any_spec] * 8,
+        in_specs=[pl.BlockSpec(memory_space=pltpu.SMEM), any_spec, vmem, vmem]
+        + [any_spec] * 3
+        + [vmem] * 4
+        + [any_spec] * 8,
         out_specs=[any_spec] * 5 + [vmem] * 3,
         out_shape=[
             jax.ShapeDtypeStruct((rows, width), bf16),
@@ -1359,6 +1371,11 @@
             dma(7),
             dma(2, 2 + len(masks)),
             dma(3, n),
+            pltpu.VMEM(qkv.shape, bf16),
+            pltpu.VMEM(wq.shape, bf16),
+            pltpu.VMEM(wk.shape, bf16),
+            pltpu.VMEM(wv.shape, bf16),
+            dma(4),
         ],
         compiler_params=pltpu.CompilerParams(
             vmem_limit_bytes=63 * MIB, collective_id=2, has_side_effects=True

time: 321 us -> 320 us (level)
  no operation moved by 1% of the time
where the time goes in v6:
time: 320 us; the launch traced here: 315 us
  Pallas kernels  314 us (98%)
    pallas_call x1, Pallas kernels, third(): pl.pallas_call(functools.partial(third_kernel, masks, inside), in_specs=[...  118 us
    pallas_call x1, Pallas kernels, second(): pl.pallas_call(second_kernel, in_specs=[any_spec] * 6 + [vmem] * 4, out_s...  95.8 us
    pallas_call x1, Pallas kernels, first(): pl.pallas_call(functools.partial(first_kernel, masks, gather), in_specs=[...  91.5 us
    pallas_call x1, Pallas kernels, outputs(): pl.pallas_call(output_kernel, grid=(rows // block,), in_specs=[by_rows(wi...  8.42 us

profile of v6, /device:TPU:0, one launch (start us, length us, event | category | flops | bytes accessed | tf_op | source)
XLA Modules:
  0.0 315.4 jit_solution(11354179547491338138)
XLA Ops:
  1.3 91.5 %shard_map.254 = (bf16[3072,1024]{1,0:T(8,128)(2,1)}, bf16[3072,1024]{1,0:T(8,128)(2,1)}, bf16[3072,1024]{1,0:T(8,128)(2,1)}, bf16[3072,768]{1,0:T(8,128)(2,1)},...) custom-call(s32[1]{0:T(128)S(6)} %copy.29.kind, ...), custom_call_target="tpu_custom_call" | custom-call | tf_op jit(solution)/shard_map/pallas_call | solution.py:418
  92.8 95.8 %shard_map.255 = (bf16[3072,256]{1,0:T(8,128)(2,1)}, bf16[3072,1024]{1,0:T(8,128)(2,1)}, bf16[3072,1024]{1,0:T(8,128)(2,1)}, f32[3072,256]{1,0:T(8,128)}, bf16[1...) custom-call(bf16[3072,1024]{1,0:T(8,128)(2,1)} %get-tuple-element.55, ...), custom_call_target="tpu_custom_call" | custom-call | tf_op jit(solution)/shard_map/pallas_call | solution.py:700
  188.6 117.9 %shard_map.256 = (bf16[3072,256]{1,0:T(8,128)(2,1)}, bf16[3072,256]{1,0:T(8,128)(2,1)}, bf16[1024,256]{1,0:T(8,128)(2,1)}, bf16[1024,384]{1,0:T(8,128)(2,1)}, bf...) custom-call(s32[1]{0:T(128)S(6)} %copy.29.kind, ...), custom_call_target="tpu_custom_call" | custom-call | tf_op jit(solution)/shard_map/pallas_call | solution.py:1316
  306.5 8.4 %shard_map.257 = (f32[3072,256]{1,0:T(8,128)}, f32[3072,256]{1,0:T(8,128)}, f32[1024,256]{1,0:T(8,128)}, f32[1024,256]{1,0:T(8,128)}, f32[1024,256]{1,0:T(8,128)...) custom-call(f32[3072,256]{1,0:T(8,128)} %get-tuple-element.61.hid_ow, ...), custom_call_target="tpu_custom_call" | custom-call | tf_op jit(solution)/shard_map/pallas_call | solution.py:1426
